TPU v7x, 32 devices: a whole 2x2x4 slice. The times are simulated.
32 devices in a mesh: row: 4 (over y, x), col: 8 (over z, core).
Axes of the slice: x: 2, y: 2, z: 4, core: 2. Of those that a mesh axis runs over, the one named last changes fastest.
Arguments:
- left_site: bfloat16 [4096, 2048], P('row', 'col')
- right_site: bfloat16 [2048, 4096], P('row', 'col'), may hold values from -0.125 to 0.125
- gate: float32 [4, 4], replicated, may hold values from -0.6 to 2.1
- omega: bfloat16 [4096, 2304], P(None, 'row'), may hold values from -0.09375 to 0.09375
Outputs:
- basis: float32 [4096, 2304], P(('row', 'col'))
- projected: float32 [2304, 4096], P('row', 'col')
All inputs are finite; a program needn't handle non-finite values.
Results may differ from a plain program's by a relative error of at most 0.0085.
Values may be sent and summed in bfloat16 or wider, within the bound.
No kernel may reach another device: no remote copies, remote signals or barrier semaphores. Data moves between devices by JAX's collectives and lax.ppermute only.
A program may use at most 192 MiB of HBM per device.

v0:
```python
import math

import jax
import jax.numpy as jnp
from jax import lax
from jax.sharding import PartitionSpec as P


def apply_gate(bare, gate):
    row_count, col_count = bare.shape
    paired = bare.reshape(row_count // 2, 2, col_count)
    lanes = jnp.arange(col_count)
    same_pair = lanes[:, None] // 2 == lanes[None, :] // 2
    source_bit = lanes[:, None] % 2
    target_bit = lanes[None, :] % 2
    gate_four = gate.reshape(2, 2, 2, 2)
    outputs = []
    for first_state in range(2):
        running = jnp.zeros((row_count // 2, col_count), jnp.float32)
        for source_state in range(2):
            coupling = gate_four[first_state, :, source_state, :]
            mixer = jnp.zeros((col_count, col_count), jnp.float32)
            for second_state in range(2):
                for other_state in range(2):
                    hit = same_pair & (target_bit == second_state) & (source_bit == other_state)
                    mixer = mixer + jnp.where(hit, coupling[second_state, other_state], 0.0)
            running = running + jnp.dot(
                paired[:, source_state, :], mixer, precision=lax.Precision.HIGHEST
            )
        outputs.append(running)
    return jnp.stack(outputs, axis=1).reshape(row_count, col_count)


def split_product(factor_rows, theta_rows):
    head = factor_rows.astype(jnp.bfloat16)
    rest = (factor_rows - head.astype(jnp.float32)).astype(jnp.bfloat16)
    dims = (((0,), (0,)), ((), ()))
    first = lax.dot_general(head, theta_rows, dims, preferred_element_type=jnp.float32)
    second = lax.dot_general(rest, theta_rows, dims, preferred_element_type=jnp.float32)
    return first + second


def gram_cross(upper_part, lower_part):
    return jnp.dot(upper_part.T, lower_part, precision=lax.Precision.HIGHEST)


def gram_blocks(sketch):
    third = sketch.shape[1] // 3
    part_one = sketch[:, :third]
    part_two = sketch[:, third : 2 * third]
    part_three = sketch[:, 2 * third :]
    return (
        gram_cross(part_one, part_one),
        gram_cross(part_one, part_two),
        gram_cross(part_one, part_three),
        gram_cross(part_two, part_two),
        gram_cross(part_two, part_three),
        gram_cross(part_three, part_three),
    )


def exact_dot(first, second):
    return jnp.dot(first, second, precision=lax.Precision.HIGHEST)


def right_solve(lower_block, values):
    return jax.scipy.linalg.solve_triangular(lower_block, values.T, lower=True).T


def factor_of(blocks, total_rows):
    scaled = [block / total_rows for block in blocks]
    diag_one = jnp.linalg.cholesky(scaled[0])
    below_one = right_solve(diag_one, scaled[1].T)
    bottom_one = right_solve(diag_one, scaled[2].T)
    diag_two = jnp.linalg.cholesky(scaled[3] - exact_dot(below_one, below_one.T))
    bottom_two = right_solve(diag_two, scaled[4].T - exact_dot(bottom_one, below_one.T))
    rest_three = (
        scaled[5] - exact_dot(bottom_one, bottom_one.T) - exact_dot(bottom_two, bottom_two.T)
    )
    diag_three = jnp.linalg.cholesky(rest_three)
    return (diag_one, below_one, bottom_one, diag_two, bottom_two, diag_three)


def basis_of(factor, sketch):
    third = sketch.shape[1] // 3
    first_cols = right_solve(factor[0], sketch[:, :third])
    second_cols = right_solve(
        factor[3], sketch[:, third : 2 * third] - exact_dot(first_cols, factor[1].T)
    )
    third_cols = (
        sketch[:, 2 * third :]
        - exact_dot(first_cols, factor[2].T)
        - exact_dot(second_cols, factor[4].T)
    )
    third_cols = right_solve(factor[5], third_cols)
    return jnp.concatenate([first_cols, second_cols, third_cols], axis=1)


def on_device(left_site, right_site, gate, omega):
    rows_here = left_site.shape[0]
    total_rows = rows_here * lax.axis_size("row")
    right_cols = lax.all_gather(right_site, "row", axis=0, tiled=True)
    cols_here = right_cols.shape[1]
    bare = jnp.dot(
        lax.all_gather(left_site, "col", axis=1, tiled=True),
        right_cols,
        preferred_element_type=jnp.float32,
    )
    theta = apply_gate(bare, gate).astype(jnp.bfloat16)
    col_start = lax.axis_index("col") * cols_here
    omega_mine = lax.dynamic_slice_in_dim(omega, col_start, cols_here, 0)
    omega_rows = lax.all_gather(omega_mine, "row", axis=1, tiled=True)
    theta_rows = theta
    sketch = lax.psum_scatter(
        jnp.dot(theta_rows, omega_rows, preferred_element_type=jnp.float32),
        "col",
        scatter_dimension=0,
        tiled=True,
    )
    blocks = lax.psum(gram_blocks(sketch), ("row", "col"))
    factor = factor_of(blocks, total_rows)
    basis = basis_of(factor, sketch)
    theta_rows = theta
    folded = split_product(lax.all_gather(basis, "col", axis=0, tiled=True), theta_rows)
    projected = lax.psum_scatter(folded, "row", scatter_dimension=0, tiled=True) / math.sqrt(
        total_rows
    )
    return (basis, projected)


def solution(mesh):
    in_specs = (P("row", "col"), P("row", "col"), P(), P(None, "row"))
    out_specs = (P(("row", "col"), None), P("row", "col"))
    return jax.shard_map(
        on_device, mesh=mesh, in_specs=in_specs, out_specs=out_specs, check_vma=False
    )
```

profile of v0, /device:TPU:0, one launch (start us, length us, event | category | flops | bytes accessed | tf_op | source)
XLA Modules:
  0.0 1609.7 jit_solution(3648599041738247919)
XLA Ops:
  13.4 34.5 %all-gather.7.cloned.1.call-done = bf16[2048,512]{1,0:T(8,128)(2,1)} async-done(((bf16[512,512]{1,0:T(8,128)(2,1)}), bf16[2048,512]{1,0:T(8,128)(2,1)}) %all-gather.7.cloned.1.call-update) | async-done | bytes 2097168 | tf_op jit(solution)/shard_map/all_gather | solution.py:102
  47.9 49.4 %all-gather.5.cloned.1.call-done = bf16[1024,2048]{1,0:T(8,128)(2,1)} async-done(((bf16[1024,256]{1,0:T(8,128)(2,1)}), bf16[1024,2048]{1,0:T(8,128)(2,1)}) %all-gather.5.cloned.1.call-update) | async-done | bytes 4194320 | tf_op jit(solution)/shard_map/all_gather | solution.py:105
  142.7 99.2 %reduce-scatter.3.cloned.1.call-done = f32[128,2304]{1,0:T(8,128)} async-done(((f32[1024,2304]{1,0:T(8,128)}), f32[128,2304]{1,0:T(8,128)}) %reduce-scatter.3.cloned.1.call-update) | async-done | bytes 1179664 | tf_op jit(solution)/shard_map/reduce_scatter | solution.py:114
  264.9 249.7 %all-reduce.4.cloned.1.call-done = (f32[768,768]{0,1:T(8,128)}, f32[768,768]{0,1:T(8,128)}, f32[768,768]{0,1:T(8,128)}, f32[768,768]{0,1:T(8,128)}, f32[768,768]{0,1:T(8,128)}, /*index=5*/f32[768,768]{0,1:T(8,128)}) async-done(((f32[768,768]{0,1:T(8,128)}, f32[768,768]{0,1:T(8,128)}, f32[768,768]{0,1:T(8,128)}, f32[768,768]{0,1:T(8,128)}, f32[768,768]{0,1:T(8,128)}, /*index=5*/f32[768,768]{0,1:T(8,128)}), ...) | async-done | bytes 14155792 | tf_op jit(solution)/shard_map/psum | solution.py:120
  524.5 11.7 cholesky.591
  538.5 11.3 custom-call.52
  553.9 13.2 cholesky.610
  570.0 11.6 custom-call.53
  585.8 13.2 cholesky.631
  601.1 11.3 custom-call.54
  616.4 13.3 cholesky.650
  632.0 11.3 custom-call.55
  647.1 13.2 cholesky.669
  662.5 11.3 custom-call.56
  676.8 13.6 cholesky.686
  697.4 18.0 %while.12 = (s32[]{:T(128)}, f32[768,768]{1,0:T(8,128)}, s32[6,2]{0,1:T(2,128)S(1)}, f32[6,128,128]{2,1,0:T(8,128)S(1)}, s32[]{:T(128)}) while((s32[]{:T(128)}, f32[768,768]{1,0:T(8,128)}, s32[6,2]{0,1:T(2,128)S(1)}, f32[6,128,128]{2,1,0:T(8,128)S(1)}, s32[]{:T(128)}) %tuple.171), condition=%wide.while_cond, body=%wide.while_body.sunk | while | flops 2 | bytes 131181 | solution.py:67
  715.5 59.0 %custom-call.57 = f32[6,128,128]{1,2,0:T(8,128)S(1)} custom-call(f32[6,128,128]{2,1,0:T(8,128)S(1)} %get-tuple-element.45), custom_call_target="InvertDiagBlocksLowerTriangular" | custom-call | tf_op jit(solution)/shard_map/jit(_solve_triangular)/triangular_solve | solution.py:67
  812.5 8.1 multiply_subtract_fusion
  820.5 8.0 multiply_subtract_fusion.1
  836.5 13.2 cholesky.701
  853.6 11.3 custom-call.59
  869.8 13.2 cholesky.720
  885.7 11.5 custom-call.60
  902.3 13.2 cholesky.741
  917.7 11.3 custom-call.61
  934.0 13.6 cholesky.760
  949.9 11.3 custom-call.62
  966.0 13.2 cholesky.779
  981.3 11.3 custom-call.63
  996.5 13.3 cholesky.796
  1019.7 21.6 %while.13 = (s32[]{:T(128)}, f32[768,768]{1,0:T(8,128)}, s32[6,2]{0,1:T(2,128)S(1)}, f32[6,128,128]{2,1,0:T(8,128)}, s32[]{:T(128)}) while((s32[]{:T(128)}, f32[768,768]{1,0:T(8,128)}, s32[6,2]{0,1:T(2,128)S(1)}, f32[6,128,128]{2,1,0:T(8,128)}, s32[]{:T(128)}) %tuple.195), condition=%wide.while_cond.clone, body=%wide.while_body.clone.sunk | while | flops 2 | bytes 132705 | solution.py:67
  1041.3 60.4 %custom-call.64 = f32[6,128,128]{1,2,0:T(8,128)} custom-call(f32[6,128,128]{2,1,0:T(8,128)} %get-tuple-element.47), custom_call_target="InvertDiagBlocksLowerTriangular" | custom-call | tf_op jit(solution)/shard_map/jit(_solve_triangular)/triangular_solve | solution.py:67
  1123.3 8.2 subtract_subtract_fusion
  1139.5 13.2 cholesky.811
  1156.6 11.3 custom-call.67
  1172.8 13.2 cholesky.830
  1188.9 11.5 custom-call.68
  1205.5 13.2 cholesky.851
  1220.8 11.3 custom-call.69
  1237.2 13.6 cholesky.870
  1253.0 11.3 custom-call.70
  1269.1 13.2 cholesky.889
  1284.6 11.3 custom-call.71
  1299.8 13.3 cholesky.906
  1323.2 21.6 %while.14 = (s32[]{:T(128)}, f32[768,768]{1,0:T(8,128)}, s32[6,2]{0,1:T(2,128)S(1)}, f32[6,128,128]{2,1,0:T(8,128)}, s32[]{:T(128)}) while((s32[]{:T(128)}, f32[768,768]{1,0:T(8,128)}, s32[6,2]{0,1:T(2,128)S(1)}, f32[6,128,128]{2,1,0:T(8,128)}, s32[]{:T(128)}) %tuple.196), condition=%wide.while_cond.clone.1, body=%wide.while_body.clone.1.sunk | while | flops 2 | bytes 132705 | solution.py:67
  1344.7 60.4 %custom-call.72 = f32[6,128,128]{1,2,0:T(8,128)} custom-call(f32[6,128,128]{2,1,0:T(8,128)} %get-tuple-element.50), custom_call_target="InvertDiagBlocksLowerTriangular" | custom-call | tf_op jit(solution)/shard_map/jit(_solve_triangular)/triangular_solve | solution.py:67
  1443.0 91.1 %all-gather.11.cloned.1.call-done = f32[1024,2304]{0,1:T(8,128)} async-done(((f32[128,2304]{0,1:T(8,128)}), f32[1024,2304]{0,1:T(8,128)}) %all-gather.11.cloned.1.call-update) | async-done | bytes 9437200 | tf_op jit(solution)/shard_map/all_gather | solution.py:124
  1547.4 52.8 %reduce-scatter.5.cloned.1.call-done = f32[576,512]{1,0:T(8,128)} async-done(((f32[2304,512]{1,0:T(8,128)}), f32[576,512]{1,0:T(8,128)}) %reduce-scatter.5.cloned.1.call-update) | async-done | bytes 1179664 | tf_op jit(solution)/shard_map/reduce_scatter | solution.py:125
  (350 shorter events, 394.8 us)
Async XLA Ops:
  7.2 3.5 copy-start.37
  7.2 40.7 %all-gather.7.cloned.1.call-start = ((), (), s32[]{:S(2)}) async-start(), calls=%async_computation.3 | async-start | bytes 2621440 | tf_op jit(solution)/shard_map/all_gather | solution.py:102
  7.9 89.4 %all-gather.5.cloned.1.call-start = ((), (), s32[]{:S(2)}) async-start(), calls=%async_computation.2 | async-start | bytes 4718592 | tf_op jit(solution)/shard_map/all_gather | solution.py:105
  8.7 126.8 %all-gather.9.cloned.1.call-start = ((), (), s32[]{:S(2)}) async-start(), calls=%async_computation.4 | async-start | bytes 2949120 | tf_op jit(solution)/shard_map/all_gather | solution.py:112
  10.7 231.3 %reduce-scatter.3.cloned.1.call-start = ((), (), s32[]{:S(2)}) async-start(), calls=%async_computation.5 | async-start | bytes 10616832 | tf_op jit(solution)/shard_map/reduce_scatter | solution.py:114
  130.1 12.1 copy-start.24
  142.2 372.4 %all-reduce.4.cloned.1.call-start = ((), (), s32[]{:S(2)}) async-start(), calls=%async_computation.8 | async-start | bytes 28311552 | tf_op jit(solution)/shard_map/psum | solution.py:120
  241.9 4.7 copy-start.4
  264.1 1270.0 %all-gather.11.cloned.1.call-start = ((), (), s32[]{:S(2)}) async-start(), calls=%async_computation.6 | async-start | bytes 10616832 | tf_op jit(solution)/shard_map/all_gather | solution.py:124
  517.9 3.2 copy-start.8
  523.1 1.4 copy-start.10
  536.2 0.6 copy-start.36
  552.6 0.7 copy-start.21
  584.5 0.7 copy-start.26
  615.1 0.7 copy-start.29
  645.9 0.6 copy-start.32
  774.4 11.2 copy-start.13
  774.4 2.5 copy-start.6
  785.6 4.1 copy-start.15
  789.7 1.0 copy-start.14
  804.4 8.0 copy-start.18
  812.4 8.1 copy-start
  812.4 8.1 copy-start.17
  834.4 1.5 copy-start.11
  868.4 0.7 copy-start.22
  901.0 0.7 copy-start.27
  932.8 0.7 copy-start.30
  964.7 0.7 copy-start.33
  1101.7 3.6 copy-start.19
  1101.7 4.1 copy-start.9
  1115.8 7.5 copy-start.5
  1115.8 7.5 copy-start.16
  1121.9 1.4 copy-start.2
  1137.4 1.4 copy-start.12
  1171.4 0.7 copy-start.23
  1204.2 0.7 copy-start.28
  1235.9 0.7 copy-start.31
  1267.9 0.6 copy-start.34
  1405.1 14.2 copy-start.1
  1415.3 5.5 copy-start.20
  1427.4 3.9 copy-start.3
  1431.3 1.5 copy-start.35
  1439.6 94.5 %copy-start.25 = (bf16[1024,512]{1,0:T(8,128)(2,1)S(1)}, bf16[1024,512]{1,0:T(8,128)(2,1)}, u32[]{:S(2)}) copy-start(bf16[1024,512]{1,0:T(8,128)(2,1)} %copy-done.24) | copy-start | bytes 3145732
  1443.0 157.3 %reduce-scatter.5.cloned.1.call-start = ((), (), s32[]{:S(2)}) async-start(), calls=%async_computation.7 | async-start | bytes 5898240 | tf_op jit(solution)/shard_map/reduce_scatter | solution.py:125
  1534.1 6.4 copy-start.38
  1544.8 1.3 copy-start.7
Sparse Core Ops, SparseCore 0:
  9.9 38.0 all-gather.6
  49.5 47.7 all-gather.4
  99.7 35.7 all-gather.8
  142.4 99.5 reduce-scatter.2
  264.2 250.3 all-reduce.3
  1443.1 90.9 all-gather.10
  1544.9 55.2 reduce-scatter.4
where the time goes:
time: 1620 us; the launch traced here: 1610 us
  other arithmetic  649 us (40%)
  waiting for transfers between devices  584 us (36%)
  matrix products  233 us (14%)
  local copies, waits for them, and re-layouts  117 us (7%)
  between operations  26.9 us (2%)
    psum x1, waiting for transfers between devices, on_device(): blocks = lax.psum(gram_blocks(sketch), ('row', 'col'))  250 us
    another operation x7, other arithmetic, right_solve(): jax.scipy.linalg.solve_triangular(lower_block, values.T, lower=True)  188 us
    another operation x23, other arithmetic, factor_of(): diag_three = jnp.linalg.cholesky(rest_three)  149 us
    another operation x23, other arithmetic, factor_of(): jnp.linalg.cholesky(scaled[3] - exact_dot(below_one, below_one.T))  149 us
    another operation x23, other arithmetic, factor_of(): diag_one = jnp.linalg.cholesky(scaled[0])  146 us
    reduce_scatter x1, waiting for transfers between devices, on_device(): lax.psum_scatter(jnp.dot(theta_rows, omega_rows, preferred_element_type=j...  99.2 us
    all_gather x1, waiting for transfers between devices, on_device(): lax.all_gather(basis, 'col', axis=0, tiled=True)  91.1 us
    another operation x66, matrix products, right_solve(): jax.scipy.linalg.solve_triangular(lower_block, values.T, lower=True)  79.4 us
  transfers between devices with their start and end apart: 7, of which 7 were waited for; matrix products, arithmetic and copies ran while one was open for 2% of the time, Pallas kernels for 0%

commit v1 on v0

v1 whole, which is shorter than its diff:
```python
import functools
import math

import jax
import jax.numpy as jnp
from jax import lax
from jax.experimental import pallas as pl
from jax.experimental.pallas import tpu as pltpu
from jax.sharding import PartitionSpec as P

F32, BF16 = jnp.float32, jnp.bfloat16
NN = (((1,), (0,)), ((), ()))
NT = (((1,), (1,)), ((), ()))
TN = (((0,), (0,)), ((), ()))
VMEM = pl.BlockSpec(memory_space=pltpu.VMEM)
TILE = 256
ROUGH_STEPS = 5
SETTLED = 1e-4


def dot(a, b, dims=NN):
    return lax.dot_general(a, b, dims, preferred_element_type=F32)


def halves(x):
    high = x.astype(BF16)
    return high, (x - high.astype(F32)).astype(BF16)


def dot3(a, b, dims=NN):
    return dot(a[0], b[0], dims) + dot(a[0], b[1], dims) + dot(a[1], b[0], dims)


def positions(shape):
    return lax.broadcasted_iota(jnp.int32, shape, 0), lax.broadcasted_iota(jnp.int32, shape, 1)


def theta_kernel(gate_ref, left_ref, right_ref, theta_ref):
    bare = dot(left_ref[...], right_ref[...])
    rows, cols = bare.shape
    row, col = positions((rows, cols))
    row_odd, col_odd = row % 2 == 1, col % 2 == 1

    def partner_row(x):
        return jnp.where(row_odd, pltpu.roll(x, 1, 0), pltpu.roll(x, rows - 1, 0))

    def partner_col(x):
        return jnp.where(col_odd, pltpu.roll(x, 1, 1), pltpu.roll(x, cols - 1, 1))

    def weight(flip_row, flip_col):
        def entry(s, t):
            return gate_ref[2 * s + t, 2 * (s ^ flip_row) + (t ^ flip_col)]

        return jnp.where(
            row_odd,
            jnp.where(col_odd, entry(1, 1), entry(1, 0)),
            jnp.where(col_odd, entry(0, 1), entry(0, 0)),
        )

    across = partner_row(bare)
    mixed = weight(0, 0) * bare + weight(0, 1) * partner_col(bare)
    mixed = mixed + weight(1, 0) * across + weight(1, 1) * partner_col(across)
    theta_ref[...] = mixed.astype(BF16)


def theta_of(left, right, gate):
    rows, depth = left.shape
    cols = right.shape[1]
    return pl.pallas_call(
        theta_kernel,
        grid=(rows // TILE,),
        out_shape=jax.ShapeDtypeStruct((rows, cols), BF16),
        in_specs=[
            pl.BlockSpec(memory_space=pltpu.SMEM),
            pl.BlockSpec((TILE, depth), lambda i: (i, 0)),
            pl.BlockSpec((depth, cols), lambda i: (0, 0)),
        ],
        out_specs=pl.BlockSpec((TILE, cols), lambda i: (i, 0)),
        compiler_params=pltpu.CompilerParams(vmem_limit_bytes=32 << 20),
        cost_estimate=pl.CostEstimate(
            flops=2 * rows * depth * cols,
            bytes_accessed=2 * (rows * depth + depth * cols + rows * cols),
            transcendentals=0,
        ),
    )(gate, left, right)


def eliminate(block, out_ref, work_ref):
    tile = block.shape[0]
    row, col = positions((tile, tile))
    work_ref[...] = block
    out_ref[...] = jnp.where(row == col, 1.0, 0.0).astype(F32)

    def column(j, carry):
        values = work_ref[...]
        pivot_row = work_ref[pl.ds(j, 1), :]
        pivot_col = jnp.sum(jnp.where(col == j, values, 0.0), axis=1, keepdims=True)
        pivot = jnp.sum(jnp.where(col[:1] == j, pivot_row, 0.0), axis=1, keepdims=True)
        root = 1.0 / jnp.sqrt(pivot)
        done = out_ref[pl.ds(j, 1), :] * root
        factor = jnp.where(row[:, :1] > j, pivot_col * root, 0.0)
        work_ref[...] = values - factor * (pivot_row * root)
        out_ref[...] = out_ref[...] - factor * done
        out_ref[pl.ds(j, 1), :] = done
        return carry

    lax.fori_loop(0, tile, column, 0)


def inverse_factor(block, out_ref, work_ref):
    row, col = positions(block.shape)
    same, below = row == col, row > col
    diagonal = jnp.where(same, block, 0.0)
    scale_row = lax.rsqrt(jnp.sum(diagonal, axis=0, keepdims=True))
    scale_col = lax.rsqrt(jnp.sum(diagonal, axis=1, keepdims=True))
    normal = block * scale_row * scale_col
    parts = halves(normal)
    near = 0.5 * normal
    inverse = jnp.where(same, math.sqrt(0.5), 0.0).astype(F32)
    for _ in range(ROUGH_STEPS):
        step = jnp.where(below, -near, jnp.where(same, 1.5 - 0.5 * near, 0.0)).astype(BF16)
        inverse = dot(step, inverse.astype(BF16))
        near = dot(dot(step, near.astype(BF16)).astype(BF16), step, NT)

    def polish(inverse):
        own = halves(inverse)
        rest = dot3(halves(dot3(own, parts)), own, NT) - jnp.where(same, 1.0, 0.0)
        shift = jnp.where(below, rest, jnp.where(same, 0.5 * rest, 0.0)).astype(BF16)
        return inverse - dot(shift, own[0]), jnp.sum(rest * rest)

    inverse, _ = polish(inverse)
    inverse, gap = polish(inverse)
    out_ref[...] = inverse

    def again(state):
        inverse, gap = polish(out_ref[...])
        out_ref[...] = inverse
        return state[0] + 1, gap

    _, gap = lax.while_loop(lambda state: (state[0] < 16) & (state[1] > SETTLED), again, (0, gap))
    settled = gap <= SETTLED

    @pl.when(settled)
    def _():
        out_ref[...] = out_ref[...] * scale_row

    @pl.when(jnp.logical_not(settled))
    def _():
        eliminate(block, out_ref, work_ref)


def basis_kernel(scale, *refs):
    count = len(refs) - 10
    gram_refs, sketch_ref = refs[:count], refs[count]
    basis_ref, short_ref, high_ref, low_ref, basis_low_ref, inv_high_ref, inv_low_ref, inverse_ref, work_ref = refs[
        count + 1 :
    ]
    for k in range(count):
        here, past = slice(k * TILE, (k + 1) * TILE), slice(0, k * TILE)
        gram_ref = gram_refs[k]

        def left_over(values, left):
            if k == 0:
                return values
            return values - dot3(left, (high_ref[here, past], low_ref[here, past]), NT)

        def factor_rows(at):
            return high_ref[pl.ds(at, TILE), past], low_ref[pl.ds(at, TILE), past]

        inverse_factor(
            left_over(gram_ref[:TILE, :] * scale, factor_rows(k * TILE) if k else None), inverse_ref, work_ref
        )
        inv_high_ref[...], inv_low_ref[...] = halves(inverse_ref[...])

        def panel(i, carry):
            own = inv_high_ref[...], inv_low_ref[...]
            at = pl.multiple_of((k + 1 + i) * TILE, TILE)
            gram_at = pl.multiple_of((1 + i) * TILE, TILE)
            values = left_over(gram_ref[pl.ds(gram_at, TILE), :] * scale, factor_rows(at) if k else None)
            solved = halves(dot3(halves(values), own, NT))
            high_ref[pl.ds(at, TILE), here], low_ref[pl.ds(at, TILE), here] = solved
            return carry

        if k + 1 < count:
            lax.fori_loop(0, count - 1 - k, panel, 0)
        values = left_over(sketch_ref[:, here], (short_ref[:, past], basis_low_ref[:, past]) if k else None)
        solved = dot3(halves(values), (inv_high_ref[...], inv_low_ref[...]), NT)
        basis_ref[:, here] = solved
        short_ref[:, here], basis_low_ref[:, here] = halves(solved)


def basis_of(gram_columns, sketch, scale):
    rows, size = sketch.shape
    return pl.pallas_call(
        functools.partial(basis_kernel, scale),
        out_shape=[jax.ShapeDtypeStruct((rows, size), F32), jax.ShapeDtypeStruct((rows, size), BF16)],
        in_specs=[VMEM] * (len(gram_columns) + 1),
        out_specs=[VMEM, VMEM],
        scratch_shapes=[
            pltpu.VMEM((size, size), BF16),
            pltpu.VMEM((size, size), BF16),
            pltpu.VMEM((rows, size), BF16),
            pltpu.VMEM((TILE, TILE), BF16),
            pltpu.VMEM((TILE, TILE), BF16),
            pltpu.VMEM((TILE, TILE), F32),
            pltpu.VMEM((TILE, TILE), F32),
        ],
        compiler_params=pltpu.CompilerParams(vmem_limit_bytes=56 << 20),
        cost_estimate=pl.CostEstimate(
            flops=24 * size**3, bytes_accessed=2 * size * size + 10 * rows * size, transcendentals=0
        ),
    )(*gram_columns, sketch)


def gram_columns_of(sketch):
    rounded = lax.reduce_precision(sketch, 8, 7)
    high, low = rounded.astype(BF16), (sketch - rounded).astype(BF16)
    left = jnp.concatenate([high, high, low], axis=0)
    right = jnp.concatenate([high, low, high], axis=0)
    return tuple(
        dot(left[:, at:], right[:, at : at + TILE], TN) for at in range(0, sketch.shape[1], TILE)
    )


def on_device(left_site, right_site, gate, omega):
    rows_here = left_site.shape[0]
    total_rows = rows_here * lax.axis_size("row")
    right_cols = lax.all_gather(right_site, "row", axis=0, tiled=True)
    left_rows = lax.all_gather(left_site, "col", axis=1, tiled=True)
    theta = theta_of(left_rows, right_cols, gate)
    cols_here = theta.shape[1]
    omega_mine = lax.dynamic_slice_in_dim(omega, lax.axis_index("col") * cols_here, cols_here, 0)
    omega_rows = lax.all_gather(omega_mine, "row", axis=1, tiled=True)
    sketch = lax.psum_scatter(dot(theta, omega_rows), "col", scatter_dimension=0, tiled=True)
    gram_columns = lax.psum(gram_columns_of(sketch), ("row", "col"))
    basis, basis_short = basis_of(gram_columns, sketch, 1.0 / total_rows)
    basis_rows = lax.all_gather(basis_short, "col", axis=0, tiled=True)
    folded = dot(basis_rows, theta, TN).astype(BF16)
    pieces = lax.all_to_all(
        folded.reshape(lax.axis_size("row"), -1, cols_here), "row", 0, 0, tiled=False
    )
    projected = jnp.sum(pieces.astype(F32), axis=0) / math.sqrt(total_rows)
    return (basis, projected)


def solution(mesh):
    in_specs = (P("row", "col"), P("row", "col"), P(), P(None, "row"))
    out_specs = (P(("row", "col"), None), P("row", "col"))
    return jax.shard_map(
        on_device, mesh=mesh, in_specs=in_specs, out_specs=out_specs, check_vma=False
    )
```

time: 1620 us -> 675 us (0.42)
  other arithmetic: 649 us -> 3.19 us
  matrix products: 233 us -> 26.5 us
  local copies, waits for them, and re-layouts: 117 us -> 5.71 us
  Pallas kernels: 0 us -> 82.5 us
  waiting for transfers between devices: 584 us -> 502 us
  blocking collectives: 0 us -> 32 us
    another operation x77 -> x0, other arithmetic: 633 us -> none  [the longest x7 188 us: right_solve(): jax.scipy.linalg.solve_triangular(lower_block, values.T, lower=True)]
    another operation x96 -> x0, matrix products: 131 us -> none  [the longest x66 79.4 us: right_solve(): jax.scipy.linalg.solve_triangular(lower_block, values.T, lower=True)]
    pallas_call x0 -> x2, Pallas kernels: none -> 82.5 us  [the longest x1 76.6 us: basis_of(): pl.pallas_call(functools.partial(basis_kernel, scale), out_shape=[jax.Sha...]
    another operation x77 -> x0, local copies, waits for them, and re-layouts: 78.3 us -> none  [the longest x58 62.7 us: right_solve(): jax.scipy.linalg.solve_triangular(lower_block, values.T, lower=True)]
    dot_general x21 -> x11, matrix products: 102 us -> 26.5 us  [dot(): return lax.dot_general(a, b, dims, preferred_element_type=F32)]
    reduce_scatter x2 -> x1, waiting for transfers between devices: 152 us -> 99.6 us  [on_device(): lax.psum_scatter(dot(theta, omega_rows), 'col', scatter_dimension=0, tile...]
    all_gather x2, waiting for transfers between devices: 140 us -> 100 us  [the longest x1 51 us: on_device(): basis_rows = lax.all_gather(basis_short, 'col', axis=0, tiled=True)]
    all_to_all x0 -> x1, blocking collectives: none -> 32 us  [on_device(): lax.all_to_all(folded.reshape(lax.axis_size('row'), -1, cols_here), 'row'...]
  transfers between devices with their start and end apart: 7 -> 6, of which waited for: 7 -> 6; matrix products, arithmetic and copies ran while one was open for 2% -> 0% of each run, Pallas kernels for 0% -> 1%
where the time goes in v1:
time: 675 us; the launch traced here: 667 us
  waiting for transfers between devices  502 us (74%)
  Pallas kernels  82.5 us (12%)
  blocking collectives  32 us (5%)
  matrix products  26.5 us (4%)
  between operations  14.6 us (2%)
    psum x1, waiting for transfers between devices, on_device(): gram_columns = lax.psum(gram_columns_of(sketch), ('row', 'col'))  235 us
    reduce_scatter x1, waiting for transfers between devices, on_device(): lax.psum_scatter(dot(theta, omega_rows), 'col', scatter_dimension=0, tile...  99.6 us
    pallas_call x1, Pallas kernels, basis_of(): pl.pallas_call(functools.partial(basis_kernel, scale), out_shape=[jax.Sha...  76.6 us
    all_gather x1, waiting for transfers between devices, on_device(): basis_rows = lax.all_gather(basis_short, 'col', axis=0, tiled=True)  51 us
    all_gather x1, waiting for transfers between devices, on_device(): left_rows = lax.all_gather(left_site, 'col', axis=1, tiled=True)  49.4 us
    all_gather x1, waiting for transfers between devices, on_device(): right_cols = lax.all_gather(right_site, 'row', axis=0, tiled=True)  37.2 us
    all_to_all x1, blocking collectives, on_device(): lax.all_to_all(folded.reshape(lax.axis_size('row'), -1, cols_here), 'row'...  32 us
    all_gather x1, waiting for transfers between devices, on_device(): omega_rows = lax.all_gather(omega_mine, 'row', axis=1, tiled=True)  28.5 us
  transfers between devices with their start and end apart: 6, of which 6 were waited for; matrix products, arithmetic and copies ran while one was open for 0% of the time, Pallas kernels for 1%

profile of v1, /device:TPU:0, one launch (start us, length us, event | category | flops | bytes accessed | tf_op | source)
XLA Modules:
  0.0 667.3 jit_solution(3400935108674370041)
XLA Ops:
  7.2 0.0 copy-start.2
  7.2 0.0 all-gather.7.cloned.1.call-start
  7.2 0.7 all-gather.7.cloned.1.call-update
  7.9 0.0 all-gather.5.cloned.1.call-start
  8.0 0.7 all-gather.5.cloned.1.call-update
  8.7 0.0 all-gather.9.cloned.1.call-start
  8.7 1.9 constant_dynamic-slice_fusion
  10.6 0.0 all-gather.9.cloned.1.call-update
  10.7 0.0 reduce-scatter.2.cloned.1.call-start
  10.7 37.2 %all-gather.7.cloned.1.call-done.right_ref = bf16[2048,512]{1,0:T(8,128)(2,1)} async-done(((bf16[512,512]{1,0:T(8,128)(2,1)}), bf16[2048,512]{1,0:T(8,128)(2,1)}) %all-gather.7.cloned.1.call-update) | async-done | bytes 2097168 | tf_op jit(solution)/shard_map/all_gather | solution.py:228
  47.9 49.4 %all-gather.5.cloned.1.call-done.left_ref = bf16[1024,2048]{1,0:T(8,128)(2,1)} async-done(((bf16[1024,256]{1,0:T(8,128)(2,1)}), bf16[1024,2048]{1,0:T(8,128)(2,1)}) %all-gather.5.cloned.1.call-update) | async-done | bytes 4194320 | tf_op jit(solution)/shard_map/all_gather | solution.py:229
  97.3 0.0 copy-done.2
  97.3 0.0 copy-start
  97.3 2.2 copy-done
  99.5 0.0 copy-start.1
  99.5 1.6 copy-done.1
  101.1 5.9 shard_map.59
  107.0 0.0 copy-start.3
  107.0 28.5 %all-gather.9.cloned.1.call-done = bf16[512,2304]{0,1:T(8,128)(2,1)} async-done(((bf16[512,576]{0,1:T(8,128)(2,1)}), bf16[512,2304]{0,1:T(8,128)(2,1)}) %all-gather.9.cloned.1.call-update) | async-done | bytes 2359312 | tf_op jit(solution)/shard_map/all_gather | solution.py:233
  135.5 6.8 %fusion.30 = f32[1024,2304]{1,0:T(8,128)} fusion(bf16[1024,512]{1,0:T(8,128)(2,1)S(1)} %shard_map.59, bf16[512,2304]{0,1:T(8,128)(2,1)} %all-gather.9.cloned.1.call-done), kind=kOutput, calls=%fused_computation.37 | convolution fusion | flops 2415919104 | bytes 12845056 | tf_op jit(solution)/shard_map/dot_general | solution.py:22
  142.2 0.0 copy-done.3
  142.3 0.0 reduce-scatter.2.cloned.1.call-update
  142.3 0.0 all-reduce.3.cloned.1.call-start
  142.3 99.6 %reduce-scatter.2.cloned.1.call-done.refs_9_ = f32[128,2304]{1,0:T(8,128)} async-done(((f32[1024,2304]{1,0:T(8,128)}), f32[128,2304]{1,0:T(8,128)}) %reduce-scatter.2.cloned.1.call-update) | async-done | bytes 1179664 | tf_op jit(solution)/shard_map/reduce_scatter | solution.py:234
  242.0 1.4 fusion.6
  243.4 0.3 fusion
  243.7 1.0 fusion.17
  244.6 1.1 fusion.15
  245.8 1.3 fusion.13
  247.1 1.4 fusion.11
  248.5 2.2 fusion.27
  250.8 1.6 fusion.9
  252.4 1.8 fusion.7
  254.1 1.9 fusion.4
  256.1 2.1 fusion.2
  258.2 0.0 all-reduce.3.cloned.1.call-update
  258.2 0.0 all-gather.11.cloned.1.call-start
  258.3 235.2 %all-reduce.3.cloned.1.call-done = (f32[2304,256]{1,0:T(8,128)}, f32[2048,256]{1,0:T(8,128)}, f32[1792,256]{1,0:T(8,128)}, f32[1536,256]{1,0:T(8,128)}, f32[1280...) async-done(((f32[2304,256]{1,0:T(8,128)}, f32[2048,256]{1,0:T(8,128)}, f32[1792,256]{1,0:T(8,128)}, ...) | async-done | bytes 11796496 | tf_op jit(solution)/shard_map/psum | solution.py:235
  493.5 0.0 copy-start.4
  493.5 76.6 %shard_map.60 = (f32[128,2304]{1,0:T(8,128)}, bf16[128,2304]{1,0:T(8,128)(2,1)}) custom-call(f32[2304,256]{1,0:T(8,128)} %get-tuple-element.6.refs_0_, f32[2048,256]{1,0:T(8,128)} %get-tuple-element.7.refs_1_, f32[1792,256]{1,0:T(8,128)} %get-tuple-element.8.refs_2_, f32[1536,256]{1,0:T(8,128)} %get-tuple-element.9.refs_3_, ...), custom_call_target="tpu_custom_call" | custom-call | flops 293534171136 | bytes 13565952 | tf_op jit(solution)/shard_map/pallas_call | solution.py:194
  570.2 0.0 all-gather.11.cloned.1.call-update
  570.2 51.0 %all-gather.11.cloned.1.call-done = bf16[1024,2304]{1,0:T(8,128)(2,1)} async-done(((bf16[128,2304]{1,0:T(8,128)(2,1)}), bf16[1024,2304]{1,0:T(8,128)(2,1)}) %all-gather.11.cloned.1.call-update) | async-done | bytes 4718608 | tf_op jit(solution)/shard_map/all_gather | solution.py:237
  621.2 0.0 copy-done.4
  621.2 5.2 convolution_convert_fusion
  626.5 32.0 %all_to_all.5 = bf16[4,576,512]{2,1,0:T(8,128)(2,1)S(1)} all-to-all(bf16[4,576,512]{2,1,0:T(8,128)(2,1)S(1)} %bitcast.5), channel_id=1, replica_groups=mesh['row'=4,'col'=8] {'row'}, dimensions={0} | all-to-all | bytes 4718592 | tf_op jit(solution)/shard_map/all_to_all | solution.py:239
  658.5 0.4 convert_reduce_fusion
  658.9 1.1 broadcast_multiply_fusion
Async XLA Ops:
  7.2 90.2 %copy-start.2 = (f32[4,4]{1,0:T(4,128)S(1)}, f32[4,4]{1,0:T(4,128)}, u32[]{:S(2)}) copy-start(f32[4,4]{1,0:T(4,128)} %gate_ref.1) | copy-start | bytes 196
  7.2 40.7 %all-gather.7.cloned.1.call-start = ((), (), s32[]{:S(2)}) async-start(), calls=%async_computation.3 | async-start | bytes 2621440 | tf_op jit(solution)/shard_map/all_gather | solution.py:228
  7.9 89.4 %all-gather.5.cloned.1.call-start = ((), (), s32[]{:S(2)}) async-start(), calls=%async_computation.2 | async-start | bytes 4718592 | tf_op jit(solution)/shard_map/all_gather | solution.py:229
  8.7 126.8 %all-gather.9.cloned.1.call-start = ((), (), s32[]{:S(2)}) async-start(), calls=%async_computation.4 | async-start | bytes 2949120 | tf_op jit(solution)/shard_map/all_gather | solution.py:233
  10.7 231.3 %reduce-scatter.2.cloned.1.call-start = ((), (), s32[]{:S(2)}) async-start(), calls=%async_computation.5 | async-start | bytes 10616832 | tf_op jit(solution)/shard_map/reduce_scatter | solution.py:234
  97.3 2.2 copy-start
  99.5 1.6 copy-start.1
  107.0 35.3 %copy-start.3 = (bf16[1024,512]{1,0:T(8,128)(2,1)}, bf16[1024,512]{1,0:T(8,128)(2,1)S(1)}, u32[]{:S(2)}) copy-start(bf16[1024,512]{1,0:T(8,128)(2,1)S(1)} %shard_map.59) | copy-start | bytes 3145732
  142.3 351.3 %all-reduce.3.cloned.1.call-start = ((), (), s32[]{:S(2)}) async-start(), calls=%async_computation.7 | async-start | bytes 23592960 | tf_op jit(solution)/shard_map/psum | solution.py:235
  258.2 363.0 %all-gather.11.cloned.1.call-start = ((), (), s32[]{:S(2)}) async-start(), calls=%async_computation.6 | async-start | bytes 5308416 | tf_op jit(solution)/shard_map/all_gather | solution.py:237
  493.5 127.7 %copy-start.4 = (bf16[1024,512]{1,0:T(8,128)(2,1)S(1)}, bf16[1024,512]{1,0:T(8,128)(2,1)}, u32[]{:S(2)}) copy-start(bf16[1024,512]{1,0:T(8,128)(2,1)} %copy-done.3) | copy-start | bytes 3145732
Sparse Core Ops, SparseCore 0:
  9.9 38.0 all-gather.6
  49.5 47.7 all-gather.4
  99.7 35.6 all-gather.8
  142.4 99.5 reduce-scatter.1
  258.4 235.1 all-reduce.2
  570.3 50.8 all-gather.10

commit v2 on v1

--- a/solution.py
+++ b/solution.py
@@ -6,13 +6,15 @@
 from jax import lax
 from jax.experimental import pallas as pl
 from jax.experimental.pallas import tpu as pltpu
-from jax.sharding import PartitionSpec as P
+from jax.sharding import Mesh, PartitionSpec as P
 
 F32, BF16 = jnp.float32, jnp.bfloat16
 NN = (((1,), (0,)), ((), ()))
 NT = (((1,), (1,)), ((), ()))
 TN = (((0,), (0,)), ((), ()))
 VMEM = pl.BlockSpec(memory_space=pltpu.VMEM)
+SMEM = pl.BlockSpec(memory_space=pltpu.SMEM)
+ANY = pl.BlockSpec(memory_space=pl.ANY)
 TILE = 256
 ROUGH_STEPS = 5
 SETTLED = 1e-4
@@ -149,15 +151,108 @@
         eliminate(block, out_ref, work_ref)
 
 
-def basis_kernel(scale, *refs):
-    count = len(refs) - 10
-    gram_refs, sketch_ref = refs[:count], refs[count]
-    basis_ref, short_ref, high_ref, low_ref, basis_low_ref, inv_high_ref, inv_low_ref, inverse_ref, work_ref = refs[
-        count + 1 :
+def tiles_before(k, count):
+    return k * count - k * (k - 1) // 2
+
+
+def shared_tiles(count):
+    total = count * (count + 1) // 2
+    return total + total % 2
+
+
+def gram_kernel(parts, spot_ref, *refs):
+    piece_refs, gram_ref = refs[:parts], refs[parts]
+    sketch_ref, high_ref, low_ref, own_high_ref, own_low_ref, sems = refs[parts + 1 :]
+    spot = spot_ref[0]
+    size = sketch_ref.shape[0]
+    width, part = size // parts, TILE // parts
+    count = size // TILE
+    copies = [
+        pltpu.make_async_copy(
+            piece_refs[d], sketch_ref.at[pl.ds(pl.multiple_of((spot ^ d) * width, 16), width), :], sems.at[d]
+        )
+        for d in range(parts)
     ]
+    for copy in copies:
+        copy.start()
+    for copy in copies:
+        copy.wait()
+    for i in range(count):
+        here = slice(i * TILE, (i + 1) * TILE)
+        high_ref[here, :], low_ref[here, :] = halves(sketch_ref[here, :])
+    for i in range(count):
+        at = pl.multiple_of(i * TILE + spot * part, 16)
+        own_high_ref[i * part : (i + 1) * part, :] = high_ref[pl.ds(at, part), :]
+        own_low_ref[i * part : (i + 1) * part, :] = low_ref[pl.ds(at, part), :]
+    for k in range(count):
+        here = slice(k * TILE, (k + 1) * TILE)
+        start = tiles_before(k, count) * part
+        gram_ref[start : start + (count - k) * part, :] = dot3(
+            (own_high_ref[k * part :, :], own_low_ref[k * part :, :]), (high_ref[here, :], low_ref[here, :]), NT
+        )
+    total = tiles_before(count, count) * part
+    if total < gram_ref.shape[0]:
+        gram_ref[total:, :] = jnp.zeros((gram_ref.shape[0] - total, TILE), F32)
+
+
+def gram_share(spot, pieces):
+    parts = len(pieces)
+    width, rows = pieces[0].shape
+    size = parts * width
+    count, part = size // TILE, TILE // parts
+    return pl.pallas_call(
+        functools.partial(gram_kernel, parts),
+        out_shape=jax.ShapeDtypeStruct((shared_tiles(count) * part, TILE), F32),
+        in_specs=[SMEM] + [ANY] * parts,
+        out_specs=VMEM,
+        scratch_shapes=[
+            pltpu.VMEM((size, rows), F32),
+            pltpu.VMEM((size, rows), BF16),
+            pltpu.VMEM((size, rows), BF16),
+            pltpu.VMEM((count * part, rows), BF16),
+            pltpu.VMEM((count * part, rows), BF16),
+            pltpu.SemaphoreType.DMA((parts,)),
+        ],
+        compiler_params=pltpu.CompilerParams(vmem_limit_bytes=40 << 20),
+        cost_estimate=pl.CostEstimate(
+            flops=3 * size * size * rows // parts, bytes_accessed=8 * size * rows, transcendentals=0
+        ),
+    )(spot, *pieces)
+
+
+def basis_kernel(scale, parts, spot_ref, *refs):
+    shares = refs[: 2 * parts]
+    sketch_ref, basis_ref, short_ref, gram_ref, high_ref, low_ref, basis_low_ref, inv_high_ref, inv_low_ref = refs[
+        2 * parts : 2 * parts + 9
+    ]
+    inverse_ref, work_ref, sems = refs[2 * parts + 9 :]
+    size = high_ref.shape[0]
+    count, part = size // TILE, TILE // parts
+    half = gram_ref.shape[2] // part
+    spot, core = spot_ref[0], spot_ref[1]
+    copies = [
+        pltpu.make_async_copy(shares[e * parts + d], gram_ref.at[core ^ e, spot ^ d], sems.at[e * parts + d])
+        for e in range(2)
+        for d in range(parts)
+    ]
+    for copy in copies:
+        copy.start()
+    for copy in copies:
+        copy.wait()
+
+    def gram_tile(index):
+        if isinstance(index, int):
+            owner, at = index // half, index % half * part
+        else:
+            owner = (index >= half).astype(jnp.int32)
+            at = pl.multiple_of((index - owner * half) * part, part)
+        return scale * jnp.concatenate(
+            [gram_ref[owner, sub, pl.ds(at, part), :] for sub in range(parts)], axis=0
+        )
+
     for k in range(count):
         here, past = slice(k * TILE, (k + 1) * TILE), slice(0, k * TILE)
-        gram_ref = gram_refs[k]
+        first = tiles_before(k, count)
 
         def left_over(values, left):
             if k == 0:
@@ -165,18 +260,15 @@
             return values - dot3(left, (high_ref[here, past], low_ref[here, past]), NT)
 
         def factor_rows(at):
-            return high_ref[pl.ds(at, TILE), past], low_ref[pl.ds(at, TILE), past]
-
-        inverse_factor(
-            left_over(gram_ref[:TILE, :] * scale, factor_rows(k * TILE) if k else None), inverse_ref, work_ref
-        )
+            return (high_ref[pl.ds(at, TILE), past], low_ref[pl.ds(at, TILE), past]) if k else None
+
+        inverse_factor(left_over(gram_tile(first), factor_rows(k * TILE)), inverse_ref, work_ref)
         inv_high_ref[...], inv_low_ref[...] = halves(inverse_ref[...])
 
         def panel(i, carry):
             own = inv_high_ref[...], inv_low_ref[...]
             at = pl.multiple_of((k + 1 + i) * TILE, TILE)
-            gram_at = pl.multiple_of((1 + i) * TILE, TILE)
-            values = left_over(gram_ref[pl.ds(gram_at, TILE), :] * scale, factor_rows(at) if k else None)
+            values = left_over(gram_tile(first + 1 + i), factor_rows(at))
             solved = halves(dot3(halves(values), own, NT))
             high_ref[pl.ds(at, TILE), here], low_ref[pl.ds(at, TILE), here] = solved
             return carry
@@ -189,14 +281,16 @@
         short_ref[:, here], basis_low_ref[:, here] = halves(solved)
 
 
-def basis_of(gram_columns, sketch, scale):
+def basis_of(spots, shares, sketch, scale):
     rows, size = sketch.shape
+    parts = len(shares) // 2
     return pl.pallas_call(
-        functools.partial(basis_kernel, scale),
+        functools.partial(basis_kernel, scale, parts),
         out_shape=[jax.ShapeDtypeStruct((rows, size), F32), jax.ShapeDtypeStruct((rows, size), BF16)],
-        in_specs=[VMEM] * (len(gram_columns) + 1),
+        in_specs=[SMEM] + [ANY] * (2 * parts) + [VMEM],
         out_specs=[VMEM, VMEM],
         scratch_shapes=[
+            pltpu.VMEM((2, parts) + shares[0].shape, F32),
             pltpu.VMEM((size, size), BF16),
             pltpu.VMEM((size, size), BF16),
             pltpu.VMEM((rows, size), BF16),
@@ -204,48 +298,98 @@
             pltpu.VMEM((TILE, TILE), BF16),
             pltpu.VMEM((TILE, TILE), F32),
             pltpu.VMEM((TILE, TILE), F32),
+            pltpu.SemaphoreType.DMA((2 * parts,)),
         ],
         compiler_params=pltpu.CompilerParams(vmem_limit_bytes=56 << 20),
         cost_estimate=pl.CostEstimate(
             flops=24 * size**3, bytes_accessed=2 * size * size + 10 * rows * size, transcendentals=0
         ),
-    )(*gram_columns, sketch)
-
-
-def gram_columns_of(sketch):
-    rounded = lax.reduce_precision(sketch, 8, 7)
-    high, low = rounded.astype(BF16), (sketch - rounded).astype(BF16)
-    left = jnp.concatenate([high, high, low], axis=0)
-    right = jnp.concatenate([high, low, high], axis=0)
-    return tuple(
-        dot(left[:, at:], right[:, at : at + TILE], TN) for at in range(0, sketch.shape[1], TILE)
+    )(spots, *shares, sketch)
+
+
+def swapped(x, axis, distance):
+    return lax.ppermute(x, axis, [(i, i ^ distance) for i in range(lax.axis_size(axis))])
+
+
+def together(*arrays):
+    return lax.optimization_barrier(arrays)
+
+
+def row_pieces(x):
+    size = lax.axis_size("row")
+    if size != 4:
+        return [x] + [swapped(x, "row", d) for d in range(1, size)]
+    half = x.shape[0] // 2
+    first, second = x[:half], x[half:]
+    first_one, second_two, first_two, second_one = together(
+        swapped(first, "row", 1), swapped(second, "row", 2), swapped(first, "row", 2), swapped(second, "row", 1)
     )
+    first_three, second_three = together(swapped(first_one, "row", 2), swapped(second_two, "row", 1))
+    return [
+        x,
+        jnp.concatenate([first_one, second_one]),
+        jnp.concatenate([first_two, second_two]),
+        jnp.concatenate([first_three, second_three]),
+    ]
+
+
+def in_row_order(pieces, axis, place):
+    shape = list(pieces[0].shape)
+    step = shape[axis]
+    shape[axis] *= len(pieces)
+    whole = jnp.zeros(shape, pieces[0].dtype)
+    for d, piece in enumerate(pieces):
+        whole = lax.dynamic_update_slice_in_dim(whole, piece, (place ^ d) * step, axis)
+    return whole
 
 
 def on_device(left_site, right_site, gate, omega):
     rows_here = left_site.shape[0]
     total_rows = rows_here * lax.axis_size("row")
-    right_cols = lax.all_gather(right_site, "row", axis=0, tiled=True)
-    left_rows = lax.all_gather(left_site, "col", axis=1, tiled=True)
+    place, core = lax.axis_index("row"), lax.axis_index("core")
+    spot = place.astype(jnp.int32).reshape(1)
+    left_rows = lax.all_gather(left_site, COL, axis=1, tiled=True)
+    right_cols = in_row_order(row_pieces(right_site), 0, place)
     theta = theta_of(left_rows, right_cols, gate)
     cols_here = theta.shape[1]
-    omega_mine = lax.dynamic_slice_in_dim(omega, lax.axis_index("col") * cols_here, cols_here, 0)
-    omega_rows = lax.all_gather(omega_mine, "row", axis=1, tiled=True)
-    sketch = lax.psum_scatter(dot(theta, omega_rows), "col", scatter_dimension=0, tiled=True)
-    gram_columns = lax.psum(gram_columns_of(sketch), ("row", "col"))
-    basis, basis_short = basis_of(gram_columns, sketch, 1.0 / total_rows)
-    basis_rows = lax.all_gather(basis_short, "col", axis=0, tiled=True)
+
+    theta_rows = lax.all_to_all(theta, COL, 0, 1, tiled=True)
+    rows = theta_rows.shape[0]
+    theta_set = in_row_order(row_pieces(theta_rows), 0, place)
+    sketch_share = dot(omega, theta_set, (((0,), (1,)), ((), ())))
+    pieces = row_pieces(sketch_share)
+    sketch = in_row_order(
+        [lax.dynamic_slice_in_dim(piece, place * rows, rows, 1).T for piece in pieces], 1, place
+    )
+
+    share = gram_share(spot, pieces)
+    half = share.shape[0] // 2
+    kept = lax.dynamic_slice_in_dim(share, core * half, half, 0)
+    given = lax.dynamic_slice_in_dim(share, (1 - core) * half, half, 0)
+    kept = kept + swapped(given, "core", 1)
+    chips = lax.axis_size("chip")
+    kept = jnp.sum(lax.all_to_all(kept.reshape(chips, half // chips, TILE), "chip", 0, 0), axis=0)
+    mine = row_pieces(lax.all_gather(kept, "chip", axis=0, tiled=True))
+    others = [swapped(piece, "core", 1) for piece in mine]
+    spots = jnp.stack([place, core]).astype(jnp.int32)
+    basis, basis_short = basis_of(spots, mine + others, sketch, 1.0 / total_rows)
+
+    basis_rows = lax.all_gather(basis_short, COL, axis=0, tiled=True)
     folded = dot(basis_rows, theta, TN).astype(BF16)
-    pieces = lax.all_to_all(
-        folded.reshape(lax.axis_size("row"), -1, cols_here), "row", 0, 0, tiled=False
+    folded = folded.reshape(lax.axis_size("row"), -1, cols_here)
+    sums = lax.all_to_all(folded, "row", 0, 0)
+    projected = jnp.sum(sums.astype(F32), axis=0) / math.sqrt(total_rows)
+    return (basis, projected)
+
+
+COL = ("chip", "core")
+
+
+def solution(mesh):
+    row, col = mesh.devices.shape
+    split = Mesh(mesh.devices.reshape(row, col // 2, 2), ("row",) + COL)
+    in_specs = (P("row", COL), P("row", COL), P(), P(None, "row"))
+    out_specs = (P(("row",) + COL, None), P("row", COL))
+    return jax.shard_map(
+        on_device, mesh=split, in_specs=in_specs, out_specs=out_specs, check_vma=False
     )
-    projected = jnp.sum(pieces.astype(F32), axis=0) / math.sqrt(total_rows)
-    return (basis, projected)
-
-
-def solution(mesh):
-    in_specs = (P("row", "col"), P("row", "col"), P(), P(None, "row"))
-    out_specs = (P(("row", "col"), None), P("row", "col"))
-    return jax.shard_map(
-        on_device, mesh=mesh, in_specs=in_specs, out_specs=out_specs, check_vma=False
-    )

time: 675 us -> 538 us (0.80)
  waiting for transfers between devices: 502 us -> 224 us
  blocking collectives: 32 us -> 101 us
  local copies, waits for them, and re-layouts: 5.71 us -> 56.9 us
  starting transfers between devices: 0.24 us -> 25.8 us
  matrix products: 26.5 us -> 10.9 us
  other arithmetic: 3.19 us -> 12.7 us
    psum x1 -> x0, waiting for transfers between devices: 235 us -> none  [on_device(): gram_columns = lax.psum(gram_columns_of(sketch), ('row', 'col'))]
    ppermute x0 -> x29, waiting for transfers between devices: none -> 113 us  [swapped(): lax.ppermute(x, axis, [(i, i ^ distance) for i in range(lax.axis_size(axi...]
    reduce_scatter x1 -> x0, waiting for transfers between devices: 99.6 us -> none  [on_device(): lax.psum_scatter(dot(theta, omega_rows), 'col', scatter_dimension=0, tile...]
    all_to_all x1 -> x3, blocking collectives: 32 us -> 101 us  [the longest x1 39.4 us: on_device(): lax.all_to_all(kept.reshape(chips, half // chips, TILE), 'chip', 0, 0)]
    all_gather x4 -> x3, waiting for transfers between devices: 166 us -> 111 us  [the longest x1 51 us: on_device(): basis_rows = lax.all_gather(basis_short, COL, axis=0, tiled=True)]
    ppermute x0 -> x29, starting transfers between devices: none -> 25.5 us  [swapped(): lax.ppermute(x, axis, [(i, i ^ distance) for i in range(lax.axis_size(axi...]
    dynamic_update_slice x0 -> x9, local copies, waits for them, and re-layouts: none -> 16.8 us  [in_row_order(): lax.dynamic_update_slice_in_dim(whole, piece, (place ^ d) * step, axis)]
    dot_general x11 -> x2, matrix products: 26.5 us -> 10.9 us  [dot(): return lax.dot_general(a, b, dims, preferred_element_type=F32)]
  transfers between devices with their start and end apart: 6 -> 32, of which waited for: 6 -> 22; matrix products, arithmetic and copies ran while one was open for 0% -> 8% of each run, Pallas kernels for 1% -> 0%
where the time goes in v2:
time: 538 us; the launch traced here: 534 us
  waiting for transfers between devices  224 us (42%)
  blocking collectives  101 us (19%)
  Pallas kernels  88.4 us (16%)
  local copies, waits for them, and re-layouts  56.9 us (11%)
  starting transfers between devices  25.8 us (5%)
  between operations  14.4 us (3%)
  other arithmetic  12.7 us (2%)
  matrix products  10.9 us (2%)
    ppermute x29, waiting for transfers between devices, swapped(): lax.ppermute(x, axis, [(i, i ^ distance) for i in range(lax.axis_size(axi...  113 us
    pallas_call x1, Pallas kernels, basis_of(): pl.pallas_call(functools.partial(basis_kernel, scale, parts), out_shape=[...  77.9 us
    all_gather x1, waiting for transfers between devices, on_device(): basis_rows = lax.all_gather(basis_short, COL, axis=0, tiled=True)  51 us
    all_to_all x1, blocking collectives, on_device(): lax.all_to_all(kept.reshape(chips, half // chips, TILE), 'chip', 0, 0)  39.4 us
    all_gather x1, waiting for transfers between devices, on_device(): mine = row_pieces(lax.all_gather(kept, 'chip', axis=0, tiled=True))  34.6 us
    all_to_all x1, blocking collectives, on_device(): sums = lax.all_to_all(folded, 'row', 0, 0)  32 us
    all_to_all x1, blocking collectives, on_device(): theta_rows = lax.all_to_all(theta, COL, 0, 1, tiled=True)  29.5 us
    ppermute x29, starting transfers between devices, swapped(): lax.ppermute(x, axis, [(i, i ^ distance) for i in range(lax.axis_size(axi...  25.5 us
  transfers between devices with their start and end apart: 32, of which 22 were waited for; matrix products, arithmetic and copies ran while one was open for 8% of the time, Pallas kernels for 0%

profile of v2, /device:TPU:0, one launch (start us, length us, event | category | flops | bytes accessed | tf_op | source)
XLA Modules:
  0.0 534.5 jit_solution(5401025490753793530)
XLA Ops:
  9.1 3.0 collective-permute-start.3
  12.1 1.5 collective-permute-start.1
  14.2 5.0 collective-permute-done.3
  19.2 2.1 collective-permute-done.1
  21.3 4.2 collective-permute-done.2
  25.5 1.5 collective-permute-start.4
  28.8 3.9 collective-permute-done.4
  34.8 25.3 %all-gather.4.cloned.1.call-done.left_ref = bf16[1024,2048]{1,0:T(8,128)(2,1)} async-done(((bf16[1024,256]{1,0:T(8,128)(2,1)}), bf16[1024,2048]{1,0:T(8,128)(2,1)}) %all-gather.4.cloned.1.call-update) | async-done | bytes 4194320 | tf_op jit(solution)/shard_map/all_gather | solution.py:351
  60.1 2.2 copy-done.7
  62.3 5.9 %shard_map.59 = bf16[1024,512]{1,0:T(8,128)(2,1)S(1)} custom-call(f32[4,4]{1,0:T(4,128)S(1)} %copy-done.8, bf16[1024,2048]{1,0:T(8,128)(2,1)S(1)} %copy-done.7, bf16[2048,512]{1,0:T(8,128)(2,1)S(1)} %maximum_dynamic-update-slice_fusion.2.right_ref), custom_call_target="tpu_custom_call" | custom-call | flops 2147483648 | bytes 7340032 | tf_op jit(solution)/shard_map/pallas_call | solution.py:71
  68.9 29.5 %all_to_all.29 = bf16[8,128,512]{1,2,0:T(8,128)(2,1)S(1)} all-to-all(bf16[8,128,512]{1,2,0:T(8,128)(2,1)S(1)} %copy.24), channel_id=1, replica_groups=mesh['row'=4,'chip'=4,'core'=2] {'chip','core'}, dimensions={0} | all-to-all | bytes 2097152 | tf_op jit(solution)/shard_map/all_to_all | solution.py:356
  100.0 1.5 collective-permute-start.8
  101.5 1.5 collective-permute-start.6
  105.0 10.1 %collective-permute-done.8 = bf16[64,4096]{1,0:T(8,128)(2,1)S(1)} collective-permute-done((bf16[64,4096]{1,0:T(8,128)(2,1)}, bf16[64,4096]{1,0:T(8,128)(2,1)S(1)}, u32[]{:S(2)}, u32[]{:S(2)}) %collective-permute-start.8) | collective-permute-done | bytes 524320 | tf_op jit(solution)/shard_map/ppermute | solution.py:311
  115.0 1.6 collective-permute-done.6
  116.7 9.3 %collective-permute-done.9 = bf16[64,4096]{1,0:T(8,128)(2,1)S(1)} collective-permute-done((bf16[64,4096]{1,0:T(8,128)(2,1)S(1)}, bf16[64,4096]{1,0:T(8,128)(2,1)S(1)}, u32[]{:S(2)}, u32[]{:S(2)}) %collective-permute-start.9) | collective-permute-done | bytes 524320 | tf_op jit(solution)/shard_map/ppermute | solution.py:311
  126.7 1.5 collective-permute-start.11
  128.2 1.5 pad_maximum_fusion.3
  133.4 5.1 collective-permute-done.10
  142.3 5.7 %fusion.10 = f32[512,576]{0,1:T(8,128)S(1)} fusion(bf16[4096,576]{0,1:T(8,128)(2,1)} %param.7, bf16[512,4096]{0,1:T(8,128)(2,1)} %constant_dynamic-update-slice_fusion.6), kind=kOutput, calls=%fused_computation.43 | convolution fusion | flops 2415919104 | bytes 10092544 | tf_op jit(solution)/shard_map/dot_general | solution.py:24
  149.1 1.5 collective-permute-start.15
  153.1 12.2 %collective-permute-done.15 = f32[288,512]{1,0:T(8,128)S(1)} collective-permute-done((f32[288,512]{1,0:T(8,128)S(1)}, f32[288,512]{1,0:T(8,128)S(1)}, u32[]{:S(2)}, u32[]{:S(2)}) %collective-permute-start.15) | collective-permute-done | bytes 589856 | tf_op jit(solution)/shard_map/ppermute | solution.py:311
  165.4 1.7 collective-permute-done.13
  167.0 9.5 %collective-permute-done.14 = f32[288,512]{1,0:T(8,128)} collective-permute-done((f32[288,512]{1,0:T(8,128)S(1)}, f32[288,512]{1,0:T(8,128)}, u32[]{:S(2)}, u32[]{:S(2)}) %collective-permute-start.14) | collective-permute-done | bytes 589856 | tf_op jit(solution)/shard_map/ppermute | solution.py:311
  179.4 1.6 copy.33
  181.3 1.6 copy.32
  184.3 2.7 copy.36.refs_1_
  188.4 2.7 copy.37.refs_2_
  192.5 1.6 copy.35
  200.9 4.7 shard_map.60
  206.9 3.7 collective-permute-done.18
  210.5 1.6 dynamic-slice_add_fusion
  212.1 39.4 %all_to_all.30 = f32[4,368,256]{2,1,0:T(8,128)S(1)} all-to-all(f32[4,368,256]{2,1,0:T(8,128)S(1)} %bitcast.26), channel_id=1, replica_groups=mesh['row'=4,'chip'=4,'core'=2] {'chip'}, dimensions={0} | all-to-all | bytes 3014656 | tf_op jit(solution)/shard_map/all_to_all | solution.py:371
  252.6 34.6 %all-gather.6.cloned.1.call-done.refs_0_ = f32[1472,256]{1,0:T(8,128)} async-done(((f32[368,256]{1,0:T(8,128)}), f32[1472,256]{1,0:T(8,128)}) %all-gather.6.cloned.1.call-update) | async-done | bytes 1507344 | tf_op jit(solution)/shard_map/all_gather | solution.py:372
  288.7 1.5 collective-permute-start.22
  290.2 1.5 collective-permute-start.20
  292.8 15.7 %collective-permute-done.22 = f32[736,256]{1,0:T(8,128)S(1)} collective-permute-done((f32[736,256]{1,0:T(8,128)S(1)}, f32[736,256]{1,0:T(8,128)S(1)}, u32[]{:S(2)}, u32[]{:S(2)}) %collective-permute-start.22) | collective-permute-done | bytes 753696 | tf_op jit(solution)/shard_map/ppermute | solution.py:311
  310.0 13.9 %collective-permute-done.21 = f32[736,256]{1,0:T(8,128)S(1)} collective-permute-done((f32[736,256]{1,0:T(8,128)S(1)}, f32[736,256]{1,0:T(8,128)S(1)}, u32[]{:S(2)}, u32[]{:S(2)}) %collective-permute-start.21) | collective-permute-done | bytes 753696 | tf_op jit(solution)/shard_map/ppermute | solution.py:311
  323.9 1.5 collective-permute-start.23
  330.2 10.3 %collective-permute-done.23 = f32[736,256]{1,0:T(8,128)S(1)} collective-permute-done((f32[736,256]{1,0:T(8,128)S(1)}, f32[736,256]{1,0:T(8,128)S(1)}, u32[]{:S(2)}, u32[]{:S(2)}) %collective-permute-start.23) | collective-permute-done | bytes 753696 | tf_op jit(solution)/shard_map/ppermute | solution.py:311
  346.5 3.3 dynamic_update_slice.44
  350.0 3.6 dynamic_update_slice.45
  353.8 3.2 dynamic_update_slice.46
  357.1 2.9 dynamic_update_slice.47.refs_8_
  360.1 77.9 %shard_map.61 = (f32[128,2304]{1,0:T(8,128)}, bf16[128,2304]{1,0:T(8,128)(2,1)}) custom-call(s32[2]{0:T(128)} %pad_add_fusion.spot_ref, f32[1472,256]{1,0:T(8,128)} %all-gather.6.cloned.1.call-done.refs_0_, f32[1472,256]{1,0:T(8,128)} %constant_dynamic-update-slice_fusion.refs_1_, f32[1472,256]{1,0:T(8,128)} %constant_dynamic-update-slice_fusion.2.refs_2_, ...), custom_call_target="tpu_custom_call" | custom-call | flops 293534171136 | bytes 13565952 | tf_op jit(solution)/shard_map/pallas_call | solution.py:287
  438.0 51.0 %all-gather.8.cloned.1.call-done = bf16[1024,2304]{1,0:T(8,128)(2,1)} async-done(((bf16[128,2304]{1,0:T(8,128)(2,1)}), bf16[1024,2304]{1,0:T(8,128)(2,1)}) %all-gather.8.cloned.1.call-update) | async-done | bytes 4718608 | tf_op jit(solution)/shard_map/all_gather | solution.py:377
  489.0 5.2 convolution_convert_fusion
  494.3 32.0 %all_to_all.31 = bf16[4,576,512]{2,1,0:T(8,128)(2,1)S(1)} all-to-all(bf16[4,576,512]{2,1,0:T(8,128)(2,1)S(1)} %bitcast.29), channel_id=1, replica_groups=mesh['row'=4,'chip'=4,'core'=2] {'row'}, dimensions={0} | all-to-all | bytes 4718592 | tf_op jit(solution)/shard_map/all_to_all | solution.py:380
  (131 shorter events, 55.5 us)
Async XLA Ops:
  7.2 53.0 %all-gather.4.cloned.1.call-start = ((), (), s32[]{:S(2)}) async-start(), calls=%async_computation.3 | async-start | bytes 4718592 | tf_op jit(solution)/shard_map/all_gather | solution.py:351
  7.9 19.8 %copy-start.22 = (bf16[512,512]{1,0:T(8,128)(2,1)S(1)}, bf16[512,512]{1,0:T(8,128)(2,1)}, u32[]{:S(2)}) copy-start(bf16[512,512]{1,0:T(8,128)(2,1)} %param.5) | copy-start | bytes 1572868
  7.9 279.3 %all-gather.6.cloned.1.call-start = ((), (), s32[]{:S(2)}) async-start(), calls=%async_computation.4 | async-start | bytes 1884160 | tf_op jit(solution)/shard_map/all_gather | solution.py:372
  9.1 10.1 %collective-permute-start.3 = (bf16[256,512]{1,0:T(8,128)(2,1)S(1)}, bf16[256,512]{1,0:T(8,128)(2,1)S(1)}, u32[]{:S(2)}, u32[]{:S(2)}) collective-permute-start(bf16[256,512]{1,0:T(8,128)(2,1)S(1)} %get-tuple-element.60), channel_id=1, source_target_pairs={{0,8},{8,0},{16,24},{24,16},{1,9},{9,1},{17,25},{25,17},{2,10},{10... | collective-permute-start | bytes 786440 | tf_op jit(solution)/shard_map/ppermute | solution.py:311
  12.1 9.2 %collective-permute-start.1 = (bf16[256,512]{1,0:T(8,128)(2,1)S(1)}, bf16[256,512]{1,0:T(8,128)(2,1)S(1)}, u32[]{:S(2)}, u32[]{:S(2)}) collective-permute-start(bf16[256,512]{1,0:T(8,128)(2,1)S(1)} %get-tuple-element.60), channel_id=1, source_target_pairs={{0,16},{8,24},{16,0},{24,8},{1,17},{9,25},{17,1},{25,9},{2,18},{10... | collective-permute-start | bytes 786440 | tf_op jit(solution)/shard_map/ppermute | solution.py:311
  13.6 11.9 %collective-permute-start.2 = (bf16[256,512]{1,0:T(8,128)(2,1)S(1)}, bf16[256,512]{1,0:T(8,128)(2,1)S(1)}, u32[]{:S(2)}, u32[]{:S(2)}) collective-permute-start(bf16[256,512]{1,0:T(8,128)(2,1)S(1)} %get-tuple-element.61), channel_id=1, source_target_pairs={{0,16},{8,24},{16,0},{24,8},{1,17},{9,25},{17,1},{25,9},{2,18},{10... | collective-permute-start | bytes 786440 | tf_op jit(solution)/shard_map/ppermute | solution.py:311
  14.1 11.4 %collective-permute-start = (bf16[256,512]{1,0:T(8,128)(2,1)S(1)}, bf16[256,512]{1,0:T(8,128)(2,1)}, u32[]{:S(2)}, u32[]{:S(2)}) collective-permute-start(bf16[256,512]{1,0:T(8,128)(2,1)S(1)} %get-tuple-element.61), channel_id=1, source_target_pairs={{0,8},{8,0},{16,24},{24,16},{1,9},{9,1},{17,25},{25,17},{2,10},{10... | collective-permute-start | bytes 786440 | tf_op jit(solution)/shard_map/ppermute | solution.py:311
  25.5 7.3 %collective-permute-start.4 = (bf16[256,512]{1,0:T(8,128)(2,1)}, bf16[256,512]{1,0:T(8,128)(2,1)}, u32[]{:S(2)}, u32[]{:S(2)}) collective-permute-start(bf16[256,512]{1,0:T(8,128)(2,1)} %collective-permute-done), channel_id=1, source_target_pairs={{0,16},{8,24},{16,0},{24,8},{1,17},{9,25},{17,1},{25,9},{2,18},{10... | collective-permute-start | bytes 786440 | tf_op jit(solution)/shard_map/ppermute | solution.py:311
  27.0 6.8 %collective-permute-start.5 = (bf16[256,512]{1,0:T(8,128)(2,1)S(1)}, bf16[256,512]{1,0:T(8,128)(2,1)}, u32[]{:S(2)}, u32[]{:S(2)}) collective-permute-start(bf16[256,512]{1,0:T(8,128)(2,1)S(1)} %collective-permute-done.1), channel_id=1, source_target_pairs={{0,8},{8,0},{16,24},{24,16},{1,9},{9,1},{17,25},{25,17},{2,10},{10... | collective-permute-start | bytes 786440 | tf_op jit(solution)/shard_map/ppermute | solution.py:311
  27.7 32.4 %copy-start.8 = (f32[4,4]{1,0:T(4,128)S(1)}, f32[4,4]{1,0:T(4,128)}, u32[]{:S(2)}) copy-start(f32[4,4]{1,0:T(4,128)} %gate_ref.1) | copy-start | bytes 196
  60.1 2.2 copy-start.7
  68.2 30.2 %copy-start.5 = (bf16[1024,512]{1,0:T(8,128)(2,1)}, bf16[1024,512]{1,0:T(8,128)(2,1)S(1)}, u32[]{:S(2)}) copy-start(bf16[1024,512]{1,0:T(8,128)(2,1)S(1)} %shard_map.59) | copy-start | bytes 3145732
  100.0 15.1 %collective-permute-start.8 = (bf16[64,4096]{1,0:T(8,128)(2,1)}, bf16[64,4096]{1,0:T(8,128)(2,1)S(1)}, u32[]{:S(2)}, u32[]{:S(2)}) collective-permute-start(bf16[64,4096]{1,0:T(8,128)(2,1)} %copy.40), channel_id=1, source_target_pairs={{0,16},{8,24},{16,0},{24,8},{1,17},{9,25},{17,1},{25,9},{2,18},{10... | collective-permute-start | bytes 1572872 | tf_op jit(solution)/shard_map/ppermute | solution.py:311
  101.5 15.2 %collective-permute-start.6 = (bf16[64,4096]{1,0:T(8,128)(2,1)}, bf16[64,4096]{1,0:T(8,128)(2,1)}, u32[]{:S(2)}, u32[]{:S(2)}) collective-permute-start(bf16[64,4096]{1,0:T(8,128)(2,1)} %copy.40), channel_id=1, source_target_pairs={{0,8},{8,0},{16,24},{24,16},{1,9},{9,1},{17,25},{25,17},{2,10},{10... | collective-permute-start | bytes 1572872 | tf_op jit(solution)/shard_map/ppermute | solution.py:311
  103.3 22.7 %collective-permute-start.9 = (bf16[64,4096]{1,0:T(8,128)(2,1)S(1)}, bf16[64,4096]{1,0:T(8,128)(2,1)S(1)}, u32[]{:S(2)}, u32[]{:S(2)}) collective-permute-start(bf16[64,4096]{1,0:T(8,128)(2,1)S(1)} %copy.41), channel_id=1, source_target_pairs={{0,8},{8,0},{16,24},{24,16},{1,9},{9,1},{17,25},{25,17},{2,10},{10... | collective-permute-start | bytes 1572872 | tf_op jit(solution)/shard_map/ppermute | solution.py:311
  103.9 22.0 %collective-permute-start.7 = (bf16[64,4096]{1,0:T(8,128)(2,1)S(1)}, bf16[64,4096]{1,0:T(8,128)(2,1)}, u32[]{:S(2)}, u32[]{:S(2)}) collective-permute-start(bf16[64,4096]{1,0:T(8,128)(2,1)S(1)} %copy.41), channel_id=1, source_target_pairs={{0,16},{8,24},{16,0},{24,8},{1,17},{9,25},{17,1},{25,9},{2,18},{10... | collective-permute-start | bytes 1572872 | tf_op jit(solution)/shard_map/ppermute | solution.py:311
  105.0 24.7 %copy-start.21 = (bf16[512,4096]{0,1:T(8,128)(2,1)}, bf16[512,4096]{0,1:T(8,128)(2,1)S(1)}, u32[]{:S(2)}) copy-start(bf16[512,4096]{0,1:T(8,128)(2,1)S(1)} %constant_dynamic-update-slice_fusion.9) | copy-start | bytes 12582916
  125.9 12.5 %collective-permute-start.10 = (bf16[64,4096]{1,0:T(8,128)(2,1)}, bf16[64,4096]{1,0:T(8,128)(2,1)}, u32[]{:S(2)}, u32[]{:S(2)}) collective-permute-start(bf16[64,4096]{1,0:T(8,128)(2,1)} %collective-permute-done.6), channel_id=1, source_target_pairs={{0,16},{8,24},{16,0},{24,8},{1,17},{9,25},{17,1},{25,9},{2,18},{10... | collective-permute-start | bytes 1572872 | tf_op jit(solution)/shard_map/ppermute | solution.py:311
  126.7 12.5 %collective-permute-start.11 = (bf16[64,4096]{1,0:T(8,128)(2,1)}, bf16[64,4096]{1,0:T(8,128)(2,1)}, u32[]{:S(2)}, u32[]{:S(2)}) collective-permute-start(bf16[64,4096]{1,0:T(8,128)(2,1)} %collective-permute-done.7), channel_id=1, source_target_pairs={{0,8},{8,0},{16,24},{24,16},{1,9},{9,1},{17,25},{25,17},{2,10},{10... | collective-permute-start | bytes 1572872 | tf_op jit(solution)/shard_map/ppermute | solution.py:311
  149.1 16.3 %collective-permute-start.15 = (f32[288,512]{1,0:T(8,128)S(1)}, f32[288,512]{1,0:T(8,128)S(1)}, u32[]{:S(2)}, u32[]{:S(2)}) collective-permute-start(f32[288,512]{1,0:T(8,128)S(1)} %get-tuple-element.56), channel_id=1, source_target_pairs={{0,8},{8,0},{16,24},{24,16},{1,9},{9,1},{17,25},{25,17},{2,10},{10... | collective-permute-start | bytes 1769480 | tf_op jit(solution)/shard_map/ppermute | solution.py:311
  150.6 16.4 %collective-permute-start.13 = (f32[288,512]{1,0:T(8,128)S(1)}, f32[288,512]{1,0:T(8,128)}, u32[]{:S(2)}, u32[]{:S(2)}) collective-permute-start(f32[288,512]{1,0:T(8,128)S(1)} %get-tuple-element.56), channel_id=1, source_target_pairs={{0,16},{8,24},{16,0},{24,8},{1,17},{9,25},{17,1},{25,9},{2,18},{10... | collective-permute-start | bytes 1769480 | tf_op jit(solution)/shard_map/ppermute | solution.py:311
  151.5 25.0 %collective-permute-start.14 = (f32[288,512]{1,0:T(8,128)S(1)}, f32[288,512]{1,0:T(8,128)}, u32[]{:S(2)}, u32[]{:S(2)}) collective-permute-start(f32[288,512]{1,0:T(8,128)S(1)} %get-tuple-element.57), channel_id=1, source_target_pairs={{0,16},{8,24},{16,0},{24,8},{1,17},{9,25},{17,1},{25,9},{2,18},{10... | collective-permute-start | bytes 1769480 | tf_op jit(solution)/shard_map/ppermute | solution.py:311
  152.7 23.9 %collective-permute-start.12 = (f32[288,512]{1,0:T(8,128)S(1)}, f32[288,512]{1,0:T(8,128)}, u32[]{:S(2)}, u32[]{:S(2)}) collective-permute-start(f32[288,512]{1,0:T(8,128)S(1)} %get-tuple-element.57), channel_id=1, source_target_pairs={{0,8},{8,0},{16,24},{24,16},{1,9},{9,1},{17,25},{25,17},{2,10},{10... | collective-permute-start | bytes 1769480 | tf_op jit(solution)/shard_map/ppermute | solution.py:311
  176.6 14.6 %collective-permute-start.16 = (f32[288,512]{1,0:T(8,128)}, f32[288,512]{1,0:T(8,128)}, u32[]{:S(2)}, u32[]{:S(2)}) collective-permute-start(f32[288,512]{1,0:T(8,128)} %collective-permute-done.12), channel_id=1, source_target_pairs={{0,16},{8,24},{16,0},{24,8},{1,17},{9,25},{17,1},{25,9},{2,18},{10... | collective-permute-start | bytes 1769480 | tf_op jit(solution)/shard_map/ppermute | solution.py:311
  177.4 13.7 %collective-permute-start.17 = (f32[288,512]{1,0:T(8,128)}, f32[288,512]{1,0:T(8,128)}, u32[]{:S(2)}, u32[]{:S(2)}) collective-permute-start(f32[288,512]{1,0:T(8,128)} %collective-permute-done.13), channel_id=1, source_target_pairs={{0,8},{8,0},{16,24},{24,16},{1,9},{9,1},{17,25},{25,17},{2,10},{10... | collective-permute-start | bytes 1769480 | tf_op jit(solution)/shard_map/ppermute | solution.py:311
  179.4 3.5 copy-start.13
  181.0 6.0 %copy-start.9 = (f32[288,512]{0,1:T(8,128)}, f32[288,512]{0,1:T(8,128)S(1)}, u32[]{:S(2)}) copy-start(f32[288,512]{0,1:T(8,128)S(1)} %copy.33) | copy-start | bytes 1769476
  181.3 3.0 copy-start.15
  182.9 4.1 copy-start.11
  206.9 3.7 collective-permute-start.18
  252.4 236.6 %all-gather.8.cloned.1.call-start = ((), (), s32[]{:S(2)}) async-start(), calls=%async_computation.5 | async-start | bytes 5308416 | tf_op jit(solution)/shard_map/all_gather | solution.py:377
  288.7 19.8 %collective-permute-start.22 = (f32[736,256]{1,0:T(8,128)S(1)}, f32[736,256]{1,0:T(8,128)S(1)}, u32[]{:S(2)}, u32[]{:S(2)}) collective-permute-start(f32[736,256]{1,0:T(8,128)S(1)} %get-tuple-element.54), channel_id=1, source_target_pairs={{0,8},{8,0},{16,24},{24,16},{1,9},{9,1},{17,25},{25,17},{2,10},{10... | collective-permute-start | bytes 2261000 | tf_op jit(solution)/shard_map/ppermute | solution.py:311
  290.2 19.8 %collective-permute-start.20 = (f32[736,256]{1,0:T(8,128)S(1)}, f32[736,256]{1,0:T(8,128)S(1)}, u32[]{:S(2)}, u32[]{:S(2)}) collective-permute-start(f32[736,256]{1,0:T(8,128)S(1)} %get-tuple-element.54), channel_id=1, source_target_pairs={{0,16},{8,24},{16,0},{24,8},{1,17},{9,25},{17,1},{25,9},{2,18},{10... | collective-permute-start | bytes 2261000 | tf_op jit(solution)/shard_map/ppermute | solution.py:311
  291.7 32.2 %collective-permute-start.21 = (f32[736,256]{1,0:T(8,128)S(1)}, f32[736,256]{1,0:T(8,128)S(1)}, u32[]{:S(2)}, u32[]{:S(2)}) collective-permute-start(f32[736,256]{1,0:T(8,128)S(1)} %get-tuple-element.55), channel_id=1, source_target_pairs={{0,16},{8,24},{16,0},{24,8},{1,17},{9,25},{17,1},{25,9},{2,18},{10... | collective-permute-start | bytes 2261000 | tf_op jit(solution)/shard_map/ppermute | solution.py:311
  292.2 31.6 %collective-permute-start.19 = (f32[736,256]{1,0:T(8,128)S(1)}, f32[736,256]{1,0:T(8,128)S(1)}, u32[]{:S(2)}, u32[]{:S(2)}) collective-permute-start(f32[736,256]{1,0:T(8,128)S(1)} %get-tuple-element.55), channel_id=1, source_target_pairs={{0,8},{8,0},{16,24},{24,16},{1,9},{9,1},{17,25},{25,17},{2,10},{10... | collective-permute-start | bytes 2261000 | tf_op jit(solution)/shard_map/ppermute | solution.py:311
  323.9 16.6 %collective-permute-start.23 = (f32[736,256]{1,0:T(8,128)S(1)}, f32[736,256]{1,0:T(8,128)S(1)}, u32[]{:S(2)}, u32[]{:S(2)}) collective-permute-start(f32[736,256]{1,0:T(8,128)S(1)} %collective-permute-done.19), channel_id=1, source_target_pairs={{0,16},{8,24},{16,0},{24,8},{1,17},{9,25},{17,1},{25,9},{2,18},{10... | collective-permute-start | bytes 2261000 | tf_op jit(solution)/shard_map/ppermute | solution.py:311
  325.4 16.3 %collective-permute-start.24 = (f32[736,256]{1,0:T(8,128)S(1)}, f32[736,256]{1,0:T(8,128)S(1)}, u32[]{:S(2)}, u32[]{:S(2)}) collective-permute-start(f32[736,256]{1,0:T(8,128)S(1)} %collective-permute-done.20), channel_id=1, source_target_pairs={{0,8},{8,0},{16,24},{24,16},{1,9},{9,1},{17,25},{25,17},{2,10},{10... | collective-permute-start | bytes 2261000 | tf_op jit(solution)/shard_map/ppermute | solution.py:311
  325.9 34.1 %collective-permute-start.25 = (f32[1472,256]{1,0:T(8,128)}, f32[1472,256]{1,0:T(8,128)}, u32[]{:S(2)}, u32[]{:S(2)}) collective-permute-start(f32[1472,256]{1,0:T(8,128)} %all-gather.6.cloned.1.call-done.refs_0_), channel_id=1, source_target_pairs={{0,1},{1,0},{2,3},{3,2},{4,5},{5,4},{6,7},{7,6},{8,9},{9,8},{10,11... | collective-permute-start | bytes 4521992 | tf_op jit(solution)/shard_map/ppermute | solution.py:311
  327.8 32.2 %collective-permute-start.26 = (f32[1472,256]{1,0:T(8,128)}, f32[1472,256]{1,0:T(8,128)}, u32[]{:S(2)}, u32[]{:S(2)}) collective-permute-start(f32[1472,256]{1,0:T(8,128)} %constant_dynamic-update-slice_fusion.refs_1_), channel_id=1, source_target_pairs={{0,1},{1,0},{2,3},{3,2},{4,5},{5,4},{6,7},{7,6},{8,9},{9,8},{10,11... | collective-permute-start | bytes 4521992 | tf_op jit(solution)/shard_map/ppermute | solution.py:311
  330.2 29.8 %collective-permute-start.27 = (f32[1472,256]{1,0:T(8,128)}, f32[1472,256]{1,0:T(8,128)}, u32[]{:S(2)}, u32[]{:S(2)}) collective-permute-start(f32[1472,256]{1,0:T(8,128)} %constant_dynamic-update-slice_fusion.2.refs_2_), channel_id=1, source_target_pairs={{0,1},{1,0},{2,3},{3,2},{4,5},{5,4},{6,7},{7,6},{8,9},{9,8},{10,11... | collective-permute-start | bytes 4521992 | tf_op jit(solution)/shard_map/ppermute | solution.py:311
  343.6 16.5 %collective-permute-start.28 = (f32[1472,256]{1,0:T(8,128)}, f32[1472,256]{1,0:T(8,128)}, u32[]{:S(2)}, u32[]{:S(2)}) collective-permute-start(f32[1472,256]{1,0:T(8,128)} %constant_dynamic-update-slice_fusion.4.refs_3_), channel_id=1, source_target_pairs={{0,1},{1,0},{2,3},{3,2},{4,5},{5,4},{6,7},{7,6},{8,9},{9,8},{10,11... | collective-permute-start | bytes 4521992 | tf_op jit(solution)/shard_map/ppermute | solution.py:311
  344.2 5.7 %copy-start.14 = (f32[288,512]{0,1:T(8,128)S(1)}, f32[288,512]{0,1:T(8,128)}, u32[]{:S(2)}) copy-start(f32[288,512]{0,1:T(8,128)} %copy-done.13) | copy-start | bytes 1769476
  344.2 5.7 %copy-start.16 = (f32[288,512]{0,1:T(8,128)S(1)}, f32[288,512]{0,1:T(8,128)}, u32[]{:S(2)}) copy-start(f32[288,512]{0,1:T(8,128)} %copy-done.15) | copy-start | bytes 1769476
  346.5 7.1 %copy-start.10 = (f32[288,512]{0,1:T(8,128)S(1)}, f32[288,512]{0,1:T(8,128)}, u32[]{:S(2)}) copy-start(f32[288,512]{0,1:T(8,128)} %copy-done.9) | copy-start | bytes 1769476
  346.5 7.1 %copy-start.12 = (f32[288,512]{0,1:T(8,128)S(1)}, f32[288,512]{0,1:T(8,128)}, u32[]{:S(2)}) copy-start(f32[288,512]{0,1:T(8,128)} %copy-done.11) | copy-start | bytes 1769476
  350.0 7.0 %copy-start.18 = (f32[288,512]{0,1:T(8,128)S(1)}, f32[288,512]{0,1:T(8,128)}, u32[]{:S(2)}) copy-start(f32[288,512]{0,1:T(8,128)} %copy-done.17) | copy-start | bytes 1769476
  350.0 7.0 %copy-start.20 = (f32[288,512]{0,1:T(8,128)S(1)}, f32[288,512]{0,1:T(8,128)}, u32[]{:S(2)}) copy-start(f32[288,512]{0,1:T(8,128)} %copy-done.19) | copy-start | bytes 1769476
  360.1 128.9 %copy-start.6 = (bf16[1024,512]{1,0:T(8,128)(2,1)S(1)}, bf16[1024,512]{1,0:T(8,128)(2,1)}, u32[]{:S(2)}) copy-start(bf16[1024,512]{1,0:T(8,128)(2,1)} %copy-done.5) | copy-start | bytes 3145732
  (8 other events, 10.6 us)
Sparse Core Ops, SparseCore 0:
  9.6 50.4 all-gather.3
  252.5 34.6 all-gather.5
  438.1 50.8 all-gather.7

commit v3 on v1

v3 whole, which is shorter than its diff:
```python
import functools
import math

import jax
import jax.numpy as jnp
from jax import lax
from jax.experimental import pallas as pl
from jax.experimental.pallas import tpu as pltpu
from jax.sharding import Mesh, PartitionSpec as P

F32, BF16 = jnp.float32, jnp.bfloat16
NN = (((1,), (0,)), ((), ()))
NT = (((1,), (1,)), ((), ()))
TN = (((0,), (0,)), ((), ()))
VMEM = pl.BlockSpec(memory_space=pltpu.VMEM)
SMEM = pl.BlockSpec(memory_space=pltpu.SMEM)
ANY = pl.BlockSpec(memory_space=pl.ANY)
TILE = 256
ROUGH_STEPS = 5
SETTLED = 1e-4


def dot(a, b, dims=NN):
    return lax.dot_general(a, b, dims, preferred_element_type=F32)


def halves(x):
    high = x.astype(BF16)
    return high, (x - high.astype(F32)).astype(BF16)


def dot3(a, b, dims=NN):
    return dot(a[0], b[0], dims) + dot(a[0], b[1], dims) + dot(a[1], b[0], dims)


def positions(shape):
    return lax.broadcasted_iota(jnp.int32, shape, 0), lax.broadcasted_iota(jnp.int32, shape, 1)


def theta_kernel(chips, gate_ref, spot_ref, *refs):
    left_refs, right_ref, theta_ref = refs[:-2], refs[-2], refs[-1]
    depth = left_refs[0].shape[1]
    bare = None
    for n, left_ref in enumerate(left_refs):
        e, d = divmod(n, chips)
        at = ((spot_ref[2] ^ d) * 2 + (spot_ref[1] ^ e)) * depth
        product = dot(left_ref[...], right_ref[pl.ds(pl.multiple_of(at, depth), depth), :])
        bare = product if bare is None else bare + product
    rows, cols = bare.shape
    row, col = positions((rows, cols))
    row_odd, col_odd = row % 2 == 1, col % 2 == 1

    def partner_row(x):
        return jnp.where(row_odd, pltpu.roll(x, 1, 0), pltpu.roll(x, rows - 1, 0))

    def partner_col(x):
        return jnp.where(col_odd, pltpu.roll(x, 1, 1), pltpu.roll(x, cols - 1, 1))

    def weight(flip_row, flip_col):
        def entry(s, t):
            return gate_ref[2 * s + t, 2 * (s ^ flip_row) + (t ^ flip_col)]

        return jnp.where(
            row_odd,
            jnp.where(col_odd, entry(1, 1), entry(1, 0)),
            jnp.where(col_odd, entry(0, 1), entry(0, 0)),
        )

    across = partner_row(bare)
    mixed = weight(0, 0) * bare + weight(0, 1) * partner_col(bare)
    mixed = mixed + weight(1, 0) * across + weight(1, 1) * partner_col(across)
    theta_ref[...] = mixed.astype(BF16)


def theta_of(gate, spots, pieces, right):
    rows, depth = pieces[0].shape
    cols = right.shape[1]
    tile = min(TILE, rows)
    return pl.pallas_call(
        functools.partial(theta_kernel, len(pieces) // 2),
        grid=(rows // tile,),
        out_shape=jax.ShapeDtypeStruct((rows, cols), BF16),
        in_specs=[SMEM, SMEM]
        + [pl.BlockSpec((tile, depth), lambda i: (i, 0))] * len(pieces)
        + [pl.BlockSpec(right.shape, lambda i: (0, 0))],
        out_specs=pl.BlockSpec((tile, cols), lambda i: (i, 0)),
        compiler_params=pltpu.CompilerParams(vmem_limit_bytes=32 << 20),
        cost_estimate=pl.CostEstimate(
            flops=rows * cols,
            bytes_accessed=rows * cols,
            transcendentals=0,
        ),
    )(gate, spots, *pieces, right)


def eliminate(block, out_ref, work_ref):
    tile = block.shape[0]
    row, col = positions((tile, tile))
    work_ref[...] = block
    out_ref[...] = jnp.where(row == col, 1.0, 0.0).astype(F32)

    def column(j, carry):
        values = work_ref[...]
        pivot_row = work_ref[pl.ds(j, 1), :]
        pivot_col = jnp.sum(jnp.where(col == j, values, 0.0), axis=1, keepdims=True)
        pivot = jnp.sum(jnp.where(col[:1] == j, pivot_row, 0.0), axis=1, keepdims=True)
        root = 1.0 / jnp.sqrt(pivot)
        done = out_ref[pl.ds(j, 1), :] * root
        factor = jnp.where(row[:, :1] > j, pivot_col * root, 0.0)
        work_ref[...] = values - factor * (pivot_row * root)
        out_ref[...] = out_ref[...] - factor * done
        out_ref[pl.ds(j, 1), :] = done
        return carry

    lax.fori_loop(0, tile, column, 0)


def inverse_factor(block, out_ref, work_ref):
    row, col = positions(block.shape)
    same, below = row == col, row > col
    diagonal = jnp.where(same, block, 0.0)
    scale_row = lax.rsqrt(jnp.sum(diagonal, axis=0, keepdims=True))
    scale_col = lax.rsqrt(jnp.sum(diagonal, axis=1, keepdims=True))
    normal = block * scale_row * scale_col
    parts = halves(normal)
    near = 0.5 * normal
    inverse = jnp.where(same, math.sqrt(0.5), 0.0).astype(F32)
    for _ in range(ROUGH_STEPS):
        step = jnp.where(below, -near, jnp.where(same, 1.5 - 0.5 * near, 0.0)).astype(BF16)
        inverse = dot(step, inverse.astype(BF16))
        near = dot(dot(step, near.astype(BF16)).astype(BF16), step, NT)

    def polish(inverse):
        own = halves(inverse)
        rest = dot3(halves(dot3(own, parts)), own, NT) - jnp.where(same, 1.0, 0.0)
        shift = jnp.where(below, rest, jnp.where(same, 0.5 * rest, 0.0)).astype(BF16)
        return inverse - dot(shift, own[0]), jnp.sum(rest * rest)

    inverse, _ = polish(inverse)
    inverse, gap = polish(inverse)
    out_ref[...] = inverse

    def again(state):
        inverse, gap = polish(out_ref[...])
        out_ref[...] = inverse
        return state[0] + 1, gap

    _, gap = lax.while_loop(lambda state: (state[0] < 16) & (state[1] > SETTLED), again, (0, gap))
    settled = gap <= SETTLED

    @pl.when(settled)
    def _():
        out_ref[...] = out_ref[...] * scale_row

    @pl.when(jnp.logical_not(settled))
    def _():
        eliminate(block, out_ref, work_ref)


def bounds_of(count):
    return (0, -(-4 * count // 9), -(-7 * count // 9), count)


def tiles_of(low, high):
    return [(i, k) for k in range(high) for i in range(max(k, low), high)]


def gram_kernel(layout, bounds, parts, spot_ref, *refs):
    piece_refs, gram_refs = refs[: len(layout)], refs[len(layout) : len(layout) + len(bounds) - 1]
    mine_ref, sketch_ref, high_ref, low_ref, own_high_ref, own_low_ref, sems = refs[len(layout) + len(bounds) - 1 :]
    spot = spot_ref[0]
    sets, size, width = sketch_ref.shape
    step, part, rows = size // parts, TILE // parts, width // parts
    copies = []
    for n, (s, d, offset) in enumerate(layout):
        at = pl.multiple_of((spot ^ d) * step + offset, 8)
        target = sketch_ref.at[s, pl.ds(at, piece_refs[n].shape[0]), :]
        copies.append(pltpu.make_async_copy(piece_refs[n], target, sems.at[n]))
    for copy in copies:
        copy.start()
    for copy in copies:
        copy.wait()
    for s in range(sets):
        for i in range(bounds[-1]):
            here = slice(i * TILE, (i + 1) * TILE)
            values = sketch_ref[s, here, :]
            high_ref[s, here, :], low_ref[s, here, :] = halves(values)
            mine = values[:, :rows]
            for other in range(1, parts):
                mine = jnp.where(spot == other, values[:, other * rows : (other + 1) * rows], mine)
            mine_ref[s * rows : (s + 1) * rows, here] = mine.T
        for i in range(bounds[-1]):
            at = pl.multiple_of(i * TILE + spot * part, 16)
            own_high_ref[s, i * part : (i + 1) * part, :] = high_ref[s, pl.ds(at, part), :]
            own_low_ref[s, i * part : (i + 1) * part, :] = low_ref[s, pl.ds(at, part), :]
    for gram_ref, low, high in zip(gram_refs, bounds, bounds[1:]):
        done = 0
        for k in range(high):
            here, own = slice(k * TILE, (k + 1) * TILE), slice(max(k, low) * part, high * part)
            products = [
                dot3((own_high_ref[s, own, :], own_low_ref[s, own, :]), (high_ref[s, here, :], low_ref[s, here, :]), NT)
                for s in range(sets)
            ]
            gram_ref[done : done + own.stop - own.start, :] = sum(products)
            done += own.stop - own.start
        if done < gram_ref.shape[0]:
            gram_ref[done:, :] = jnp.zeros((gram_ref.shape[0] - done, TILE), F32)


def gram_shares(spot, sets, parts):
    layout = [(s, d, offset) for s, pieces in enumerate(sets) for d, offset, _ in pieces]
    arrays = [array for pieces in sets for _, _, array in pieces]
    width, rows = arrays[0].shape
    size = parts * width
    count, part = size // TILE, TILE // parts
    bounds = bounds_of(count)
    shapes = []
    for low, high in zip(bounds, bounds[1:]):
        tiles = len(tiles_of(low, high))
        shapes.append(jax.ShapeDtypeStruct(((tiles + tiles % 2) * part, TILE), F32))
    shapes.append(jax.ShapeDtypeStruct((len(sets) * rows // parts, size), F32))
    return pl.pallas_call(
        functools.partial(gram_kernel, layout, bounds, parts),
        out_shape=shapes,
        in_specs=[SMEM] + [ANY] * len(arrays),
        out_specs=[VMEM] * len(shapes),
        scratch_shapes=[
            pltpu.VMEM((len(sets), size, rows), F32),
            pltpu.VMEM((len(sets), size, rows), BF16),
            pltpu.VMEM((len(sets), size, rows), BF16),
            pltpu.VMEM((len(sets), count * part, rows), BF16),
            pltpu.VMEM((len(sets), count * part, rows), BF16),
            pltpu.SemaphoreType.DMA((len(arrays),)),
        ],
        compiler_params=pltpu.CompilerParams(vmem_limit_bytes=60 << 20),
        cost_estimate=pl.CostEstimate(
            flops=3 * size * size * rows // parts, bytes_accessed=8 * size * rows, transcendentals=0
        ),
    )(spot, *arrays)


def basis_kernel(scale, layout, cuts, parts, spot_ref, *refs):
    refs = list(refs)
    take = lambda n: [refs.pop(0) for _ in range(n)]
    share_refs = take(len(layout))
    (sketch_ref,) = take(1)
    past = [take(6) for _ in cuts[:-2]]
    basis_ref, short_ref, rest_ref, high_ref, low_ref, inv_high_ref, inv_low_ref = take(7)
    gram_ref, inverse_ref, work_ref, sems = refs
    first, last = cuts[-2:]
    part, half = TILE // parts, gram_ref.shape[2]
    spot, core = spot_ref[0], spot_ref[1]
    copies = []
    for n, (e, d, offset) in enumerate(layout):
        target = gram_ref.at[core ^ e, spot ^ d, pl.ds(offset, share_refs[n].shape[0]), :]
        copies.append(pltpu.make_async_copy(share_refs[n], target, sems.at[n]))
    for copy in copies:
        copy.start()
    for copy in copies:
        copy.wait()
    index = {tile: n * part for n, tile in enumerate(tiles_of(first, last))}

    def gram_rows(low, high, k):
        blocks = []
        for i in range(low, high):
            owner, at = divmod(index[i, k], half)
            blocks += [gram_ref[owner, sub, at : at + part, :] for sub in range(parts)]
        return scale * jnp.concatenate(blocks, axis=0)

    def rows_of(low, high, width):
        here = slice((low - first) * TILE, (high - first) * TILE)
        return high_ref[here, : width * TILE], low_ref[here, : width * TILE]

    def store_rows(low, high, k, values):
        here, cols = slice((low - first) * TILE, (high - first) * TILE), slice(k * TILE, (k + 1) * TILE)
        high_ref[here, cols], low_ref[here, cols] = halves(values)

    for (top, bottom), (_, _, past_high, past_low, past_inv_high, past_inv_low) in zip(zip(cuts, cuts[1:]), past):
        for k in range(top, bottom):
            here = slice((k - top) * TILE, (k - top + 1) * TILE)
            values = gram_rows(first, last, k)
            if k:
                factor = past_high[here, : k * TILE], past_low[here, : k * TILE]
                values = values - dot3(rows_of(first, last, k), factor, NT)
            own = past_inv_high[here, :], past_inv_low[here, :]
            store_rows(first, last, k, dot3(halves(values), own, NT))

    for k in range(first, last):
        here = slice((k - first) * TILE, (k - first + 1) * TILE)
        factor = rows_of(k, k + 1, k)

        def left_over(low, high):
            values = gram_rows(low, high, k)
            return values - dot3(rows_of(low, high, k), factor, NT) if k else values

        inverse_factor(left_over(k, k + 1), inverse_ref, work_ref)
        inv_high_ref[here, :], inv_low_ref[here, :] = halves(inverse_ref[...])
        own = inv_high_ref[here, :], inv_low_ref[here, :]
        if k + 1 < last:
            store_rows(k + 1, last, k, dot3(halves(left_over(k + 1, last)), own, NT))
        values = sketch_ref[:, here]
        for (top, bottom), (past_short, past_rest, *_) in zip(zip(cuts, cuts[1:]), past):
            cols = slice(top * TILE, bottom * TILE)
            values = values - dot3(
                (past_short[...], past_rest[...]), (factor[0][:, cols], factor[1][:, cols]), NT
            )
        if k > first:
            cols = slice(first * TILE, k * TILE)
            done = slice(0, (k - first) * TILE)
            values = values - dot3(
                (short_ref[:, done], rest_ref[:, done]), (factor[0][:, cols], factor[1][:, cols]), NT
            )
        solved = dot3(halves(values), own, NT)
        basis_ref[:, here] = solved
        short_ref[:, here], rest_ref[:, here] = halves(solved)


def basis_part(spots, shares, sketch, past, cuts, parts, scale):
    first, last = cuts[-2:]
    rows, width = sketch.shape
    layout = [(e, d, offset) for e, d, offset, _ in shares]
    arrays = [array for _, _, _, array in shares]
    half = (len(tiles_of(first, last)) + 1) // 2 * (TILE // parts)
    flat = [array for arrays_of_part in past for array in arrays_of_part]
    shape = jax.ShapeDtypeStruct
    size = last * TILE
    basis, *kept = pl.pallas_call(
        functools.partial(basis_kernel, scale, layout, cuts, parts),
        out_shape=[shape((rows, width), F32)]
        + [shape((rows, width), BF16)] * 2
        + [shape((width, size), BF16)] * 2
        + [shape((width, TILE), BF16)] * 2,
        in_specs=[SMEM] + [ANY] * len(arrays) + [VMEM] * (1 + len(flat)),
        out_specs=[VMEM] * 7,
        scratch_shapes=[
            pltpu.VMEM((2, parts, half, TILE), F32),
            pltpu.VMEM((TILE, TILE), F32),
            pltpu.VMEM((TILE, TILE), F32),
            pltpu.SemaphoreType.DMA((len(arrays),)),
        ],
        compiler_params=pltpu.CompilerParams(vmem_limit_bytes=60 << 20),
        cost_estimate=pl.CostEstimate(
            flops=128 * size * size * width, bytes_accessed=4 * size * width, transcendentals=0
        ),
    )(spots, *arrays, sketch, *flat)
    return basis, kept


def swapped(x, axis, distance):
    return lax.ppermute(x, axis, [(i, i ^ distance) for i in range(lax.axis_size(axis))])


def together(*arrays):
    return lax.optimization_barrier(arrays)


def row_pieces(x, direct=False):
    size = lax.axis_size("row")
    if size != 4 or direct:
        return [(0, 0, x)] + [(d, 0, swapped(x, "row", d)) for d in range(1, size)]
    half = x.shape[0] // 2
    first, second = x[:half], x[half:]
    first_one, second_two, first_two, second_one = together(
        swapped(first, "row", 1), swapped(second, "row", 2), swapped(first, "row", 2), swapped(second, "row", 1)
    )
    first_three, second_three = swapped(first_one, "row", 2), swapped(second_two, "row", 1)
    return [
        (0, 0, x),
        (1, 0, first_one),
        (1, half, second_one),
        (2, 0, first_two),
        (2, half, second_two),
        (3, 0, first_three),
        (3, half, second_three),
    ]


def in_row_order(pieces, place):
    step, cols = pieces[0][2].shape
    size = lax.axis_size("row")
    whole = jnp.zeros((step * size, cols), pieces[0][2].dtype)
    for d in range(size):
        block = jnp.concatenate([piece for e, _, piece in pieces if e == d], axis=0)
        whole = lax.dynamic_update_slice_in_dim(whole, block, (place ^ d) * step, 0)
    return whole


def gathered_chips(x):
    spread = jnp.broadcast_to(x[None], (lax.axis_size("chip"),) + x.shape)
    return lax.all_to_all(spread, "chip", 0, 0).reshape(-1, x.shape[1])


def on_device(left_site, right_site, gate, omega):
    parts, chips = lax.axis_size("row"), lax.axis_size("chip")
    total_rows = left_site.shape[0] * parts
    place, chip, core = lax.axis_index("row"), lax.axis_index("chip"), lax.axis_index("core")
    spots = jnp.stack([place, core, chip]).astype(jnp.int32)
    left_sets = left_site.reshape(chips * lax.axis_size("core"), 2, -1, left_site.shape[1])
    right_cols = in_row_order(row_pieces(right_site), place)

    thetas, sets = [], []
    for s in range(2):
        left = left_sets[:, s].reshape(-1, left_site.shape[1])
        pieces = [left] + [swapped(left, "chip", d) for d in range(1, chips)]
        thetas.append(pieces)
    for s in range(2):
        pieces = thetas[s] + [swapped(x, "core", 1) for x in thetas[s]]
        theta = theta_of(gate, spots, pieces, right_cols)
        if s == 0:
            theta, *thetas[1] = together(theta, *thetas[1])
        thetas[s] = theta.reshape(left_sets.shape[0], -1, theta.shape[1])
        theta_set = in_row_order(row_pieces(lax.all_to_all(theta, COL, 0, 1, tiled=True)), place)
        sets.append(row_pieces(dot(omega, theta_set, (((0,), (1,)), ((), ())))))
    theta = jnp.stack(thetas, axis=1).reshape(-1, right_cols.shape[1])
    cols_here = theta.shape[1]
    *gram, sketch = gram_shares(spots, sets, parts)
    bounds = bounds_of(sketch.shape[1] // TILE)

    halved = []
    for share in gram:
        half = share.shape[0] // 2
        kept = lax.dynamic_slice_in_dim(share, core * half, half, 0)
        given = lax.dynamic_slice_in_dim(share, (1 - core) * half, half, 0)
        halved.append((kept + swapped(given, "core", 1)).reshape(chips, half // chips, TILE))
    lengths = [x.shape[1] for x in halved]
    summed = jnp.sum(lax.all_to_all(jnp.concatenate(halved, axis=1), "chip", 0, 0), axis=0)
    gathered = []
    for n, length in enumerate(lengths):
        share = summed[sum(lengths[:n]) : sum(lengths[: n + 1])]
        gathered.append(gathered_chips(share))

    past, basis, rows, mine = [], [], [], []
    for n in range(len(gathered)):
        mine.append(row_pieces(gathered[n], direct=True))
        if n:
            arrays = together(past[-1][0], *[x for _, _, x in mine[n]])
            past[-1][0] = arrays[0]
            mine[n] = [(d, at, x) for (d, at, _), x in zip(mine[n], arrays[1:])]
        shares = [(0, d, at, x) for d, at, x in mine[n]]
        shares += [(1, d, at, swapped(x, "core", 1)) for d, at, x in mine[n]]
        cuts = bounds[: n + 2]
        columns = sketch[:, cuts[-2] * TILE : cuts[-1] * TILE]
        if n == 0:
            columns, gathered[1] = together(columns, gathered[1])
        if n > 1:
            columns, rows[n - 2] = together(columns, rows[n - 2])
        done, kept = basis_part(spots, shares, columns, past, cuts, parts, 1.0 / total_rows)
        past.append(kept)
        basis.append(done)
        short = kept[0]
        if n:
            short, rows[n - 1] = together(short, rows[n - 1])
        rows.append(lax.all_gather(short, COL, axis=0, tiled=True))

    folded = [dot(part, theta, TN).astype(BF16) for part in rows]
    folded = jnp.concatenate(folded, axis=0).reshape(parts, -1, cols_here)
    sums = lax.all_to_all(folded, "row", 0, 0)
    projected = jnp.sum(sums.astype(F32), axis=0) / math.sqrt(total_rows)
    return (jnp.concatenate(basis, axis=1), projected)


COL = ("chip", "core")


def solution(mesh):
    row, col = mesh.devices.shape
    split = Mesh(mesh.devices.reshape(row, col // 2, 2), ("row",) + COL)
    in_specs = (P("row", COL), P("row", COL), P(), P(None, "row"))
    out_specs = (P(("row",) + COL, None), P("row", COL))
    return jax.shard_map(
        on_device, mesh=split, in_specs=in_specs, out_specs=out_specs, check_vma=False
    )
```

time: 675 us -> 454 us (0.67)
  waiting for transfers between devices: 502 us -> 155 us
  starting transfers between devices: 0.24 us -> 91.1 us
  Pallas kernels: 82.5 us -> 104 us
  matrix products: 26.5 us -> 9.58 us
  local copies, waits for them, and re-layouts: 5.71 us -> 22.3 us
  other arithmetic: 3.19 us -> 13.5 us
  blocking collectives: 32 us -> 38.9 us
    psum x1 -> x0, waiting for transfers between devices: 235 us -> none  [on_device(): gram_columns = lax.psum(gram_columns_of(sketch), ('row', 'col'))]
    all_gather x4 -> x3, waiting for transfers between devices: 166 us -> 17.7 us  [on_device(): rows.append(lax.all_gather(short, COL, axis=0, tiled=True))]
    reduce_scatter x1 -> x0, waiting for transfers between devices: 99.6 us -> none  [on_device(): lax.psum_scatter(dot(theta, omega_rows), 'col', scatter_dimension=0, tile...]
    ppermute x0 -> x68, waiting for transfers between devices: none -> 85.9 us  [swapped(): lax.ppermute(x, axis, [(i, i ^ distance) for i in range(lax.axis_size(axi...]
    ppermute x0 -> x68, starting transfers between devices: none -> 64.8 us  [swapped(): lax.ppermute(x, axis, [(i, i ^ distance) for i in range(lax.axis_size(axi...]
    all_to_all x0 -> x6, waiting for transfers between devices: none -> 51.1 us  [the longest x1 27.2 us: on_device(): sums = lax.all_to_all(folded, 'row', 0, 0)]
    all_to_all x0 -> x6, starting transfers between devices: none -> 25.9 us  [the longest x3 12.3 us: gathered_chips(): return lax.all_to_all(spread, 'chip', 0, 0).reshape(-1, x.shape[1])]
    pallas_call x2 -> x6, Pallas kernels: 82.5 us -> 104 us  [the longest x3 84.6 us: basis_part(): pl.pallas_call(functools.partial(basis_kernel, scale, layout, cuts, parts...]
  transfers between devices with their start and end apart: 6 -> 77, of which waited for: 6 -> 32; matrix products, arithmetic and copies ran while one was open for 0% -> 6% of each run, Pallas kernels for 1% -> 21%
where the time goes in v3:
time: 454 us; the launch traced here: 449 us
  waiting for transfers between devices  155 us (34%)
  Pallas kernels  104 us (23%)
  starting transfers between devices  91.1 us (20%)
  blocking collectives  38.9 us (9%)
  local copies, waits for them, and re-layouts  22.3 us (5%)
  between operations  14.8 us (3%)
  other arithmetic  13.5 us (3%)
  matrix products  9.58 us (2%)
    ppermute x68, waiting for transfers between devices, swapped(): lax.ppermute(x, axis, [(i, i ^ distance) for i in range(lax.axis_size(axi...  85.9 us
    pallas_call x3, Pallas kernels, basis_part(): pl.pallas_call(functools.partial(basis_kernel, scale, layout, cuts, parts...  84.6 us
    ppermute x68, starting transfers between devices, swapped(): lax.ppermute(x, axis, [(i, i ^ distance) for i in range(lax.axis_size(axi...  64.8 us
    all_to_all x1, blocking collectives, on_device(): lax.all_to_all(jnp.concatenate(halved, axis=1), 'chip', 0, 0)  38.9 us
    all_to_all x1, waiting for transfers between devices, on_device(): sums = lax.all_to_all(folded, 'row', 0, 0)  27.2 us
    all_gather x3, waiting for transfers between devices, on_device(): rows.append(lax.all_gather(short, COL, axis=0, tiled=True))  17.7 us
    all_to_all x2, waiting for transfers between devices, on_device(): lax.all_to_all(theta, COL, 0, 1, tiled=True)  14.2 us
    all_to_all x3, starting transfers between devices, gathered_chips(): return lax.all_to_all(spread, 'chip', 0, 0).reshape(-1, x.shape[1])  12.3 us
  transfers between devices with their start and end apart: 77, of which 32 were waited for; matrix products, arithmetic and copies ran while one was open for 6% of the time, Pallas kernels for 21%

profile of v3, /device:TPU:0, one launch (start us, length us, event | category | flops | bytes accessed | tf_op | source)
XLA Modules:
  0.0 448.6 jit_solution(118584021934882850)
XLA Ops:
  8.2 3.0 collective-permute-start.10
  14.4 2.1 collective-permute-start
  16.5 1.9 collective-permute-done.10
  18.4 3.2 collective-permute-start.1
  21.5 1.7 collective-permute-done.7
  23.3 3.9 collective-permute-start.2
  27.1 1.6 collective-permute-start.11
  30.2 9.0 %collective-permute-done.1.refs_2_ = bf16[512,256]{1,0:T(8,128)(2,1)S(1)} collective-permute-done((bf16[512,256]{1,0:T(8,128)(2,1)S(1)}, bf16[512,256]{1,0:T(8,128)(2,1)S(1)}, u32[]{:S(2)}, u32[]{:S(2)}) %collective-permute-start.1) | collective-permute-done | bytes 262176 | tf_op jit(solution)/shard_map/ppermute | solution.py:350
  40.4 3.2 collective-permute-start.13
  43.6 1.9 collective-permute-start.14
  50.7 4.4 shard_map.59
  55.1 9.9 %collective-permute-done.14.refs_2_ = bf16[512,256]{1,0:T(8,128)(2,1)S(1)} collective-permute-done((bf16[512,256]{1,0:T(8,128)(2,1)S(1)}, bf16[512,256]{1,0:T(8,128)(2,1)S(1)}, u32[]{:S(2)}, u32[]{:S(2)}) %collective-permute-start.14) | collective-permute-done | bytes 262176 | tf_op jit(solution)/shard_map/ppermute | solution.py:350
  66.4 6.1 %all-to-all-start = ((bf16[8,64,512]{2,1,0:T(8,128)(2,1)}), bf16[8,64,512]{2,1,0:T(8,128)(2,1)}, u32[]{:S(2)}, u32[]{:S(2)}) async-start(bf16[8,64,512]{2,1,0:T(8,128)(2,1)} %bitcast.6), calls=%async_computation | async-start | bytes 1048576 | tf_op jit(solution)/shard_map/all_to_all | solution.py:412
  78.3 3.9 shard_map.60
  82.2 5.7 %all-to-all-done = bf16[8,64,512]{2,1,0:T(8,128)(2,1)} async-done(((bf16[8,64,512]{2,1,0:T(8,128)(2,1)}), bf16[8,64,512]{2,1,0:T(8,128)(2,1)}, u32[]{:S(2)}, u32[]{:S(2)}) %all-to-all-start) | async-done | bytes 524320 | tf_op jit(solution)/shard_map/all_to_all | solution.py:412
  87.9 3.8 all-to-all-start.1
  98.4 8.6 %all-to-all-done.1 = bf16[8,64,512]{2,1,0:T(8,128)(2,1)S(1)} async-done(((bf16[8,64,512]{2,1,0:T(8,128)(2,1)}), bf16[8,64,512]{2,1,0:T(8,128)(2,1)S(1)}, u32[]{:S(2)}, u32[]{:S(2)}) %all-to-all-start.1) | async-done | bytes 524320 | tf_op jit(solution)/shard_map/all_to_all | solution.py:412
  115.2 12.4 %collective-permute-done.20 = bf16[32,4096]{1,0:T(8,128)(2,1)S(1)} collective-permute-done((bf16[32,4096]{1,0:T(8,128)(2,1)S(1)}, bf16[32,4096]{1,0:T(8,128)(2,1)S(1)}, u32[]{:S(2)}, u32[]{:S(2)}) %collective-permute-start.20) | collective-permute-done | bytes 262176 | tf_op jit(solution)/shard_map/ppermute | solution.py:350
  128.1 3.9 convolution_bitcast_fusion.1.refs_0_
  137.9 11.3 %collective-permute-done.36 = bf16[32,4096]{1,0:T(8,128)(2,1)S(1)} collective-permute-done((bf16[32,4096]{1,0:T(8,128)(2,1)S(1)}, bf16[32,4096]{1,0:T(8,128)(2,1)S(1)}, u32[]{:S(2)}, u32[]{:S(2)}) %collective-permute-start.36) | collective-permute-done | bytes 262176 | tf_op jit(solution)/shard_map/ppermute | solution.py:350
  157.1 1.7 collective-permute-done.25.refs_2_
  158.8 1.9 collective-permute-start.26
  160.7 4.4 collective-permute-done.38.refs_8_
  165.7 3.5 collective-permute-done.39.refs_11_
  169.2 2.3 collective-permute-done.41.refs_9_
  174.9 3.4 collective-permute-done.42.refs_12_
  179.9 10.8 %shard_map.61 = (f32[640,256]{1,0:T(8,128)}, f32[1152,256]{1,0:T(8,128)}, f32[1152,256]{1,0:T(8,128)}, f32[128,2304]{1,0:T(8,128)}) custom-call(s32[3]{0:T(128)} %copy-done.7, f32[576,256]{1,0:T(8,128)} %copy-done.8, f32[288,256]{1,0:T(8,128)} %copy-done.19, f32[288,256]{1,0:T(8,128)} %copy-done.22, f32[288,256]{1,0:T(8,128)} %copy-done.20, ...), custom_call_target="tpu_custom_call" | custom-call | flops 1019215872 | bytes 4718592 | tf_op jit(solution)/shard_map/pallas_call | solution.py:222
  190.7 2.1 constant_dynamic-slice_fusion.1
  192.8 1.7 constant_dynamic-slice_fusion.2
  199.5 38.9 %all_to_all.63 = f32[4,368,256]{2,1,0:T(8,128)S(1)} all-to-all(f32[4,368,256]{2,1,0:T(8,128)S(1)} %pad_maximum_fusion.1), channel_id=1, replica_groups=mesh['row'=4,'chip'=4,'core'=2] {'chip'}, dimensions={0} | all-to-all | bytes 3014656 | tf_op jit(solution)/shard_map/all_to_all | solution.py:426
  239.2 3.5 all-to-all-start.3
  242.7 9.7 %all-to-all-done.3 = f32[4,80,256]{2,1,0:T(8,128)S(1)} async-done(((f32[4,80,256]{2,1,0:T(8,128)}), f32[4,80,256]{2,1,0:T(8,128)S(1)}, u32[]{:S(2)}, u32[]{:S(2)}) %all-to-all-start.3) | async-done | bytes 327712 | tf_op jit(solution)/shard_map/all_to_all | solution.py:390
  253.3 4.0 all-to-all-start.4
  258.1 2.8 collective-permute-start.49
  260.9 7.2 %collective-permute-done.47.refs_1_ = f32[320,256]{1,0:T(8,128)S(1)} collective-permute-done((f32[320,256]{1,0:T(8,128)S(1)}, f32[320,256]{1,0:T(8,128)S(1)}, u32[]{:S(2)}, u32[]{:S(2)}) %collective-permute-start.47) | collective-permute-done | bytes 327712 | tf_op jit(solution)/shard_map/ppermute | solution.py:350
  268.1 4.1 collective-permute-done.48.refs_2_
  274.5 4.8 %all-to-all-start.5 = ((f32[4,144,256]{2,1,0:T(8,128)}), f32[4,144,256]{2,1,0:T(8,128)}, u32[]{:S(2)}, u32[]{:S(2)}) async-start(f32[4,144,256]{2,1,0:T(8,128)} %broadcast_in_dim.11), calls=%async_computation.5 | async-start | bytes 1179648 | tf_op jit(solution)/shard_map/all_to_all | solution.py:390
  280.8 2.0 collective-permute-start.56
  282.8 21.1 %shard_map.62 = (f32[128,1024]{1,0:T(8,128)}, bf16[128,1024]{1,0:T(8,128)(2,1)}, bf16[128,1024]{1,0:T(8,128)(2,1)}, bf16[1024,1024]{1,0:T(8,128)(2,1)}, bf16[102...) custom-call(s32[3]{0:T(128)} %copy-done.7, f32[320,256]{1,0:T(8,128)} %bitcast.89, ...), custom_call_target="tpu_custom_call" | custom-call | flops 137438953472 | bytes 4194304 | tf_op jit(solution)/shard_map/pallas_call | solution.py:327
  304.0 4.1 collective-permute-done.55.refs_2_
  311.8 1.8 collective-permute-start.63
  313.6 30.2 %shard_map.63 = (f32[128,768]{1,0:T(8,128)}, bf16[128,768]{1,0:T(8,128)(2,1)}, bf16[128,768]{1,0:T(8,128)(2,1)}, bf16[768,1792]{1,0:T(8,128)(2,1)}, bf16[768,179...) custom-call(s32[3]{0:T(128)} %copy-done.7, f32[576,256]{1,0:T(8,128)} %bitcast.83, ...), custom_call_target="tpu_custom_call" | custom-call | flops 315680096256 | bytes 5505024 | tf_op jit(solution)/shard_map/pallas_call | solution.py:327
  345.0 1.7 slice.87.refs_8_
  349.5 33.2 %shard_map.64 = (f32[128,512]{1,0:T(8,128)}, bf16[128,512]{1,0:T(8,128)(2,1)}, bf16[128,512]{1,0:T(8,128)(2,1)}, bf16[512,2304]{1,0:T(8,128)(2,1)}, bf16[512,230...) custom-call(s32[3]{0:T(128)} %copy-done.7, f32[576,256]{1,0:T(8,128)} %bitcast.17.refs_0_, ...), custom_call_target="tpu_custom_call" | custom-call | flops 347892350976 | bytes 4718592 | tf_op jit(solution)/shard_map/pallas_call | solution.py:327
  387.1 17.7 %all-gather.8.cloned.1.call-done = bf16[1024,512]{1,0:T(8,128)(2,1)} async-done(((bf16[128,512]{1,0:T(8,128)(2,1)}), bf16[1024,512]{1,0:T(8,128)(2,1)}) %all-gather.8.cloned.1.call-update) | async-done | bytes 1048592 | tf_op jit(solution)/shard_map/all_gather | solution.py:453
  404.8 2.0 convolution_convert_fusion.2
  408.3 3.8 all-to-all-start.6
  413.2 27.2 %all-to-all-done.6 = bf16[4,576,512]{2,1,0:T(8,128)(2,1)S(1)} async-done(((bf16[4,576,512]{2,1,0:T(8,128)(2,1)}), bf16[4,576,512]{2,1,0:T(8,128)(2,1)S(1)}, u32[]{:S(2)}, u32[]{:S(2)}) %all-to-all-start.6) | async-done | bytes 2359328 | tf_op jit(solution)/shard_map/all_to_all | solution.py:457
  (263 shorter events, 81.0 us)
Async XLA Ops:
  11.2 15.9 %collective-permute-start.8 = (bf16[256,512]{1,0:T(8,128)(2,1)S(1)}, bf16[256,512]{1,0:T(8,128)(2,1)}, u32[]{:S(2)}, u32[]{:S(2)}) collective-permute-start(bf16[256,512]{1,0:T(8,128)(2,1)S(1)} %get-tuple-element.138), channel_id=1, source_target_pairs={{0,16},{8,24},{16,0},{24,8},{1,17},{9,25},{17,1},{25,9},{2,18},{10... | collective-permute-start | bytes 786440 | tf_op jit(solution)/shard_map/ppermute | solution.py:350
  13.3 13.8 %collective-permute-start.9 = (bf16[256,512]{1,0:T(8,128)(2,1)S(1)}, bf16[256,512]{1,0:T(8,128)(2,1)S(1)}, u32[]{:S(2)}, u32[]{:S(2)}) collective-permute-start(bf16[256,512]{1,0:T(8,128)(2,1)S(1)} %get-tuple-element.139), channel_id=1, source_target_pairs={{0,16},{8,24},{16,0},{24,8},{1,17},{9,25},{17,1},{25,9},{2,18},{10... | collective-permute-start | bytes 786440 | tf_op jit(solution)/shard_map/ppermute | solution.py:350
  14.4 14.3 %collective-permute-start = (bf16[512,256]{1,0:T(8,128)(2,1)S(1)}, bf16[512,256]{1,0:T(8,128)(2,1)S(1)}, u32[]{:S(2)}, u32[]{:S(2)}) collective-permute-start(bf16[512,256]{1,0:T(8,128)(2,1)S(1)} %bitcast.63), channel_id=1, source_target_pairs={{0,2},{2,0},{4,6},{6,4},{1,3},{3,1},{5,7},{7,5},{8,10},{10,8},{12,... | collective-permute-start | bytes 786440 | tf_op jit(solution)/shard_map/ppermute | solution.py:350
  18.4 20.9 %collective-permute-start.1 = (bf16[512,256]{1,0:T(8,128)(2,1)S(1)}, bf16[512,256]{1,0:T(8,128)(2,1)S(1)}, u32[]{:S(2)}, u32[]{:S(2)}) collective-permute-start(bf16[512,256]{1,0:T(8,128)(2,1)S(1)} %bitcast.64), channel_id=1, source_target_pairs={{0,4},{2,6},{4,0},{6,2},{1,5},{3,7},{5,1},{7,3},{8,12},{10,14},{12... | collective-permute-start | bytes 786440 | tf_op jit(solution)/shard_map/ppermute | solution.py:350
  23.3 17.1 %collective-permute-start.2 = (bf16[512,256]{1,0:T(8,128)(2,1)S(1)}, bf16[512,256]{1,0:T(8,128)(2,1)S(1)}, u32[]{:S(2)}, u32[]{:S(2)}) collective-permute-start(bf16[512,256]{1,0:T(8,128)(2,1)S(1)} %bitcast.65), channel_id=1, source_target_pairs={{0,6},{2,4},{4,2},{6,0},{1,7},{3,5},{5,3},{7,1},{8,14},{10,12},{12... | collective-permute-start | bytes 786440 | tf_op jit(solution)/shard_map/ppermute | solution.py:350
  27.1 16.5 %collective-permute-start.3 = (bf16[512,256]{1,0:T(8,128)(2,1)S(1)}, bf16[512,256]{1,0:T(8,128)(2,1)}, u32[]{:S(2)}, u32[]{:S(2)}) collective-permute-start(bf16[512,256]{1,0:T(8,128)(2,1)S(1)} %bitcast.66), channel_id=1, source_target_pairs={{0,1},{1,0},{2,3},{3,2},{4,5},{5,4},{6,7},{7,6},{8,9},{9,8},{10,11... | collective-permute-start | bytes 786440 | tf_op jit(solution)/shard_map/ppermute | solution.py:350
  27.1 18.4 %collective-permute-start.11 = (bf16[256,512]{1,0:T(8,128)(2,1)}, bf16[256,512]{1,0:T(8,128)(2,1)}, u32[]{:S(2)}, u32[]{:S(2)}) collective-permute-start(bf16[256,512]{1,0:T(8,128)(2,1)} %collective-permute-done.7), channel_id=1, source_target_pairs={{0,16},{8,24},{16,0},{24,8},{1,17},{9,25},{17,1},{25,9},{2,18},{10... | collective-permute-start | bytes 786440 | tf_op jit(solution)/shard_map/ppermute | solution.py:350
  28.7 18.3 %collective-permute-start.12 = (bf16[256,512]{1,0:T(8,128)(2,1)}, bf16[256,512]{1,0:T(8,128)(2,1)}, u32[]{:S(2)}, u32[]{:S(2)}) collective-permute-start(bf16[256,512]{1,0:T(8,128)(2,1)} %collective-permute-done.8), channel_id=1, source_target_pairs={{0,8},{8,0},{16,24},{24,16},{1,9},{9,1},{17,25},{25,17},{2,10},{10... | collective-permute-start | bytes 786440 | tf_op jit(solution)/shard_map/ppermute | solution.py:350
  40.4 14.7 %collective-permute-start.13 = (bf16[512,256]{1,0:T(8,128)(2,1)S(1)}, bf16[512,256]{1,0:T(8,128)(2,1)S(1)}, u32[]{:S(2)}, u32[]{:S(2)}) collective-permute-start(bf16[512,256]{1,0:T(8,128)(2,1)S(1)} %bitcast.58), channel_id=1, source_target_pairs={{0,2},{2,0},{4,6},{6,4},{1,3},{3,1},{5,7},{7,5},{8,10},{10,8},{12,... | collective-permute-start | bytes 786440 | tf_op jit(solution)/shard_map/ppermute | solution.py:350
  43.6 21.4 %collective-permute-start.14 = (bf16[512,256]{1,0:T(8,128)(2,1)S(1)}, bf16[512,256]{1,0:T(8,128)(2,1)S(1)}, u32[]{:S(2)}, u32[]{:S(2)}) collective-permute-start(bf16[512,256]{1,0:T(8,128)(2,1)S(1)} %bitcast.59), channel_id=1, source_target_pairs={{0,4},{2,6},{4,0},{6,2},{1,5},{3,7},{5,1},{7,3},{8,12},{10,14},{12... | collective-permute-start | bytes 786440 | tf_op jit(solution)/shard_map/ppermute | solution.py:350
  45.5 19.5 %collective-permute-start.15 = (bf16[512,256]{1,0:T(8,128)(2,1)S(1)}, bf16[512,256]{1,0:T(8,128)(2,1)S(1)}, u32[]{:S(2)}, u32[]{:S(2)}) collective-permute-start(bf16[512,256]{1,0:T(8,128)(2,1)S(1)} %bitcast.60), channel_id=1, source_target_pairs={{0,6},{2,4},{4,2},{6,0},{1,7},{3,5},{5,3},{7,1},{8,14},{10,12},{12... | collective-permute-start | bytes 786440 | tf_op jit(solution)/shard_map/ppermute | solution.py:350
  66.4 21.5 %all-to-all-start = ((bf16[8,64,512]{2,1,0:T(8,128)(2,1)}), bf16[8,64,512]{2,1,0:T(8,128)(2,1)}, u32[]{:S(2)}, u32[]{:S(2)}) async-start(bf16[8,64,512]{2,1,0:T(8,128)(2,1)} %bitcast.6), calls=%async_computation | async-start | bytes 1048576 | tf_op jit(solution)/shard_map/all_to_all | solution.py:412
  87.9 19.1 %all-to-all-start.1 = ((bf16[8,64,512]{2,1,0:T(8,128)(2,1)}), bf16[8,64,512]{2,1,0:T(8,128)(2,1)S(1)}, u32[]{:S(2)}, u32[]{:S(2)}) async-start(bf16[8,64,512]{2,1,0:T(8,128)(2,1)} %bitcast.9), calls=%async_computation.1 | async-start | bytes 1048576 | tf_op jit(solution)/shard_map/all_to_all | solution.py:412
  92.8 15.8 %collective-permute-start.16 = (bf16[32,4096]{1,0:T(8,128)(2,1)S(1)}, bf16[32,4096]{1,0:T(8,128)(2,1)S(1)}, u32[]{:S(2)}, u32[]{:S(2)}) collective-permute-start(bf16[32,4096]{1,0:T(8,128)(2,1)S(1)} %bitcast.94), channel_id=1, source_target_pairs={{0,8},{8,0},{16,24},{24,16},{1,9},{9,1},{17,25},{25,17},{2,10},{10... | collective-permute-start | bytes 786440 | tf_op jit(solution)/shard_map/ppermute | solution.py:350
  94.4 16.4 %collective-permute-start.18 = (bf16[32,4096]{1,0:T(8,128)(2,1)S(1)}, bf16[32,4096]{1,0:T(8,128)(2,1)}, u32[]{:S(2)}, u32[]{:S(2)}) collective-permute-start(bf16[32,4096]{1,0:T(8,128)(2,1)S(1)} %bitcast.95), channel_id=1, source_target_pairs={{0,16},{8,24},{16,0},{24,8},{1,17},{9,25},{17,1},{25,9},{2,18},{10... | collective-permute-start | bytes 786440 | tf_op jit(solution)/shard_map/ppermute | solution.py:350
  95.9 14.3 %collective-permute-start.17 = (bf16[32,4096]{1,0:T(8,128)(2,1)S(1)}, bf16[32,4096]{1,0:T(8,128)(2,1)}, u32[]{:S(2)}, u32[]{:S(2)}) collective-permute-start(bf16[32,4096]{1,0:T(8,128)(2,1)S(1)} %bitcast.96), channel_id=1, source_target_pairs={{0,16},{8,24},{16,0},{24,8},{1,17},{9,25},{17,1},{25,9},{2,18},{10... | collective-permute-start | bytes 786440 | tf_op jit(solution)/shard_map/ppermute | solution.py:350
  96.5 14.3 %collective-permute-start.19 = (bf16[32,4096]{1,0:T(8,128)(2,1)S(1)}, bf16[32,4096]{1,0:T(8,128)(2,1)}, u32[]{:S(2)}, u32[]{:S(2)}) collective-permute-start(bf16[32,4096]{1,0:T(8,128)(2,1)S(1)} %bitcast.97), channel_id=1, source_target_pairs={{0,8},{8,0},{16,24},{24,16},{1,9},{9,1},{17,25},{25,17},{2,10},{10... | collective-permute-start | bytes 786440 | tf_op jit(solution)/shard_map/ppermute | solution.py:350
  107.0 26.6 %collective-permute-start.32 = (bf16[32,4096]{1,0:T(8,128)(2,1)S(1)}, bf16[32,4096]{1,0:T(8,128)(2,1)S(1)}, u32[]{:S(2)}, u32[]{:S(2)}) collective-permute-start(bf16[32,4096]{1,0:T(8,128)(2,1)S(1)} %bitcast.90), channel_id=1, source_target_pairs={{0,8},{8,0},{16,24},{24,16},{1,9},{9,1},{17,25},{25,17},{2,10},{10... | collective-permute-start | bytes 786440 | tf_op jit(solution)/shard_map/ppermute | solution.py:350
  108.7 26.5 %collective-permute-start.34 = (bf16[32,4096]{1,0:T(8,128)(2,1)S(1)}, bf16[32,4096]{1,0:T(8,128)(2,1)S(1)}, u32[]{:S(2)}, u32[]{:S(2)}) collective-permute-start(bf16[32,4096]{1,0:T(8,128)(2,1)S(1)} %bitcast.91), channel_id=1, source_target_pairs={{0,16},{8,24},{16,0},{24,8},{1,17},{9,25},{17,1},{25,9},{2,18},{10... | collective-permute-start | bytes 786440 | tf_op jit(solution)/shard_map/ppermute | solution.py:350
  110.3 24.9 %collective-permute-start.33 = (bf16[32,4096]{1,0:T(8,128)(2,1)S(1)}, bf16[32,4096]{1,0:T(8,128)(2,1)S(1)}, u32[]{:S(2)}, u32[]{:S(2)}) collective-permute-start(bf16[32,4096]{1,0:T(8,128)(2,1)S(1)} %bitcast.92), channel_id=1, source_target_pairs={{0,16},{8,24},{16,0},{24,8},{1,17},{9,25},{17,1},{25,9},{2,18},{10... | collective-permute-start | bytes 786440 | tf_op jit(solution)/shard_map/ppermute | solution.py:350
  110.8 16.8 %collective-permute-start.20 = (bf16[32,4096]{1,0:T(8,128)(2,1)S(1)}, bf16[32,4096]{1,0:T(8,128)(2,1)S(1)}, u32[]{:S(2)}, u32[]{:S(2)}) collective-permute-start(bf16[32,4096]{1,0:T(8,128)(2,1)S(1)} %collective-permute-done.16), channel_id=1, source_target_pairs={{0,16},{8,24},{16,0},{24,8},{1,17},{9,25},{17,1},{25,9},{2,18},{10... | collective-permute-start | bytes 786440 | tf_op jit(solution)/shard_map/ppermute | solution.py:350
  112.3 15.8 %collective-permute-start.21 = (bf16[32,4096]{1,0:T(8,128)(2,1)}, bf16[32,4096]{1,0:T(8,128)(2,1)S(1)}, u32[]{:S(2)}, u32[]{:S(2)}) collective-permute-start(bf16[32,4096]{1,0:T(8,128)(2,1)} %collective-permute-done.17), channel_id=1, source_target_pairs={{0,8},{8,0},{16,24},{24,16},{1,9},{9,1},{17,25},{25,17},{2,10},{10... | collective-permute-start | bytes 786440 | tf_op jit(solution)/shard_map/ppermute | solution.py:350
  132.1 20.8 %collective-permute-start.22 = (f32[288,256]{1,0:T(8,128)S(1)}, f32[288,256]{1,0:T(8,128)S(1)}, u32[]{:S(2)}, u32[]{:S(2)}) collective-permute-start(f32[288,256]{1,0:T(8,128)S(1)} %get-tuple-element.131), channel_id=1, source_target_pairs={{0,8},{8,0},{16,24},{24,16},{1,9},{9,1},{17,25},{25,17},{2,10},{10... | collective-permute-start | bytes 884744 | tf_op jit(solution)/shard_map/ppermute | solution.py:350
  133.7 23.4 %collective-permute-start.24 = (f32[288,256]{1,0:T(8,128)S(1)}, f32[288,256]{1,0:T(8,128)S(1)}, u32[]{:S(2)}, u32[]{:S(2)}) collective-permute-start(f32[288,256]{1,0:T(8,128)S(1)} %get-tuple-element.131), channel_id=1, source_target_pairs={{0,16},{8,24},{16,0},{24,8},{1,17},{9,25},{17,1},{25,9},{2,18},{10... | collective-permute-start | bytes 884744 | tf_op jit(solution)/shard_map/ppermute | solution.py:350
  135.4 13.8 %collective-permute-start.36 = (bf16[32,4096]{1,0:T(8,128)(2,1)S(1)}, bf16[32,4096]{1,0:T(8,128)(2,1)S(1)}, u32[]{:S(2)}, u32[]{:S(2)}) collective-permute-start(bf16[32,4096]{1,0:T(8,128)(2,1)S(1)} %collective-permute-done.32), channel_id=1, source_target_pairs={{0,16},{8,24},{16,0},{24,8},{1,17},{9,25},{17,1},{25,9},{2,18},{10... | collective-permute-start | bytes 786440 | tf_op jit(solution)/shard_map/ppermute | solution.py:350
  136.9 12.8 %collective-permute-start.37 = (bf16[32,4096]{1,0:T(8,128)(2,1)S(1)}, bf16[32,4096]{1,0:T(8,128)(2,1)S(1)}, u32[]{:S(2)}, u32[]{:S(2)}) collective-permute-start(bf16[32,4096]{1,0:T(8,128)(2,1)S(1)} %collective-permute-done.33), channel_id=1, source_target_pairs={{0,8},{8,0},{16,24},{24,16},{1,9},{9,1},{17,25},{25,17},{2,10},{10... | collective-permute-start | bytes 786440 | tf_op jit(solution)/shard_map/ppermute | solution.py:350
  136.9 18.6 %collective-permute-start.23 = (f32[288,256]{1,0:T(8,128)S(1)}, f32[288,256]{1,0:T(8,128)S(1)}, u32[]{:S(2)}, u32[]{:S(2)}) collective-permute-start(f32[288,256]{1,0:T(8,128)S(1)} %get-tuple-element.130), channel_id=1, source_target_pairs={{0,16},{8,24},{16,0},{24,8},{1,17},{9,25},{17,1},{25,9},{2,18},{10... | collective-permute-start | bytes 884744 | tf_op jit(solution)/shard_map/ppermute | solution.py:350
  151.3 13.8 %collective-permute-start.38 = (f32[288,256]{1,0:T(8,128)S(1)}, f32[288,256]{1,0:T(8,128)S(1)}, u32[]{:S(2)}, u32[]{:S(2)}) collective-permute-start(f32[288,256]{1,0:T(8,128)S(1)} %get-tuple-element.129), channel_id=1, source_target_pairs={{0,8},{8,0},{16,24},{24,16},{1,9},{9,1},{17,25},{25,17},{2,10},{10... | collective-permute-start | bytes 884744 | tf_op jit(solution)/shard_map/ppermute | solution.py:350
  152.9 16.3 %collective-permute-start.40 = (f32[288,256]{1,0:T(8,128)S(1)}, f32[288,256]{1,0:T(8,128)S(1)}, u32[]{:S(2)}, u32[]{:S(2)}) collective-permute-start(f32[288,256]{1,0:T(8,128)S(1)} %get-tuple-element.129), channel_id=1, source_target_pairs={{0,16},{8,24},{16,0},{24,8},{1,17},{9,25},{17,1},{25,9},{2,18},{10... | collective-permute-start | bytes 884744 | tf_op jit(solution)/shard_map/ppermute | solution.py:350
  155.6 13.6 %collective-permute-start.39 = (f32[288,256]{1,0:T(8,128)S(1)}, f32[288,256]{1,0:T(8,128)S(1)}, u32[]{:S(2)}, u32[]{:S(2)}) collective-permute-start(f32[288,256]{1,0:T(8,128)S(1)} %get-tuple-element.128), channel_id=1, source_target_pairs={{0,16},{8,24},{16,0},{24,8},{1,17},{9,25},{17,1},{25,9},{2,18},{10... | collective-permute-start | bytes 884744 | tf_op jit(solution)/shard_map/ppermute | solution.py:350
  157.1 14.4 %collective-permute-start.41 = (f32[288,256]{1,0:T(8,128)S(1)}, f32[288,256]{1,0:T(8,128)S(1)}, u32[]{:S(2)}, u32[]{:S(2)}) collective-permute-start(f32[288,256]{1,0:T(8,128)S(1)} %get-tuple-element.128), channel_id=1, source_target_pairs={{0,8},{8,0},{16,24},{24,16},{1,9},{9,1},{17,25},{25,17},{2,10},{10... | collective-permute-start | bytes 884744 | tf_op jit(solution)/shard_map/ppermute | solution.py:350
  158.8 15.7 %collective-permute-start.26 = (f32[288,256]{1,0:T(8,128)S(1)}, f32[288,256]{1,0:T(8,128)S(1)}, u32[]{:S(2)}, u32[]{:S(2)}) collective-permute-start(f32[288,256]{1,0:T(8,128)S(1)} %collective-permute-done.22.refs_1_), channel_id=1, source_target_pairs={{0,16},{8,24},{16,0},{24,8},{1,17},{9,25},{17,1},{25,9},{2,18},{10... | collective-permute-start | bytes 884744 | tf_op jit(solution)/shard_map/ppermute | solution.py:350
  239.2 13.2 %all-to-all-start.3 = ((f32[4,80,256]{2,1,0:T(8,128)}), f32[4,80,256]{2,1,0:T(8,128)S(1)}, u32[]{:S(2)}, u32[]{:S(2)}) async-start(f32[4,80,256]{2,1,0:T(8,128)} %broadcast_in_dim.9), calls=%async_computation.3 | async-start | bytes 655360 | tf_op jit(solution)/shard_map/all_to_all | solution.py:390
  253.3 20.2 %all-to-all-start.4 = ((f32[4,144,256]{2,1,0:T(8,128)}), f32[4,144,256]{2,1,0:T(8,128)S(1)}, u32[]{:S(2)}, u32[]{:S(2)}) async-start(f32[4,144,256]{2,1,0:T(8,128)} %broadcast_in_dim.10), calls=%async_computation.4 | async-start | bytes 1179648 | tf_op jit(solution)/shard_map/all_to_all | solution.py:390
  257.9 14.3 %collective-permute-start.48 = (f32[320,256]{1,0:T(8,128)S(1)}, f32[320,256]{1,0:T(8,128)}, u32[]{:S(2)}, u32[]{:S(2)}) collective-permute-start(f32[320,256]{1,0:T(8,128)S(1)} %bitcast.86), channel_id=1, source_target_pairs={{0,16},{8,24},{16,0},{24,8},{1,17},{9,25},{17,1},{25,9},{2,18},{10... | collective-permute-start | bytes 983048 | tf_op jit(solution)/shard_map/ppermute | solution.py:350
  258.1 14.1 %collective-permute-start.49 = (f32[320,256]{1,0:T(8,128)S(1)}, f32[320,256]{1,0:T(8,128)}, u32[]{:S(2)}, u32[]{:S(2)}) collective-permute-start(f32[320,256]{1,0:T(8,128)S(1)} %bitcast.87), channel_id=1, source_target_pairs={{0,24},{8,16},{16,8},{24,0},{1,25},{9,17},{17,9},{25,1},{2,26},{10... | collective-permute-start | bytes 983048 | tf_op jit(solution)/shard_map/ppermute | solution.py:350
  260.9 19.9 %collective-permute-start.50 = (f32[320,256]{1,0:T(8,128)S(1)}, f32[320,256]{1,0:T(8,128)}, u32[]{:S(2)}, u32[]{:S(2)}) collective-permute-start(f32[320,256]{1,0:T(8,128)S(1)} %bitcast.88), channel_id=1, source_target_pairs={{0,1},{1,0},{2,3},{3,2},{4,5},{5,4},{6,7},{7,6},{8,9},{9,8},{10,11... | collective-permute-start | bytes 983048 | tf_op jit(solution)/shard_map/ppermute | solution.py:350
  274.5 35.5 %all-to-all-start.5 = ((f32[4,144,256]{2,1,0:T(8,128)}), f32[4,144,256]{2,1,0:T(8,128)}, u32[]{:S(2)}, u32[]{:S(2)}) async-start(f32[4,144,256]{2,1,0:T(8,128)} %broadcast_in_dim.11), calls=%async_computation.5 | async-start | bytes 1179648 | tf_op jit(solution)/shard_map/all_to_all | solution.py:390
  279.3 67.4 %all-gather.4.cloned.1.call-start = ((), (), s32[]{:S(2)}) async-start(), calls=%async_computation.7 | async-start | bytes 2359296 | tf_op jit(solution)/shard_map/all_gather | solution.py:453
  279.3 24.7 %collective-permute-start.54 = (f32[576,256]{1,0:T(8,128)S(1)}, f32[576,256]{1,0:T(8,128)S(1)}, u32[]{:S(2)}, u32[]{:S(2)}) collective-permute-start(f32[576,256]{1,0:T(8,128)S(1)} %bitcast.79), channel_id=1, source_target_pairs={{0,8},{8,0},{16,24},{24,16},{1,9},{9,1},{17,25},{25,17},{2,10},{10... | collective-permute-start | bytes 1769480 | tf_op jit(solution)/shard_map/ppermute | solution.py:350
  280.8 27.3 %collective-permute-start.55 = (f32[576,256]{1,0:T(8,128)S(1)}, f32[576,256]{1,0:T(8,128)S(1)}, u32[]{:S(2)}, u32[]{:S(2)}) collective-permute-start(f32[576,256]{1,0:T(8,128)S(1)} %bitcast.80), channel_id=1, source_target_pairs={{0,16},{8,24},{16,0},{24,8},{1,17},{9,25},{17,1},{25,9},{2,18},{10... | collective-permute-start | bytes 1769480 | tf_op jit(solution)/shard_map/ppermute | solution.py:350
  280.8 27.3 %collective-permute-start.56 = (f32[576,256]{1,0:T(8,128)S(1)}, f32[576,256]{1,0:T(8,128)S(1)}, u32[]{:S(2)}, u32[]{:S(2)}) collective-permute-start(f32[576,256]{1,0:T(8,128)S(1)} %bitcast.81), channel_id=1, source_target_pairs={{0,24},{8,16},{16,8},{24,0},{1,25},{9,17},{17,9},{25,1},{2,26},{10... | collective-permute-start | bytes 1769480 | tf_op jit(solution)/shard_map/ppermute | solution.py:350
  310.0 33.9 %collective-permute-start.61 = (f32[576,256]{1,0:T(8,128)}, f32[576,256]{1,0:T(8,128)}, u32[]{:S(2)}, u32[]{:S(2)}) collective-permute-start(f32[576,256]{1,0:T(8,128)} %bitcast.17.refs_0_), channel_id=1, source_target_pairs={{0,8},{8,0},{16,24},{24,16},{1,9},{9,1},{17,25},{25,17},{2,10},{10... | collective-permute-start | bytes 1769480 | tf_op jit(solution)/shard_map/ppermute | solution.py:350
  310.5 72.3 %all-gather.6.cloned.1.call-start = ((), (), s32[]{:S(2)}) async-start(), calls=%async_computation.8 | async-start | bytes 1769472 | tf_op jit(solution)/shard_map/all_gather | solution.py:453
  310.6 33.3 %collective-permute-start.62 = (f32[576,256]{1,0:T(8,128)}, f32[576,256]{1,0:T(8,128)}, u32[]{:S(2)}, u32[]{:S(2)}) collective-permute-start(f32[576,256]{1,0:T(8,128)} %bitcast.17.refs_0_), channel_id=1, source_target_pairs={{0,16},{8,24},{16,0},{24,8},{1,17},{9,25},{17,1},{25,9},{2,18},{10... | collective-permute-start | bytes 1769480 | tf_op jit(solution)/shard_map/ppermute | solution.py:350
  311.8 32.1 %collective-permute-start.63 = (f32[576,256]{1,0:T(8,128)}, f32[576,256]{1,0:T(8,128)}, u32[]{:S(2)}, u32[]{:S(2)}) collective-permute-start(f32[576,256]{1,0:T(8,128)} %bitcast.17.refs_0_), channel_id=1, source_target_pairs={{0,24},{8,16},{16,8},{24,0},{1,25},{9,17},{17,9},{25,1},{2,26},{10... | collective-permute-start | bytes 1769480 | tf_op jit(solution)/shard_map/ppermute | solution.py:350
  346.7 58.2 %all-gather.8.cloned.1.call-start = ((), (), s32[]{:S(2)}) async-start(), calls=%async_computation.9 | async-start | bytes 1179648 | tf_op jit(solution)/shard_map/all_gather | solution.py:453
  408.3 32.1 %all-to-all-start.6 = ((bf16[4,576,512]{2,1,0:T(8,128)(2,1)}), bf16[4,576,512]{2,1,0:T(8,128)(2,1)S(1)}, u32[]{:S(2)}, u32[]{:S(2)}) async-start(bf16[4,576,512]{2,1,0:T(8,128)(2,1)} %bitcast.68), calls=%async_computation.6 | async-start | bytes 4718592 | tf_op jit(solution)/shard_map/all_to_all | solution.py:457
  (75 other events, 677.9 us)
Sparse Core Ops, SparseCore 0:
  310.6 29.3 all-gather.3
  346.8 24.7 all-gather.5
  382.9 21.8 all-gather.7

commit v4 on v3

--- a/solution.py
+++ b/solution.py
@@ -165,10 +165,14 @@
     return [(i, k) for k in range(high) for i in range(max(k, low), high)]
 
 
+def lengths_of(bounds, part):
+    return [(len(tiles_of(low, high)) + 1) // 2 * part for low, high in zip(bounds, bounds[1:])]
+
+
 def gram_kernel(layout, bounds, parts, spot_ref, *refs):
-    piece_refs, gram_refs = refs[: len(layout)], refs[len(layout) : len(layout) + len(bounds) - 1]
-    mine_ref, sketch_ref, high_ref, low_ref, own_high_ref, own_low_ref, sems = refs[len(layout) + len(bounds) - 1 :]
-    spot = spot_ref[0]
+    piece_refs, refs = refs[: len(layout)], refs[len(layout) :]
+    kept_ref, given_ref, mine_ref, gram_ref, sketch_ref, high_ref, low_ref, own_high_ref, own_low_ref, sems = refs
+    spot, core = spot_ref[0], spot_ref[1]
     sets, size, width = sketch_ref.shape
     step, part, rows = size // parts, TILE // parts, width // parts
     copies = []
@@ -185,46 +189,70 @@
             here = slice(i * TILE, (i + 1) * TILE)
             values = sketch_ref[s, here, :]
             high_ref[s, here, :], low_ref[s, here, :] = halves(values)
-            mine = values[:, :rows]
-            for other in range(1, parts):
-                mine = jnp.where(spot == other, values[:, other * rows : (other + 1) * rows], mine)
-            mine_ref[s * rows : (s + 1) * rows, here] = mine.T
         for i in range(bounds[-1]):
             at = pl.multiple_of(i * TILE + spot * part, 16)
             own_high_ref[s, i * part : (i + 1) * part, :] = high_ref[s, pl.ds(at, part), :]
             own_low_ref[s, i * part : (i + 1) * part, :] = low_ref[s, pl.ds(at, part), :]
-    for gram_ref, low, high in zip(gram_refs, bounds, bounds[1:]):
-        done = 0
+    lengths = lengths_of(bounds, part)
+    chips = gram_ref.shape[1]
+    base = 0
+    for length, low, high in zip(lengths, bounds, bounds[1:]):
+        step, at = length // chips, 0
+
+        def store(at, values):
+            done = 0
+            while done < values.shape[0]:
+                owner, rest = divmod(at + done, length)
+                chip, offset = divmod(rest, step)
+                rows = min(values.shape[0] - done, step - offset)
+                gram_ref[owner, chip, base + offset : base + offset + rows, :] = values[done : done + rows]
+                done += rows
+            return at + done
+
         for k in range(high):
             here, own = slice(k * TILE, (k + 1) * TILE), slice(max(k, low) * part, high * part)
             products = [
                 dot3((own_high_ref[s, own, :], own_low_ref[s, own, :]), (high_ref[s, here, :], low_ref[s, here, :]), NT)
                 for s in range(sets)
             ]
-            gram_ref[done : done + own.stop - own.start, :] = sum(products)
-            done += own.stop - own.start
-        if done < gram_ref.shape[0]:
-            gram_ref[done:, :] = jnp.zeros((gram_ref.shape[0] - done, TILE), F32)
-
-
-def gram_shares(spot, sets, parts):
+            at = store(at, sum(products))
+        if at < 2 * length:
+            store(at, jnp.zeros((2 * length - at, TILE), F32))
+        base += step
+    copies = [
+        pltpu.make_async_copy(gram_ref.at[core], kept_ref, sems.at[0]),
+        pltpu.make_async_copy(gram_ref.at[1 - core], given_ref, sems.at[1]),
+    ]
+    for copy in copies:
+        copy.start()
+    for s in range(sets):
+        for i in range(bounds[-1]):
+            here = slice(i * TILE, (i + 1) * TILE)
+            values = sketch_ref[s, here, :]
+            mine = values[:, :rows]
+            for other in range(1, parts):
+                mine = jnp.where(spot == other, values[:, other * rows : (other + 1) * rows], mine)
+            mine_ref[s * rows : (s + 1) * rows, here] = mine.T
+    for copy in copies:
+        copy.wait()
+
+
+def gram_shares(spots, sets, parts, chips):
     layout = [(s, d, offset) for s, pieces in enumerate(sets) for d, offset, _ in pieces]
     arrays = [array for pieces in sets for _, _, array in pieces]
     width, rows = arrays[0].shape
     size = parts * width
     count, part = size // TILE, TILE // parts
     bounds = bounds_of(count)
-    shapes = []
-    for low, high in zip(bounds, bounds[1:]):
-        tiles = len(tiles_of(low, high))
-        shapes.append(jax.ShapeDtypeStruct(((tiles + tiles % 2) * part, TILE), F32))
-    shapes.append(jax.ShapeDtypeStruct((len(sets) * rows // parts, size), F32))
+    shared = (chips, sum(lengths_of(bounds, part)) // chips, TILE)
+    shape = jax.ShapeDtypeStruct
     return pl.pallas_call(
         functools.partial(gram_kernel, layout, bounds, parts),
-        out_shape=shapes,
+        out_shape=[shape(shared, F32), shape(shared, F32), shape((len(sets) * rows // parts, size), F32)],
         in_specs=[SMEM] + [ANY] * len(arrays),
-        out_specs=[VMEM] * len(shapes),
+        out_specs=[ANY, ANY, VMEM],
         scratch_shapes=[
+            pltpu.VMEM((2,) + shared, F32),
             pltpu.VMEM((len(sets), size, rows), F32),
             pltpu.VMEM((len(sets), size, rows), BF16),
             pltpu.VMEM((len(sets), size, rows), BF16),
@@ -236,18 +264,26 @@
         cost_estimate=pl.CostEstimate(
             flops=3 * size * size * rows // parts, bytes_accessed=8 * size * rows, transcendentals=0
         ),
-    )(spot, *arrays)
-
-
-def basis_kernel(scale, layout, cuts, parts, spot_ref, *refs):
+    )(spots, *arrays)
+
+
+def basis_kernel(scale, layout, cuts, parts, final, spot_ref, *refs):
     refs = list(refs)
-    take = lambda n: [refs.pop(0) for _ in range(n)]
+
+    def take(number):
+        return [refs.pop(0) for _ in range(number)]
+
     share_refs = take(len(layout))
     (sketch_ref,) = take(1)
+    past_refs = [take(6) for _ in cuts[:-2]]
+    first, last = cuts[-2:]
+    if final:
+        basis_ref, short_ref, rest_ref, inv_high_ref, inv_low_ref = take(5)
+    else:
+        basis_ref, short_ref, rest_ref, high_out, low_out, inv_high_ref, inv_low_ref = take(7)
+    high_ref, low_ref, gram_ref, inverse_ref, work_ref = take(5)
     past = [take(6) for _ in cuts[:-2]]
-    basis_ref, short_ref, rest_ref, high_ref, low_ref, inv_high_ref, inv_low_ref = take(7)
-    gram_ref, inverse_ref, work_ref, sems = refs
-    first, last = cuts[-2:]
+    sems, past_sems, out_sems = refs
     part, half = TILE // parts, gram_ref.shape[2]
     spot, core = spot_ref[0], spot_ref[1]
     copies = []
@@ -256,6 +292,41 @@
         copies.append(pltpu.make_async_copy(share_refs[n], target, sems.at[n]))
     for copy in copies:
         copy.start()
+    whole_copies, row_copies = [], []
+    for n, (sources, targets, top, bottom) in enumerate(zip(past_refs, past, cuts, cuts[1:])):
+        whole_copies.append(
+            [pltpu.make_async_copy(sources[m], targets[m], past_sems.at[n, m]) for m in (0, 1, 4, 5)]
+        )
+        for k in range(top, bottom):
+            here, cols = pl.ds((k - top) * TILE, TILE), pl.ds(0, k * TILE)
+            row_copies.append(
+                [
+                    pltpu.make_async_copy(
+                        sources[m].at[here, cols], targets[m].at[here, cols], past_sems.at[n, 4 + m + 2 * (k - top)]
+                    )
+                    for m in (2, 3)
+                    if k
+                ]
+            )
+    for group in whole_copies:
+        group[2].start()
+        group[3].start()
+    for group in row_copies:
+        for copy in group:
+            copy.start()
+    for group in whole_copies:
+        group[0].start()
+        group[1].start()
+    out_copies = []
+
+    def send(k, start):
+        if not final and start < (last - first) * TILE:
+            here, cols = pl.ds(start, (last - first) * TILE - start), pl.ds(k * TILE, TILE)
+            for m, (source, target) in enumerate(((high_ref, high_out), (low_ref, low_out))):
+                copy = pltpu.make_async_copy(source.at[here, cols], target.at[here, cols], out_sems.at[m, k])
+                copy.start()
+                out_copies.append(copy)
+
     for copy in copies:
         copy.wait()
     index = {tile: n * part for n, tile in enumerate(tiles_of(first, last))}
@@ -275,16 +346,26 @@
         here, cols = slice((low - first) * TILE, (high - first) * TILE), slice(k * TILE, (k + 1) * TILE)
         high_ref[here, cols], low_ref[here, cols] = halves(values)
 
-    for (top, bottom), (_, _, past_high, past_low, past_inv_high, past_inv_low) in zip(zip(cuts, cuts[1:]), past):
+    for n, (top, bottom) in enumerate(zip(cuts[:-2], cuts[1:])):
+        _, _, past_high, past_low, past_inv_high, past_inv_low = past[n]
         for k in range(top, bottom):
+            if k == top:
+                whole_copies[n][2].wait()
+                whole_copies[n][3].wait()
+            for copy in row_copies[k]:
+                copy.wait()
             here = slice((k - top) * TILE, (k - top + 1) * TILE)
             values = gram_rows(first, last, k)
             if k:
                 factor = past_high[here, : k * TILE], past_low[here, : k * TILE]
                 values = values - dot3(rows_of(first, last, k), factor, NT)
             own = past_inv_high[here, :], past_inv_low[here, :]
-            store_rows(first, last, k, dot3(halves(values), own, NT))
-
+            store_rows(first, last, k, dot3(halves(values), own))
+            send(k, 0)
+
+    for group in whole_copies:
+        group[0].wait()
+        group[1].wait()
     for k in range(first, last):
         here = slice((k - first) * TILE, (k - first + 1) * TILE)
         factor = rows_of(k, k + 1, k)
@@ -294,10 +375,11 @@
             return values - dot3(rows_of(low, high, k), factor, NT) if k else values
 
         inverse_factor(left_over(k, k + 1), inverse_ref, work_ref)
-        inv_high_ref[here, :], inv_low_ref[here, :] = halves(inverse_ref[...])
+        inv_high_ref[here, :], inv_low_ref[here, :] = halves(inverse_ref[...].T)
         own = inv_high_ref[here, :], inv_low_ref[here, :]
         if k + 1 < last:
-            store_rows(k + 1, last, k, dot3(halves(left_over(k + 1, last)), own, NT))
+            store_rows(k + 1, last, k, dot3(halves(left_over(k + 1, last)), own))
+            send(k, (k + 1 - first) * TILE)
         values = sketch_ref[:, here]
         for (top, bottom), (past_short, past_rest, *_) in zip(zip(cuts, cuts[1:]), past):
             cols = slice(top * TILE, bottom * TILE)
@@ -310,12 +392,14 @@
             values = values - dot3(
                 (short_ref[:, done], rest_ref[:, done]), (factor[0][:, cols], factor[1][:, cols]), NT
             )
-        solved = dot3(halves(values), own, NT)
+        solved = dot3(halves(values), own)
         basis_ref[:, here] = solved
         short_ref[:, here], rest_ref[:, here] = halves(solved)
-
-
-def basis_part(spots, shares, sketch, past, cuts, parts, scale):
+    for copy in out_copies:
+        copy.wait()
+
+
+def basis_part(spots, shares, sketch, past, cuts, parts, scale, final):
     first, last = cuts[-2:]
     rows, width = sketch.shape
     layout = [(e, d, offset) for e, d, offset, _ in shares]
@@ -324,20 +408,26 @@
     flat = [array for arrays_of_part in past for array in arrays_of_part]
     shape = jax.ShapeDtypeStruct
     size = last * TILE
+    factor = shape((width, size), BF16)
+    kept_shapes = [shape((rows, width), BF16)] * 2 + [factor] * 2 + [shape((width, TILE), BF16)] * 2
+    kept_specs = [VMEM, VMEM, ANY, ANY, VMEM, VMEM]
+    scratch = [pltpu.VMEM((width, size), BF16)] * 2
+    scratch += [pltpu.VMEM((2, parts, half, TILE), F32)] + [pltpu.VMEM((TILE, TILE), F32)] * 2
+    scratch += [pltpu.VMEM(x.shape, x.dtype) for x in flat]
+    scratch += [
+        pltpu.SemaphoreType.DMA((len(arrays),)),
+        pltpu.SemaphoreType.DMA((max(len(past), 1), 6 + 2 * last)),
+        pltpu.SemaphoreType.DMA((2, last)),
+    ]
+    if final:
+        scratch = [pltpu.VMEM(kept_shapes[n].shape, BF16) for n in (1, 4, 5)] + scratch
+        kept_shapes, kept_specs = kept_shapes[:1], kept_specs[:1]
     basis, *kept = pl.pallas_call(
-        functools.partial(basis_kernel, scale, layout, cuts, parts),
-        out_shape=[shape((rows, width), F32)]
-        + [shape((rows, width), BF16)] * 2
-        + [shape((width, size), BF16)] * 2
-        + [shape((width, TILE), BF16)] * 2,
-        in_specs=[SMEM] + [ANY] * len(arrays) + [VMEM] * (1 + len(flat)),
-        out_specs=[VMEM] * 7,
-        scratch_shapes=[
-            pltpu.VMEM((2, parts, half, TILE), F32),
-            pltpu.VMEM((TILE, TILE), F32),
-            pltpu.VMEM((TILE, TILE), F32),
-            pltpu.SemaphoreType.DMA((len(arrays),)),
-        ],
+        functools.partial(basis_kernel, scale, layout, cuts, parts, final),
+        out_shape=[shape((rows, width), F32)] + kept_shapes,
+        in_specs=[SMEM] + [ANY] * len(arrays) + [VMEM] + [ANY] * len(flat),
+        out_specs=[VMEM] + kept_specs,
+        scratch_shapes=scratch,
         compiler_params=pltpu.CompilerParams(vmem_limit_bytes=60 << 20),
         cost_estimate=pl.CostEstimate(
             flops=128 * size * size * width, bytes_accessed=4 * size * width, transcendentals=0
@@ -413,17 +503,10 @@
         sets.append(row_pieces(dot(omega, theta_set, (((0,), (1,)), ((), ())))))
     theta = jnp.stack(thetas, axis=1).reshape(-1, right_cols.shape[1])
     cols_here = theta.shape[1]
-    *gram, sketch = gram_shares(spots, sets, parts)
+    kept, given, sketch = gram_shares(spots, sets, parts, chips)
     bounds = bounds_of(sketch.shape[1] // TILE)
-
-    halved = []
-    for share in gram:
-        half = share.shape[0] // 2
-        kept = lax.dynamic_slice_in_dim(share, core * half, half, 0)
-        given = lax.dynamic_slice_in_dim(share, (1 - core) * half, half, 0)
-        halved.append((kept + swapped(given, "core", 1)).reshape(chips, half // chips, TILE))
-    lengths = [x.shape[1] for x in halved]
-    summed = jnp.sum(lax.all_to_all(jnp.concatenate(halved, axis=1), "chip", 0, 0), axis=0)
+    lengths = [length // chips for length in lengths_of(bounds, TILE // parts)]
+    summed = jnp.sum(lax.all_to_all(kept + swapped(given, "core", 1), "chip", 0, 0), axis=0)
     gathered = []
     for n, length in enumerate(lengths):
         share = summed[sum(lengths[:n]) : sum(lengths[: n + 1])]
@@ -444,7 +527,7 @@
             columns, gathered[1] = together(columns, gathered[1])
         if n > 1:
             columns, rows[n - 2] = together(columns, rows[n - 2])
-        done, kept = basis_part(spots, shares, columns, past, cuts, parts, 1.0 / total_rows)
+        done, kept = basis_part(spots, shares, columns, past, cuts, parts, 1.0 / total_rows, n + 2 == len(bounds))
         past.append(kept)
         basis.append(done)
         short = kept[0]

time: 454 us -> 453 us (level)
    dynamic_slice x3 -> x0, local copies, waits for them, and re-layouts: 4.67 us -> none  [on_device(): given = lax.dynamic_slice_in_dim(share, (1 - core) * half, half, 0)]
    ppermute x68 -> x66, waiting for transfers between devices: 85.9 us -> 88.1 us  [swapped(): lax.ppermute(x, axis, [(i, i ^ distance) for i in range(lax.axis_size(axi...]
    ppermute x68 -> x66, starting transfers between devices: 64.8 us -> 64.5 us  [swapped(): lax.ppermute(x, axis, [(i, i ^ distance) for i in range(lax.axis_size(axi...]
  transfers between devices with their start and end apart: 77 -> 75, of which waited for: 32 -> 31; matrix products, arithmetic and copies ran while one was open for 6% -> 5% of each run, Pallas kernels for 21% -> 21%
where the time goes in v4:
time: 453 us; the launch traced here: 448 us
  waiting for transfers between devices  157 us (35%)
  Pallas kernels  106 us (23%)
  starting transfers between devices  90.9 us (20%)
  blocking collectives  38.9 us (9%)
  local copies, waits for them, and re-layouts  18.4 us (4%)
  between operations  14.7 us (3%)
  other arithmetic  12.6 us (3%)
  matrix products  9.58 us (2%)
    ppermute x66, waiting for transfers between devices, swapped(): lax.ppermute(x, axis, [(i, i ^ distance) for i in range(lax.axis_size(axi...  88.1 us
    pallas_call x3, Pallas kernels, basis_part(): pl.pallas_call(functools.partial(basis_kernel, scale, layout, cuts, parts...  85.9 us
    ppermute x66, starting transfers between devices, swapped(): lax.ppermute(x, axis, [(i, i ^ distance) for i in range(lax.axis_size(axi...  64.5 us
    all_to_all x1, blocking collectives, on_device(): lax.all_to_all(kept + swapped(given, 'core', 1), 'chip', 0, 0)  38.9 us
    all_to_all x1, waiting for transfers between devices, on_device(): sums = lax.all_to_all(folded, 'row', 0, 0)  27.2 us
    all_gather x3, waiting for transfers between devices, on_device(): rows.append(lax.all_gather(short, COL, axis=0, tiled=True))  17.5 us
    all_to_all x2, waiting for transfers between devices, on_device(): lax.all_to_all(theta, COL, 0, 1, tiled=True)  14.2 us
    all_to_all x3, starting transfers between devices, gathered_chips(): return lax.all_to_all(spread, 'chip', 0, 0).reshape(-1, x.shape[1])  12.3 us
  transfers between devices with their start and end apart: 75, of which 31 were waited for; matrix products, arithmetic and copies ran while one was open for 5% of the time, Pallas kernels for 21%

profile of v4, /device:TPU:0, one launch (start us, length us, event | category | flops | bytes accessed | tf_op | source)
XLA Modules:
  0.0 448.0 jit_solution(17511511735884509095)
XLA Ops:
  8.2 3.0 collective-permute-start.10
  14.4 2.1 collective-permute-start
  16.5 1.9 collective-permute-done.10
  18.4 3.2 collective-permute-start.1
  21.5 1.7 collective-permute-done.7
  23.3 3.9 collective-permute-start.2
  27.1 1.6 collective-permute-start.11
  30.2 9.0 %collective-permute-done.1.refs_2_ = bf16[512,256]{1,0:T(8,128)(2,1)S(1)} collective-permute-done((bf16[512,256]{1,0:T(8,128)(2,1)S(1)}, bf16[512,256]{1,0:T(8,128)(2,1)S(1)}, u32[]{:S(2)}, u32[]{:S(2)}) %collective-permute-start.1) | collective-permute-done | bytes 262176 | tf_op jit(solution)/shard_map/ppermute | solution.py:440
  40.4 3.2 collective-permute-start.13
  43.6 1.9 collective-permute-start.14
  50.7 4.4 shard_map.59
  55.1 9.9 %collective-permute-done.14.refs_2_ = bf16[512,256]{1,0:T(8,128)(2,1)S(1)} collective-permute-done((bf16[512,256]{1,0:T(8,128)(2,1)S(1)}, bf16[512,256]{1,0:T(8,128)(2,1)S(1)}, u32[]{:S(2)}, u32[]{:S(2)}) %collective-permute-start.14) | collective-permute-done | bytes 262176 | tf_op jit(solution)/shard_map/ppermute | solution.py:440
  66.4 6.1 %all-to-all-start = ((bf16[8,64,512]{2,1,0:T(8,128)(2,1)}), bf16[8,64,512]{2,1,0:T(8,128)(2,1)}, u32[]{:S(2)}, u32[]{:S(2)}) async-start(bf16[8,64,512]{2,1,0:T(8,128)(2,1)} %bitcast.6), calls=%async_computation | async-start | bytes 1048576 | tf_op jit(solution)/shard_map/all_to_all | solution.py:502
  78.3 4.0 shard_map.60
  82.3 5.7 %all-to-all-done = bf16[8,64,512]{2,1,0:T(8,128)(2,1)} async-done(((bf16[8,64,512]{2,1,0:T(8,128)(2,1)}), bf16[8,64,512]{2,1,0:T(8,128)(2,1)}, u32[]{:S(2)}, u32[]{:S(2)}) %all-to-all-start) | async-done | bytes 524320 | tf_op jit(solution)/shard_map/all_to_all | solution.py:502
  87.9 3.8 all-to-all-start.1
  98.4 8.6 %all-to-all-done.1 = bf16[8,64,512]{2,1,0:T(8,128)(2,1)S(1)} async-done(((bf16[8,64,512]{2,1,0:T(8,128)(2,1)}), bf16[8,64,512]{2,1,0:T(8,128)(2,1)S(1)}, u32[]{:S(2)}, u32[]{:S(2)}) %all-to-all-start.1) | async-done | bytes 524320 | tf_op jit(solution)/shard_map/all_to_all | solution.py:502
  108.7 1.6 collective-permute-start.34
  115.2 12.4 %collective-permute-done.20 = bf16[32,4096]{1,0:T(8,128)(2,1)S(1)} collective-permute-done((bf16[32,4096]{1,0:T(8,128)(2,1)S(1)}, bf16[32,4096]{1,0:T(8,128)(2,1)S(1)}, u32[]{:S(2)}, u32[]{:S(2)}) %collective-permute-start.20) | collective-permute-done | bytes 262176 | tf_op jit(solution)/shard_map/ppermute | solution.py:440
  128.1 3.9 convolution_bitcast_fusion.1.refs_0_
  137.9 11.3 %collective-permute-done.36 = bf16[32,4096]{1,0:T(8,128)(2,1)S(1)} collective-permute-done((bf16[32,4096]{1,0:T(8,128)(2,1)S(1)}, bf16[32,4096]{1,0:T(8,128)(2,1)S(1)}, u32[]{:S(2)}, u32[]{:S(2)}) %collective-permute-start.36) | collective-permute-done | bytes 262176 | tf_op jit(solution)/shard_map/ppermute | solution.py:440
  157.1 1.7 collective-permute-done.25.refs_2_
  158.8 1.9 collective-permute-start.26
  160.7 4.4 collective-permute-done.38.refs_8_
  165.7 3.5 collective-permute-done.39.refs_11_
  169.2 2.3 collective-permute-done.41.refs_9_
  174.9 3.2 collective-permute-done.42.refs_12_
  180.5 12.0 %shard_map.61 = (f32[4,368,256]{2,1,0:T(8,128)}, f32[4,368,256]{2,1,0:T(8,128)}, f32[128,2304]{1,0:T(8,128)}) custom-call(s32[3]{0:T(128)} %copy-done.7, f32[576,256]{1,0:T(8,128)} %copy-done.8, f32[288,256]{1,0:T(8,128)} %copy-done.16, f32[288,256]{1,0:T(8,128)} %copy-done.19, f32[288,256]{1,0:T(8,128)} %copy-done.17, f32[288,256]{1,0:T(8,128)} %copy-done.18, ...), custom_call_target="tpu_custom_call" | custom-call | flops 1019215872 | bytes 4718592 | tf_op jit(solution)/shard_map/pallas_call | solution.py:249
  192.6 3.5 collective-permute-done.44
  196.1 1.6 add.39
  197.7 38.9 %all_to_all.63 = f32[4,368,256]{2,1,0:T(8,128)S(1)} all-to-all(f32[4,368,256]{2,1,0:T(8,128)S(1)} %add.39), channel_id=1, replica_groups=mesh['row'=4,'chip'=4,'core'=2] {'chip'}, dimensions={0} | all-to-all | bytes 3014656 | tf_op jit(solution)/shard_map/all_to_all | solution.py:509
  237.4 3.5 all-to-all-start.3
  240.9 9.7 %all-to-all-done.3 = f32[4,80,256]{2,1,0:T(8,128)S(1)} async-done(((f32[4,80,256]{2,1,0:T(8,128)}), f32[4,80,256]{2,1,0:T(8,128)S(1)}, u32[]{:S(2)}, u32[]{:S(2)}) %all-to-all-start.3) | async-done | bytes 327712 | tf_op jit(solution)/shard_map/all_to_all | solution.py:480
  251.5 4.0 all-to-all-start.4
  256.7 2.3 collective-permute-start.47
  259.0 7.2 %collective-permute-done.45.refs_1_ = f32[320,256]{1,0:T(8,128)S(1)} collective-permute-done((f32[320,256]{1,0:T(8,128)S(1)}, f32[320,256]{1,0:T(8,128)S(1)}, u32[]{:S(2)}, u32[]{:S(2)}) %collective-permute-start.45) | collective-permute-done | bytes 327712 | tf_op jit(solution)/shard_map/ppermute | solution.py:440
  266.2 4.2 collective-permute-done.46.refs_2_
  272.7 4.8 %all-to-all-start.5 = ((f32[4,144,256]{2,1,0:T(8,128)}), f32[4,144,256]{2,1,0:T(8,128)}, u32[]{:S(2)}, u32[]{:S(2)}) async-start(f32[4,144,256]{2,1,0:T(8,128)} %broadcast_in_dim.11), calls=%async_computation.5 | async-start | bytes 1179648 | tf_op jit(solution)/shard_map/all_to_all | solution.py:480
  281.0 21.1 %shard_map.62 = (f32[128,1024]{1,0:T(8,128)}, bf16[128,1024]{1,0:T(8,128)(2,1)}, bf16[128,1024]{1,0:T(8,128)(2,1)}, bf16[1024,1024]{1,0:T(8,128)(2,1)}, bf16[102...) custom-call(s32[3]{0:T(128)} %copy-done.7, f32[320,256]{1,0:T(8,128)} %bitcast.83, ...), custom_call_target="tpu_custom_call" | custom-call | flops 137438953472 | bytes 4194304 | tf_op jit(solution)/shard_map/pallas_call | solution.py:425
  302.2 4.1 collective-permute-done.53.refs_2_
  310.0 1.8 collective-permute-start.61
  311.9 31.1 %shard_map.63 = (f32[128,768]{1,0:T(8,128)}, bf16[128,768]{1,0:T(8,128)(2,1)}, bf16[128,768]{1,0:T(8,128)(2,1)}, bf16[768,1792]{1,0:T(8,128)(2,1)}, bf16[768,179...) custom-call(s32[3]{0:T(128)} %copy-done.7, f32[576,256]{1,0:T(8,128)} %bitcast.77, ...), custom_call_target="tpu_custom_call" | custom-call | flops 315680096256 | bytes 5505024 | tf_op jit(solution)/shard_map/pallas_call | solution.py:425
  344.1 1.7 slice.87.refs_8_
  348.7 33.7 %shard_map.64 = (f32[128,512]{1,0:T(8,128)}, bf16[128,512]{1,0:T(8,128)(2,1)}) custom-call(s32[3]{0:T(128)} %copy-done.7, f32[576,256]{1,0:T(8,128)} %bitcast.14.refs_0_, f32[576,256]{1,0:T(8,128)} %collective-permute-done.59.refs_1_, f32[576,256]{1,0:T(8,128)} %collective-permute-done.60.refs_2_, f32[576,256]{1,0:T(8,128)} %collective-permute-done.61.refs_3_, ...), custom_call_target="tpu_custom_call" | custom-call | flops 347892350976 | bytes 4718592 | tf_op jit(solution)/shard_map/pallas_call | solution.py:425
  386.7 17.5 %all-gather.8.cloned.1.call-done = bf16[1024,512]{1,0:T(8,128)(2,1)} async-done(((bf16[128,512]{1,0:T(8,128)(2,1)}), bf16[1024,512]{1,0:T(8,128)(2,1)}) %all-gather.8.cloned.1.call-update) | async-done | bytes 1048592 | tf_op jit(solution)/shard_map/all_gather | solution.py:536
  404.2 2.0 convolution_convert_fusion.2
  407.7 3.8 all-to-all-start.6
  412.6 27.2 %all-to-all-done.6 = bf16[4,576,512]{2,1,0:T(8,128)(2,1)S(1)} async-done(((bf16[4,576,512]{2,1,0:T(8,128)(2,1)}), bf16[4,576,512]{2,1,0:T(8,128)(2,1)S(1)}, u32[]{:S(2)}, u32[]{:S(2)}) %all-to-all-start.6) | async-done | bytes 2359328 | tf_op jit(solution)/shard_map/all_to_all | solution.py:540
  (251 shorter events, 77.9 us)
Async XLA Ops:
  11.2 15.9 %collective-permute-start.8 = (bf16[256,512]{1,0:T(8,128)(2,1)S(1)}, bf16[256,512]{1,0:T(8,128)(2,1)}, u32[]{:S(2)}, u32[]{:S(2)}) collective-permute-start(bf16[256,512]{1,0:T(8,128)(2,1)S(1)} %get-tuple-element.136), channel_id=1, source_target_pairs={{0,16},{8,24},{16,0},{24,8},{1,17},{9,25},{17,1},{25,9},{2,18},{10... | collective-permute-start | bytes 786440 | tf_op jit(solution)/shard_map/ppermute | solution.py:440
  13.3 13.8 %collective-permute-start.9 = (bf16[256,512]{1,0:T(8,128)(2,1)S(1)}, bf16[256,512]{1,0:T(8,128)(2,1)S(1)}, u32[]{:S(2)}, u32[]{:S(2)}) collective-permute-start(bf16[256,512]{1,0:T(8,128)(2,1)S(1)} %get-tuple-element.137), channel_id=1, source_target_pairs={{0,16},{8,24},{16,0},{24,8},{1,17},{9,25},{17,1},{25,9},{2,18},{10... | collective-permute-start | bytes 786440 | tf_op jit(solution)/shard_map/ppermute | solution.py:440
  14.4 14.3 %collective-permute-start = (bf16[512,256]{1,0:T(8,128)(2,1)S(1)}, bf16[512,256]{1,0:T(8,128)(2,1)S(1)}, u32[]{:S(2)}, u32[]{:S(2)}) collective-permute-start(bf16[512,256]{1,0:T(8,128)(2,1)S(1)} %bitcast.60), channel_id=1, source_target_pairs={{0,2},{2,0},{4,6},{6,4},{1,3},{3,1},{5,7},{7,5},{8,10},{10,8},{12,... | collective-permute-start | bytes 786440 | tf_op jit(solution)/shard_map/ppermute | solution.py:440
  18.4 20.9 %collective-permute-start.1 = (bf16[512,256]{1,0:T(8,128)(2,1)S(1)}, bf16[512,256]{1,0:T(8,128)(2,1)S(1)}, u32[]{:S(2)}, u32[]{:S(2)}) collective-permute-start(bf16[512,256]{1,0:T(8,128)(2,1)S(1)} %bitcast.61), channel_id=1, source_target_pairs={{0,4},{2,6},{4,0},{6,2},{1,5},{3,7},{5,1},{7,3},{8,12},{10,14},{12... | collective-permute-start | bytes 786440 | tf_op jit(solution)/shard_map/ppermute | solution.py:440
  23.3 17.1 %collective-permute-start.2 = (bf16[512,256]{1,0:T(8,128)(2,1)S(1)}, bf16[512,256]{1,0:T(8,128)(2,1)S(1)}, u32[]{:S(2)}, u32[]{:S(2)}) collective-permute-start(bf16[512,256]{1,0:T(8,128)(2,1)S(1)} %bitcast.62), channel_id=1, source_target_pairs={{0,6},{2,4},{4,2},{6,0},{1,7},{3,5},{5,3},{7,1},{8,14},{10,12},{12... | collective-permute-start | bytes 786440 | tf_op jit(solution)/shard_map/ppermute | solution.py:440
  27.1 16.5 %collective-permute-start.3 = (bf16[512,256]{1,0:T(8,128)(2,1)S(1)}, bf16[512,256]{1,0:T(8,128)(2,1)}, u32[]{:S(2)}, u32[]{:S(2)}) collective-permute-start(bf16[512,256]{1,0:T(8,128)(2,1)S(1)} %bitcast.63), channel_id=1, source_target_pairs={{0,1},{1,0},{2,3},{3,2},{4,5},{5,4},{6,7},{7,6},{8,9},{9,8},{10,11... | collective-permute-start | bytes 786440 | tf_op jit(solution)/shard_map/ppermute | solution.py:440
  27.1 18.4 %collective-permute-start.11 = (bf16[256,512]{1,0:T(8,128)(2,1)}, bf16[256,512]{1,0:T(8,128)(2,1)}, u32[]{:S(2)}, u32[]{:S(2)}) collective-permute-start(bf16[256,512]{1,0:T(8,128)(2,1)} %collective-permute-done.7), channel_id=1, source_target_pairs={{0,16},{8,24},{16,0},{24,8},{1,17},{9,25},{17,1},{25,9},{2,18},{10... | collective-permute-start | bytes 786440 | tf_op jit(solution)/shard_map/ppermute | solution.py:440
  28.7 18.3 %collective-permute-start.12 = (bf16[256,512]{1,0:T(8,128)(2,1)}, bf16[256,512]{1,0:T(8,128)(2,1)}, u32[]{:S(2)}, u32[]{:S(2)}) collective-permute-start(bf16[256,512]{1,0:T(8,128)(2,1)} %collective-permute-done.8), channel_id=1, source_target_pairs={{0,8},{8,0},{16,24},{24,16},{1,9},{9,1},{17,25},{25,17},{2,10},{10... | collective-permute-start | bytes 786440 | tf_op jit(solution)/shard_map/ppermute | solution.py:440
  40.4 14.7 %collective-permute-start.13 = (bf16[512,256]{1,0:T(8,128)(2,1)S(1)}, bf16[512,256]{1,0:T(8,128)(2,1)S(1)}, u32[]{:S(2)}, u32[]{:S(2)}) collective-permute-start(bf16[512,256]{1,0:T(8,128)(2,1)S(1)} %bitcast.55), channel_id=1, source_target_pairs={{0,2},{2,0},{4,6},{6,4},{1,3},{3,1},{5,7},{7,5},{8,10},{10,8},{12,... | collective-permute-start | bytes 786440 | tf_op jit(solution)/shard_map/ppermute | solution.py:440
  43.6 21.4 %collective-permute-start.14 = (bf16[512,256]{1,0:T(8,128)(2,1)S(1)}, bf16[512,256]{1,0:T(8,128)(2,1)S(1)}, u32[]{:S(2)}, u32[]{:S(2)}) collective-permute-start(bf16[512,256]{1,0:T(8,128)(2,1)S(1)} %bitcast.56), channel_id=1, source_target_pairs={{0,4},{2,6},{4,0},{6,2},{1,5},{3,7},{5,1},{7,3},{8,12},{10,14},{12... | collective-permute-start | bytes 786440 | tf_op jit(solution)/shard_map/ppermute | solution.py:440
  45.5 19.5 %collective-permute-start.15 = (bf16[512,256]{1,0:T(8,128)(2,1)S(1)}, bf16[512,256]{1,0:T(8,128)(2,1)S(1)}, u32[]{:S(2)}, u32[]{:S(2)}) collective-permute-start(bf16[512,256]{1,0:T(8,128)(2,1)S(1)} %bitcast.57), channel_id=1, source_target_pairs={{0,6},{2,4},{4,2},{6,0},{1,7},{3,5},{5,3},{7,1},{8,14},{10,12},{12... | collective-permute-start | bytes 786440 | tf_op jit(solution)/shard_map/ppermute | solution.py:440
  66.4 21.5 %all-to-all-start = ((bf16[8,64,512]{2,1,0:T(8,128)(2,1)}), bf16[8,64,512]{2,1,0:T(8,128)(2,1)}, u32[]{:S(2)}, u32[]{:S(2)}) async-start(bf16[8,64,512]{2,1,0:T(8,128)(2,1)} %bitcast.6), calls=%async_computation | async-start | bytes 1048576 | tf_op jit(solution)/shard_map/all_to_all | solution.py:502
  87.9 19.1 %all-to-all-start.1 = ((bf16[8,64,512]{2,1,0:T(8,128)(2,1)}), bf16[8,64,512]{2,1,0:T(8,128)(2,1)S(1)}, u32[]{:S(2)}, u32[]{:S(2)}) async-start(bf16[8,64,512]{2,1,0:T(8,128)(2,1)} %bitcast.9), calls=%async_computation.1 | async-start | bytes 1048576 | tf_op jit(solution)/shard_map/all_to_all | solution.py:502
  92.8 15.8 %collective-permute-start.16 = (bf16[32,4096]{1,0:T(8,128)(2,1)S(1)}, bf16[32,4096]{1,0:T(8,128)(2,1)S(1)}, u32[]{:S(2)}, u32[]{:S(2)}) collective-permute-start(bf16[32,4096]{1,0:T(8,128)(2,1)S(1)} %bitcast.88), channel_id=1, source_target_pairs={{0,8},{8,0},{16,24},{24,16},{1,9},{9,1},{17,25},{25,17},{2,10},{10... | collective-permute-start | bytes 786440 | tf_op jit(solution)/shard_map/ppermute | solution.py:440
  94.4 16.4 %collective-permute-start.18 = (bf16[32,4096]{1,0:T(8,128)(2,1)S(1)}, bf16[32,4096]{1,0:T(8,128)(2,1)}, u32[]{:S(2)}, u32[]{:S(2)}) collective-permute-start(bf16[32,4096]{1,0:T(8,128)(2,1)S(1)} %bitcast.89), channel_id=1, source_target_pairs={{0,16},{8,24},{16,0},{24,8},{1,17},{9,25},{17,1},{25,9},{2,18},{10... | collective-permute-start | bytes 786440 | tf_op jit(solution)/shard_map/ppermute | solution.py:440
  95.9 14.3 %collective-permute-start.17 = (bf16[32,4096]{1,0:T(8,128)(2,1)S(1)}, bf16[32,4096]{1,0:T(8,128)(2,1)}, u32[]{:S(2)}, u32[]{:S(2)}) collective-permute-start(bf16[32,4096]{1,0:T(8,128)(2,1)S(1)} %bitcast.90), channel_id=1, source_target_pairs={{0,16},{8,24},{16,0},{24,8},{1,17},{9,25},{17,1},{25,9},{2,18},{10... | collective-permute-start | bytes 786440 | tf_op jit(solution)/shard_map/ppermute | solution.py:440
  96.5 14.3 %collective-permute-start.19 = (bf16[32,4096]{1,0:T(8,128)(2,1)S(1)}, bf16[32,4096]{1,0:T(8,128)(2,1)}, u32[]{:S(2)}, u32[]{:S(2)}) collective-permute-start(bf16[32,4096]{1,0:T(8,128)(2,1)S(1)} %bitcast.91), channel_id=1, source_target_pairs={{0,8},{8,0},{16,24},{24,16},{1,9},{9,1},{17,25},{25,17},{2,10},{10... | collective-permute-start | bytes 786440 | tf_op jit(solution)/shard_map/ppermute | solution.py:440
  107.0 26.6 %collective-permute-start.32 = (bf16[32,4096]{1,0:T(8,128)(2,1)S(1)}, bf16[32,4096]{1,0:T(8,128)(2,1)S(1)}, u32[]{:S(2)}, u32[]{:S(2)}) collective-permute-start(bf16[32,4096]{1,0:T(8,128)(2,1)S(1)} %bitcast.84), channel_id=1, source_target_pairs={{0,8},{8,0},{16,24},{24,16},{1,9},{9,1},{17,25},{25,17},{2,10},{10... | collective-permute-start | bytes 786440 | tf_op jit(solution)/shard_map/ppermute | solution.py:440
  108.7 26.5 %collective-permute-start.34 = (bf16[32,4096]{1,0:T(8,128)(2,1)S(1)}, bf16[32,4096]{1,0:T(8,128)(2,1)S(1)}, u32[]{:S(2)}, u32[]{:S(2)}) collective-permute-start(bf16[32,4096]{1,0:T(8,128)(2,1)S(1)} %bitcast.85), channel_id=1, source_target_pairs={{0,16},{8,24},{16,0},{24,8},{1,17},{9,25},{17,1},{25,9},{2,18},{10... | collective-permute-start | bytes 786440 | tf_op jit(solution)/shard_map/ppermute | solution.py:440
  110.3 24.9 %collective-permute-start.33 = (bf16[32,4096]{1,0:T(8,128)(2,1)S(1)}, bf16[32,4096]{1,0:T(8,128)(2,1)S(1)}, u32[]{:S(2)}, u32[]{:S(2)}) collective-permute-start(bf16[32,4096]{1,0:T(8,128)(2,1)S(1)} %bitcast.86), channel_id=1, source_target_pairs={{0,16},{8,24},{16,0},{24,8},{1,17},{9,25},{17,1},{25,9},{2,18},{10... | collective-permute-start | bytes 786440 | tf_op jit(solution)/shard_map/ppermute | solution.py:440
  110.8 16.8 %collective-permute-start.20 = (bf16[32,4096]{1,0:T(8,128)(2,1)S(1)}, bf16[32,4096]{1,0:T(8,128)(2,1)S(1)}, u32[]{:S(2)}, u32[]{:S(2)}) collective-permute-start(bf16[32,4096]{1,0:T(8,128)(2,1)S(1)} %collective-permute-done.16), channel_id=1, source_target_pairs={{0,16},{8,24},{16,0},{24,8},{1,17},{9,25},{17,1},{25,9},{2,18},{10... | collective-permute-start | bytes 786440 | tf_op jit(solution)/shard_map/ppermute | solution.py:440
  112.3 15.8 %collective-permute-start.21 = (bf16[32,4096]{1,0:T(8,128)(2,1)}, bf16[32,4096]{1,0:T(8,128)(2,1)S(1)}, u32[]{:S(2)}, u32[]{:S(2)}) collective-permute-start(bf16[32,4096]{1,0:T(8,128)(2,1)} %collective-permute-done.17), channel_id=1, source_target_pairs={{0,8},{8,0},{16,24},{24,16},{1,9},{9,1},{17,25},{25,17},{2,10},{10... | collective-permute-start | bytes 786440 | tf_op jit(solution)/shard_map/ppermute | solution.py:440
  132.1 20.8 %collective-permute-start.22 = (f32[288,256]{1,0:T(8,128)S(1)}, f32[288,256]{1,0:T(8,128)S(1)}, u32[]{:S(2)}, u32[]{:S(2)}) collective-permute-start(f32[288,256]{1,0:T(8,128)S(1)} %get-tuple-element.129), channel_id=1, source_target_pairs={{0,8},{8,0},{16,24},{24,16},{1,9},{9,1},{17,25},{25,17},{2,10},{10... | collective-permute-start | bytes 884744 | tf_op jit(solution)/shard_map/ppermute | solution.py:440
  133.7 23.4 %collective-permute-start.24 = (f32[288,256]{1,0:T(8,128)S(1)}, f32[288,256]{1,0:T(8,128)S(1)}, u32[]{:S(2)}, u32[]{:S(2)}) collective-permute-start(f32[288,256]{1,0:T(8,128)S(1)} %get-tuple-element.129), channel_id=1, source_target_pairs={{0,16},{8,24},{16,0},{24,8},{1,17},{9,25},{17,1},{25,9},{2,18},{10... | collective-permute-start | bytes 884744 | tf_op jit(solution)/shard_map/ppermute | solution.py:440
  135.4 13.8 %collective-permute-start.36 = (bf16[32,4096]{1,0:T(8,128)(2,1)S(1)}, bf16[32,4096]{1,0:T(8,128)(2,1)S(1)}, u32[]{:S(2)}, u32[]{:S(2)}) collective-permute-start(bf16[32,4096]{1,0:T(8,128)(2,1)S(1)} %collective-permute-done.32), channel_id=1, source_target_pairs={{0,16},{8,24},{16,0},{24,8},{1,17},{9,25},{17,1},{25,9},{2,18},{10... | collective-permute-start | bytes 786440 | tf_op jit(solution)/shard_map/ppermute | solution.py:440
  136.9 18.6 %collective-permute-start.23 = (f32[288,256]{1,0:T(8,128)S(1)}, f32[288,256]{1,0:T(8,128)S(1)}, u32[]{:S(2)}, u32[]{:S(2)}) collective-permute-start(f32[288,256]{1,0:T(8,128)S(1)} %get-tuple-element.128), channel_id=1, source_target_pairs={{0,16},{8,24},{16,0},{24,8},{1,17},{9,25},{17,1},{25,9},{2,18},{10... | collective-permute-start | bytes 884744 | tf_op jit(solution)/shard_map/ppermute | solution.py:440
  151.3 13.8 %collective-permute-start.38 = (f32[288,256]{1,0:T(8,128)S(1)}, f32[288,256]{1,0:T(8,128)S(1)}, u32[]{:S(2)}, u32[]{:S(2)}) collective-permute-start(f32[288,256]{1,0:T(8,128)S(1)} %get-tuple-element.127), channel_id=1, source_target_pairs={{0,8},{8,0},{16,24},{24,16},{1,9},{9,1},{17,25},{25,17},{2,10},{10... | collective-permute-start | bytes 884744 | tf_op jit(solution)/shard_map/ppermute | solution.py:440
  152.9 16.3 %collective-permute-start.40 = (f32[288,256]{1,0:T(8,128)S(1)}, f32[288,256]{1,0:T(8,128)S(1)}, u32[]{:S(2)}, u32[]{:S(2)}) collective-permute-start(f32[288,256]{1,0:T(8,128)S(1)} %get-tuple-element.127), channel_id=1, source_target_pairs={{0,16},{8,24},{16,0},{24,8},{1,17},{9,25},{17,1},{25,9},{2,18},{10... | collective-permute-start | bytes 884744 | tf_op jit(solution)/shard_map/ppermute | solution.py:440
  155.6 13.6 %collective-permute-start.39 = (f32[288,256]{1,0:T(8,128)S(1)}, f32[288,256]{1,0:T(8,128)S(1)}, u32[]{:S(2)}, u32[]{:S(2)}) collective-permute-start(f32[288,256]{1,0:T(8,128)S(1)} %get-tuple-element.126), channel_id=1, source_target_pairs={{0,16},{8,24},{16,0},{24,8},{1,17},{9,25},{17,1},{25,9},{2,18},{10... | collective-permute-start | bytes 884744 | tf_op jit(solution)/shard_map/ppermute | solution.py:440
  157.1 14.3 %collective-permute-start.41 = (f32[288,256]{1,0:T(8,128)S(1)}, f32[288,256]{1,0:T(8,128)S(1)}, u32[]{:S(2)}, u32[]{:S(2)}) collective-permute-start(f32[288,256]{1,0:T(8,128)S(1)} %get-tuple-element.126), channel_id=1, source_target_pairs={{0,8},{8,0},{16,24},{24,16},{1,9},{9,1},{17,25},{25,17},{2,10},{10... | collective-permute-start | bytes 884744 | tf_op jit(solution)/shard_map/ppermute | solution.py:440
  158.8 15.7 %collective-permute-start.26 = (f32[288,256]{1,0:T(8,128)S(1)}, f32[288,256]{1,0:T(8,128)S(1)}, u32[]{:S(2)}, u32[]{:S(2)}) collective-permute-start(f32[288,256]{1,0:T(8,128)S(1)} %collective-permute-done.22.refs_1_), channel_id=1, source_target_pairs={{0,16},{8,24},{16,0},{24,8},{1,17},{9,25},{17,1},{25,9},{2,18},{10... | collective-permute-start | bytes 884744 | tf_op jit(solution)/shard_map/ppermute | solution.py:440
  237.4 13.2 %all-to-all-start.3 = ((f32[4,80,256]{2,1,0:T(8,128)}), f32[4,80,256]{2,1,0:T(8,128)S(1)}, u32[]{:S(2)}, u32[]{:S(2)}) async-start(f32[4,80,256]{2,1,0:T(8,128)} %broadcast_in_dim.9), calls=%async_computation.3 | async-start | bytes 655360 | tf_op jit(solution)/shard_map/all_to_all | solution.py:480
  251.5 20.3 %all-to-all-start.4 = ((f32[4,144,256]{2,1,0:T(8,128)}), f32[4,144,256]{2,1,0:T(8,128)S(1)}, u32[]{:S(2)}, u32[]{:S(2)}) async-start(f32[4,144,256]{2,1,0:T(8,128)} %broadcast_in_dim.10), calls=%async_computation.4 | async-start | bytes 1179648 | tf_op jit(solution)/shard_map/all_to_all | solution.py:480
  256.1 14.3 %collective-permute-start.46 = (f32[320,256]{1,0:T(8,128)S(1)}, f32[320,256]{1,0:T(8,128)}, u32[]{:S(2)}, u32[]{:S(2)}) collective-permute-start(f32[320,256]{1,0:T(8,128)S(1)} %bitcast.80), channel_id=1, source_target_pairs={{0,16},{8,24},{16,0},{24,8},{1,17},{9,25},{17,1},{25,9},{2,18},{10... | collective-permute-start | bytes 983048 | tf_op jit(solution)/shard_map/ppermute | solution.py:440
  256.7 13.7 %collective-permute-start.47 = (f32[320,256]{1,0:T(8,128)S(1)}, f32[320,256]{1,0:T(8,128)}, u32[]{:S(2)}, u32[]{:S(2)}) collective-permute-start(f32[320,256]{1,0:T(8,128)S(1)} %bitcast.81), channel_id=1, source_target_pairs={{0,24},{8,16},{16,8},{24,0},{1,25},{9,17},{17,9},{25,1},{2,26},{10... | collective-permute-start | bytes 983048 | tf_op jit(solution)/shard_map/ppermute | solution.py:440
  259.0 20.0 %collective-permute-start.48 = (f32[320,256]{1,0:T(8,128)S(1)}, f32[320,256]{1,0:T(8,128)}, u32[]{:S(2)}, u32[]{:S(2)}) collective-permute-start(f32[320,256]{1,0:T(8,128)S(1)} %bitcast.82), channel_id=1, source_target_pairs={{0,1},{1,0},{2,3},{3,2},{4,5},{5,4},{6,7},{7,6},{8,9},{9,8},{10,11... | collective-permute-start | bytes 983048 | tf_op jit(solution)/shard_map/ppermute | solution.py:440
  266.2 13.5 %collective-permute-start.49 = (f32[320,256]{1,0:T(8,128)S(1)}, f32[320,256]{1,0:T(8,128)}, u32[]{:S(2)}, u32[]{:S(2)}) collective-permute-start(f32[320,256]{1,0:T(8,128)S(1)} %collective-permute-done.45.refs_1_), channel_id=1, source_target_pairs={{0,1},{1,0},{2,3},{3,2},{4,5},{5,4},{6,7},{7,6},{8,9},{9,8},{10,11... | collective-permute-start | bytes 983048 | tf_op jit(solution)/shard_map/ppermute | solution.py:440
  272.7 35.5 %all-to-all-start.5 = ((f32[4,144,256]{2,1,0:T(8,128)}), f32[4,144,256]{2,1,0:T(8,128)}, u32[]{:S(2)}, u32[]{:S(2)}) async-start(f32[4,144,256]{2,1,0:T(8,128)} %broadcast_in_dim.11), calls=%async_computation.5 | async-start | bytes 1179648 | tf_op jit(solution)/shard_map/all_to_all | solution.py:480
  277.5 68.3 %all-gather.4.cloned.1.call-start = ((), (), s32[]{:S(2)}) async-start(), calls=%async_computation.7 | async-start | bytes 2359296 | tf_op jit(solution)/shard_map/all_gather | solution.py:536
  277.5 24.6 %collective-permute-start.52 = (f32[576,256]{1,0:T(8,128)S(1)}, f32[576,256]{1,0:T(8,128)S(1)}, u32[]{:S(2)}, u32[]{:S(2)}) collective-permute-start(f32[576,256]{1,0:T(8,128)S(1)} %bitcast.73), channel_id=1, source_target_pairs={{0,8},{8,0},{16,24},{24,16},{1,9},{9,1},{17,25},{25,17},{2,10},{10... | collective-permute-start | bytes 1769480 | tf_op jit(solution)/shard_map/ppermute | solution.py:440
  279.0 27.3 %collective-permute-start.53 = (f32[576,256]{1,0:T(8,128)S(1)}, f32[576,256]{1,0:T(8,128)S(1)}, u32[]{:S(2)}, u32[]{:S(2)}) collective-permute-start(f32[576,256]{1,0:T(8,128)S(1)} %bitcast.74), channel_id=1, source_target_pairs={{0,16},{8,24},{16,0},{24,8},{1,17},{9,25},{17,1},{25,9},{2,18},{10... | collective-permute-start | bytes 1769480 | tf_op jit(solution)/shard_map/ppermute | solution.py:440
  279.7 26.7 %collective-permute-start.54 = (f32[576,256]{1,0:T(8,128)S(1)}, f32[576,256]{1,0:T(8,128)S(1)}, u32[]{:S(2)}, u32[]{:S(2)}) collective-permute-start(f32[576,256]{1,0:T(8,128)S(1)} %bitcast.75), channel_id=1, source_target_pairs={{0,24},{8,16},{16,8},{24,0},{1,25},{9,17},{17,9},{25,1},{2,26},{10... | collective-permute-start | bytes 1769480 | tf_op jit(solution)/shard_map/ppermute | solution.py:440
  308.2 34.8 %collective-permute-start.59 = (f32[576,256]{1,0:T(8,128)}, f32[576,256]{1,0:T(8,128)}, u32[]{:S(2)}, u32[]{:S(2)}) collective-permute-start(f32[576,256]{1,0:T(8,128)} %bitcast.14.refs_0_), channel_id=1, source_target_pairs={{0,8},{8,0},{16,24},{24,16},{1,9},{9,1},{17,25},{25,17},{2,10},{10... | collective-permute-start | bytes 1769480 | tf_op jit(solution)/shard_map/ppermute | solution.py:440
  308.8 73.6 %all-gather.6.cloned.1.call-start = ((), (), s32[]{:S(2)}) async-start(), calls=%async_computation.8 | async-start | bytes 1769472 | tf_op jit(solution)/shard_map/all_gather | solution.py:536
  308.9 34.2 %collective-permute-start.60 = (f32[576,256]{1,0:T(8,128)}, f32[576,256]{1,0:T(8,128)}, u32[]{:S(2)}, u32[]{:S(2)}) collective-permute-start(f32[576,256]{1,0:T(8,128)} %bitcast.14.refs_0_), channel_id=1, source_target_pairs={{0,16},{8,24},{16,0},{24,8},{1,17},{9,25},{17,1},{25,9},{2,18},{10... | collective-permute-start | bytes 1769480 | tf_op jit(solution)/shard_map/ppermute | solution.py:440
  310.0 33.0 %collective-permute-start.61 = (f32[576,256]{1,0:T(8,128)}, f32[576,256]{1,0:T(8,128)}, u32[]{:S(2)}, u32[]{:S(2)}) collective-permute-start(f32[576,256]{1,0:T(8,128)} %bitcast.14.refs_0_), channel_id=1, source_target_pairs={{0,24},{8,16},{16,8},{24,0},{1,25},{9,17},{17,9},{25,1},{2,26},{10... | collective-permute-start | bytes 1769480 | tf_op jit(solution)/shard_map/ppermute | solution.py:440
  345.8 58.4 %all-gather.8.cloned.1.call-start = ((), (), s32[]{:S(2)}) async-start(), calls=%async_computation.9 | async-start | bytes 1179648 | tf_op jit(solution)/shard_map/all_gather | solution.py:536
  407.7 32.1 %all-to-all-start.6 = ((bf16[4,576,512]{2,1,0:T(8,128)(2,1)}), bf16[4,576,512]{2,1,0:T(8,128)(2,1)S(1)}, u32[]{:S(2)}, u32[]{:S(2)}) async-start(bf16[4,576,512]{2,1,0:T(8,128)(2,1)} %bitcast.65), calls=%async_computation.6 | async-start | bytes 4718592 | tf_op jit(solution)/shard_map/all_to_all | solution.py:540
  (72 other events, 659.6 us)
Sparse Core Ops, SparseCore 0:
  308.9 29.3 all-gather.3
  345.9 24.8 all-gather.5
  382.5 21.6 all-gather.7
